TPU v7x, 512 devices: a whole 4x8x8 slice. The times are simulated.
512 devices in a mesh: gx: 16 (over z, x_lo), gy: 8 (over y), gz: 4 (over x_hi, core).
Axes of the slice: x: 4 (x_hi: 2, x_lo: 2; x = x_hi * 2 + x_lo), y: 8, z: 8, core: 2. Of those that a mesh axis runs over, the one named last changes fastest.
Arguments:
- blocks: float32 [3, 3, 3, 3, 3, 16, 64, 2048], P(None, None, None, None, None, 'gz', 'gy', 'gx'), may hold values from -0.02 to 3, as said below
- classes: int32 [16, 64, 2048], P('gz', 'gy', 'gx'), may hold values from 0 to 3
- residual: float32 [3, 16, 64, 2048], P(None, 'gz', 'gy', 'gx'), may hold values from -6 to 6
Outputs:
- coarse_operator: float32 [3, 3, 3, 3, 3, 8, 32, 1024], P(None, None, None, None, None, 'gz', 'gy', 'gx')
- coarse_solution: float32 [3, 8, 32, 1024], P(None, 'gz', 'gy', 'gx')
Inputs may be any that keep to these rules, and one draw needn't show every extreme that they name: In each row of a node's 27 blocks the entry on the diagonal of the middle block is positive and larger than the sum of magnitudes of the row's other 80 entries.
All inputs are finite; a program needn't handle non-finite values.
Results may differ from a plain program's by a relative error of at most 0.0003.
Values sent between devices are 32-bit elements; how exact they have to be, the bound alone decides.
No kernel may reach another device: no remote copies, remote signals or barrier semaphores. Data moves between devices by JAX's collectives and lax.ppermute only.
A program may use at most 128 MiB of HBM per device.

v0:
```python
import functools

import jax
import jax.numpy as jnp
from jax import lax
from jax.experimental import pallas as pl
from jax.experimental.pallas import tpu as pltpu
from jax.sharding import PartitionSpec as P

STEPS = 4
CHEB_LOW = 0.1
CHEB_HIGH = 1.0
CENTRE = (CHEB_HIGH + CHEB_LOW) / 2.0
HALF = (CHEB_HIGH - CHEB_LOW) / 2.0
SIGMA = CENTRE / HALF

ITEMS = 42
VMEM = pl.BlockSpec(memory_space=pltpu.VMEM)
LIMIT = pltpu.CompilerParams(vmem_limit_bytes=40 * 1024 * 1024)


def lanes_of():
    return lax.broadcasted_iota(jnp.int32, (8, 128), 1)


def rows_of():
    return lax.broadcasted_iota(jnp.int32, (8, 128), 0)


def lroll(v, s):
    s = s % 128
    return v if s == 0 else pltpu.roll(v, s, 1)


def sroll(v, s):
    s = s % 8
    return v if s == 0 else pltpu.roll(v, s, 0)


def slot_mask(lane, j):
    right = jnp.logical_and(lane >= 3 * j, lane < 3 * j + 3)
    left = jnp.logical_and(lane >= 3 * j + 61, lane < 3 * j + 64)
    return jnp.logical_or(right, left)


def packed_size(n):
    return (n + 1) // 2 + (n + 19) // 20


def pack(vs):
    lane = lanes_of()
    out = []
    for i in range(0, len(vs), 2):
        other = lroll(vs[i + 1], 64) if i + 1 < len(vs) else jnp.zeros_like(vs[i])
        out.append(jnp.where(lane < 64, vs[i], other))
    for base in range(0, len(vs), 20):
        held = jnp.zeros((8, 128), jnp.float32)
        for j, v in enumerate(vs[base : base + 20]):
            held = jnp.where(slot_mask(lane, j), lroll(v, 3 * j - 64), held)
        out.append(held)
    return out


def unpack(load, n):
    lane = lanes_of()
    edge = jnp.logical_or(jnp.logical_and(lane >= 64, lane < 67), lane >= 125)
    mains = (n + 1) // 2
    out = []
    for i in range(n):
        main = load(i // 2)
        if i % 2:
            main = lroll(main, 64)
        held = lroll(load(mains + i // 20), 64 - 3 * (i % 20))
        out.append(jnp.where(lane < 64, main, jnp.where(edge, held, 0.0)))
    return out


def to_right(v, j):
    return lroll(v, 4 * j - 61)


def to_left(v, j):
    return lroll(v, 4 * j)


def pack_sides(vs, store_right, store_left):
    lane = lanes_of()
    for base in range(0, len(vs), 32):
        right = jnp.zeros((8, 128), jnp.float32)
        left = jnp.zeros((8, 128), jnp.float32)
        for j, v in enumerate(vs[base : base + 32]):
            mask = lane // 4 == j
            right = jnp.where(mask, to_right(v, j), right)
            left = jnp.where(mask, to_left(v, j), left)
        store_right(base // 32, right)
        store_left(base // 32, left)


def add_sides(v, t, from_left, from_right):
    lane = lanes_of()
    j = t % 32
    low = jnp.logical_or(lane >= 125, lane == 0)
    high = jnp.logical_and(lane >= 64, lane < 67)
    left = lroll(from_left(t // 32), 125 - 4 * j)
    right = lroll(from_right(t // 32), 64 - 4 * j)
    return v + jnp.where(low, left, jnp.where(high, right, 0.0))


def halves(minus, zero, plus):
    h, g = 0.5 * minus, 0.5 * plus
    quarter = 0.25 * zero
    return h, g, h + quarter, g + quarter


def coarsen_kernel(blocks, classes, residual, w, wl, right, left, scale):
    step = pl.program_id(0)
    gx, gy, gz = (lax.axis_index(a) for a in ("gx", "gy", "gz"))
    lane, row = lanes_of(), rows_of()
    even = row % 2 == 0
    not_last_x = (gx < lax.axis_size("gx") - 1).astype(jnp.float32)
    not_last_y = (gy < lax.axis_size("gy") - 1).astype(jnp.float32)
    not_last_z = (gz < lax.axis_size("gz") - 1).astype(jnp.float32)
    pick = jnp.where(lane < 64, 2 * lane, 127) % 128

    def squeeze(v):
        g = jnp.take_along_axis(v, pick, axis=1, mode="promise_in_bounds")
        return jnp.where(lane <= 64, g, 0.0)

    @pl.when(step == 0)
    def _():
        low_x = jnp.where(jnp.logical_and(lane == 0, gx == 0), 0.0, 1.0)
        low_y = jnp.where(jnp.logical_and(row == 0, gy == 0), 0.0, 1.0)
        low_z = (gz > 0).astype(jnp.float32)
        for z in range(4):
            k = classes[z].astype(jnp.float32)
            s = 0.05 + 0.95 * (k * k * k) / 27.0
            for cy in range(2):
                for cx in range(2):
                    v = s
                    if cy:
                        v = v * low_y
                    if cx:
                        v = v * low_x
                    scale[cy * 2 + cx, z] = v
                    if z == 0:
                        scale[cy * 2 + cx, 4] = v * low_z

    @pl.when(step == 0)
    def _():
        items = []
        for c in range(3):
            f = [residual[c, z] for z in range(4)]
            planes = [f[0] + 0.5 * f[1], 0.5 * f[1] + f[2] + 0.5 * f[3], 0.5 * f[3]]
            full, beyond = [], []
            for v in planes:
                h = 0.5 * v
                before = sroll(h, 1)
                full.append(v + sroll(h, -1) + jnp.where(row == 0, 0.0, before))
                beyond.append(h * not_last_y)
            main = jnp.where(even, full[0], sroll(full[1], 1))
            ghost = jnp.where(even, full[2], 0.0)
            for z in range(3):
                ghost = jnp.where(row == 1 + 2 * z, sroll(beyond[z], 2 + 2 * z), ghost)
            items.append((main, ghost))
        vs = []
        for v in [m for m, _ in items] + [g for _, g in items]:
            h = 0.5 * v
            v = v + lroll(h, -1) + jnp.where(lane == 0, 0.0, lroll(h, 1))
            v = jnp.where(lane == 127, h * not_last_x, v)
            vs.append(squeeze(v))
        for i, v in enumerate(vs):
            wl[i] = v

        def put_right(i, v):
            right[9, i] = v

        def put_left(i, v):
            left[9, i] = v

        pack_sides(vs, put_right, put_left)
        right[9, 1] = jnp.zeros((8, 128), jnp.float32)
        left[9, 1] = jnp.zeros((8, 128), jnp.float32)

    ydone = {}
    for ox in range(3):
        slots = {}
        for oy in range(3):
            kind = (2 if oy == 0 else 0) + (1 if ox == 0 else 0)
            s = [[None] * 4 for _ in range(3)]
            for oz in range(3):
                for z in range(4):
                    factor = scale[kind, 4 if (z == 0 and oz == 0) else z]
                    s[oz][z] = blocks[oz, oy, ox, 0, 0, z] * factor
            _, _, a1, b1 = halves(s[0][1], s[1][1], s[2][1])
            _, _, a3, b3 = halves(s[0][3], s[1][3], s[2][3])
            h0, g0 = 0.5 * s[0][0], 0.5 * s[2][0]
            h2, g2 = 0.5 * s[0][2], 0.5 * s[2][2]
            slots[0, 0, oy] = h0
            slots[1, 0, oy] = h0 + g0 + s[1][0] + a1
            slots[2, 0, oy] = g0 + b1
            slots[0, 1, oy] = h2 + a1
            slots[1, 1, oy] = h2 + g2 + s[1][2] + b1 + a3
            slots[2, 1, oy] = (g2 + b3) * not_last_z
            slots[3, 0, oy] = a3
            slots[3, 1, oy] = b3
        beyond = [jnp.zeros((8, 128), jnp.float32) for _ in range(2)]
        for slot in range(4):
            parts = []
            for z in range(2):
                v = [slots[slot, z, oy] for oy in range(3)]
                h, g, a, b = halves(*v)
                first = row == 0
                lower = h + jnp.where(first, 0.0, sroll(a, 1))
                middle = h + g + v[1] + jnp.where(first, 0.0, sroll(b, 1)) + sroll(a, -1)
                upper = g + sroll(b, -1)
                upper = jnp.where(row == 6, upper * not_last_y, upper)
                parts.append((lower, middle, upper))
                for cy, ghost in enumerate((a, b)):
                    at = (slot % 2) * 4 + cy * 2 + z
                    beyond[slot // 2] = jnp.where(row == at, sroll(ghost, at + 1) * not_last_y, beyond[slot // 2])
            for cy in range(3):
                ydone[slot * 3 + cy, ox] = jnp.where(even, parts[0][cy], sroll(parts[1][cy], 1))
        ydone[12, ox], ydone[13, ox] = beyond
    vs = [None] * ITEMS
    for i in range(14):
        v = [ydone[i, ox] for ox in range(3)]
        h, g, a, b = halves(*v)
        first, end = lane == 0, lane == 127
        lower = h + jnp.where(first, 0.0, lroll(a, 1))
        lower = jnp.where(end, a * not_last_x, lower)
        middle = h + g + v[1] + jnp.where(first, 0.0, lroll(b, 1)) + lroll(a, -1)
        middle = jnp.where(end, b * not_last_x, middle)
        upper = g + lroll(b, -1)
        upper = jnp.where(end, 0.0, jnp.where(lane == 126, upper * not_last_x, upper))
        for cx, done in enumerate((lower, middle, upper)):
            at = i * 3 + cx if i < 12 else 36 + cx * 2 + i - 12
            vs[at] = squeeze(done)
            w[step, at] = vs[at]

    def keep_right(i, v):
        right[step, i] = v

    def keep_left(i, v):
        left[step, i] = v

    pack_sides(vs, keep_right, keep_left)


def sides_kernel(w, wl, from_left, from_right, w_out, wl_out, message):
    row = rows_of()

    def body(rc, carry):
        vs = []
        for t in range(ITEMS):
            v = add_sides(w[rc, t], t, lambda g: from_left[rc, g], lambda g: from_right[rc, g])
            w_out[rc, t] = v
            vs.append(v)
        ends = [vs[36 + cx * 2 + 1] for cx in range(3)]
        sent = vs[27:36] + [jnp.where(row < 4, sroll(ends[0], 4), ends[1]), ends[2]]
        for i, v in enumerate(pack(sent)):
            message[rc, i] = v
        return carry

    lax.fori_loop(0, 9, body, 0)
    vs = []
    for t in range(6):
        v = add_sides(wl[t], t, lambda g: from_left[9, g], lambda g: from_right[9, g])
        wl_out[t] = v
        vs.append(v)
    done = pack(vs[3:])
    for i in range(packed_size(11)):
        message[9, i] = done[i] if i < len(done) else jnp.zeros((8, 128), jnp.float32)


def planes_kernel(w, wl, received, w_out, wl_out, up, down, total):
    row = rows_of()
    even = row % 2 == 0
    total[...] = jnp.zeros_like(total)

    def body(rc, carry):
        got = unpack(lambda i: received[rc, i], 11)
        f = [None] * 27
        for k in range(27):
            v = w[rc, k]
            if k < 9:
                v = v + jnp.where(even, got[k], 0.0)
            elif k < 18:
                v = v + jnp.where(even, sroll(got[k - 9], -1), 0.0)
            f[k] = v
            w_out[rc, k] = v
        for k in range(27, 36):
            w_out[rc, k] = jnp.zeros((8, 128), jnp.float32)
        firsts, seconds = [], []
        for cx in range(3):
            end = (sroll(got[9], 4), got[9], got[10])[cx]
            v = w[rc, 36 + cx * 2]
            moved = jnp.where(row < 4, sroll(end, 4), sroll(end, -1))
            v = v + jnp.where(even, moved, 0.0)
            firsts.append(v)
            w_out[rc, 36 + cx * 2] = v
            v = w[rc, 36 + cx * 2 + 1]
            seconds.append(v)
            w_out[rc, 36 + cx * 2 + 1] = v
        magnitude = jnp.abs(f[0])
        for k in range(1, 27):
            magnitude = magnitude + jnp.abs(f[k])
        total[rc // 3] += magnitude
        ups, downs = [], []
        for k in range(0, 27, 2):
            one, two = f[k], f[k + 1] if k + 1 < 27 else jnp.zeros((8, 128), jnp.float32)
            ups.append(jnp.where(row < 4, sroll(one, 4), two))
            downs.append(jnp.where(row < 4, one, sroll(two, 4)))
        ups += firsts + [jnp.where(row < 4, seconds[0], sroll(seconds[1], 4)), seconds[2]]
        for i, v in enumerate(pack(ups)):
            up[rc, i] = v
        for i, v in enumerate(pack(downs)):
            down[rc, i] = v
        return carry

    lax.fori_loop(0, 9, body, 0)
    got = unpack(lambda i: received[9, i], 3)
    ups, downs = [], []
    for c in range(3):
        load = wl[c] + jnp.where(even, got[c], 0.0)
        ghost = wl[3 + c] + jnp.where(row == 1, sroll(got[c], -4), 0.0)
        wl_out[c] = load
        wl_out[3 + c] = ghost
        d = load * (1.0 / (total[c] + 1e-06)) / CENTRE
        v = jnp.where(row < 4, sroll(load, 4), 0.0)
        v = jnp.where(row == 4, sroll(ghost, 3), v)
        v = jnp.where(row == 5, sroll(ghost, 2), v)
        ups.append(jnp.where(row >= 6, sroll(d, 4), v))
        downs.append(jnp.where(row < 4, load, jnp.where(row >= 6, sroll(d, 2), 0.0)))
    for ref, vs, size in ((up, ups, packed_size(19)), (down, downs, packed_size(14))):
        done = pack(vs)
        for i in range(size):
            ref[9, i] = done[i] if i < len(done) else jnp.zeros((8, 128), jnp.float32)


def share_planes(d, piece):
    gz = lax.axis_index("gz")
    even = lax.broadcasted_iota(jnp.int32, (24, 128), 0) % 2 == 0

    def pair(one, two, z):
        if z == 0:
            return jnp.where(even, one, pltpu.roll(two, 1, 0))
        return jnp.where(even, pltpu.roll(one, 23, 0), two)

    for i, (one, two) in enumerate(((d[0], d[1]), (d[2], d[2]))):
        first, last = pair(one, two, 0), pair(one, two, 1)
        for to in range(piece.shape[0]):
            piece[to, i] = jnp.where(to < gz, first, last)


def rows_kernel(w, wl, from_low, from_high, operator, whole, q, d, inverse, piece, total, turned):
    row = rows_of()
    ghosts = jnp.logical_or(row == 4, row == 5)
    total[...] = jnp.zeros_like(total)

    def body(rc, carry):
        ups = unpack(lambda i: from_low[rc, i], 19)
        downs = unpack(lambda i: from_high[rc, i], 14)
        seconds = [ups[17], sroll(ups[17], 4), ups[18]]
        top_sum = jnp.zeros((8, 128), jnp.float32)
        bottom_sum = jnp.zeros((8, 128), jnp.float32)
        for cz in range(3):
            for cy in range(3):
                for cx in range(3):
                    k = cz * 9 + cy * 3 + cx
                    f = sroll(w[rc, k], 4)
                    above, below = ups[k // 2], downs[k // 2]
                    top = jnp.where(row < 4, sroll(above, 4) if k % 2 else above, f)
                    bottom = jnp.where(row < 4, f, below if k % 2 else sroll(below, 4))
                    if cy < 2:
                        at = (cz % 2) * 4 + cy * 2
                        got = ups[14 + cx] if cz < 2 else seconds[cx]
                        own = w[rc, 36 + cx * 2 + cz // 2]
                        top = top + jnp.where(ghosts, sroll(got, 4 - at), 0.0)
                        bottom = bottom + jnp.where(ghosts, sroll(own, 4 - at), 0.0)
                    whole[rc, k, 0:8] = top
                    whole[rc, k, 8:16] = bottom
                    top_sum = top_sum + jnp.abs(top)
                    bottom_sum = bottom_sum + jnp.abs(bottom)
        total[rc // 3, 0:8] += top_sum
        total[rc // 3, 8:16] += bottom_sum
        for cz in range(3):
            for cy in range(3):
                for cx in range(3):
                    for z in range(2):
                        v = whole[rc, cz * 9 + cy * 3 + cx, pl.ds(4 + z, 4, stride=2), :]
                        operator[cz, cy, cx, rc // 3, rc % 3, z] = v[:, 0:64]
        return carry

    lax.fori_loop(0, 9, body, 0)
    ups = unpack(lambda i: from_low[9, i], 3)
    downs = unpack(lambda i: from_high[9, i], 3)
    for c in range(3):
        load, ghost = sroll(wl[c], 4), wl[3 + c]
        q[c, 0:8] = jnp.where(row < 4, ups[c], load + jnp.where(ghosts, ups[c], 0.0))
        below = sroll(downs[c], 4)
        below = below + jnp.where(row == 4, sroll(ghost, 3), jnp.where(row == 5, sroll(ghost, 2), 0.0))
        q[c, 8:16] = jnp.where(row < 4, load, below)
        part = 1.0 / (total[c] + 1e-06)
        inverse[c] = part
        d[c, 16:24] = jnp.zeros((8, 128), jnp.float32)
        d[c, 2:18] = part * q[c] / CENTRE
        turned[...] = ups[c]
        d[c, 0:2] = turned[6:8]
        turned[...] = downs[c]
        d[c, 18:20] = turned[6:8]
    share_planes([d[c] for c in range(3)], piece)


def apply_to(whole, d, received, near, out):
    gz = lax.axis_index("gz")
    even = lax.broadcasted_iota(jnp.int32, (24, 128), 0) % 2 == 0
    below = jnp.maximum(gz - 1, 0)
    above = jnp.minimum(gz + 1, received.shape[0] - 1)
    for c in range(3):
        own = d[c]
        low, high = received[below, c // 2], received[above, c // 2]
        if c == 1:
            low = pltpu.roll(low, 23, 0)
        else:
            high = pltpu.roll(high, 1, 0)
        near[0, c] = jnp.where(even, low, pltpu.roll(own, 1, 0))
        near[1, c] = own
        near[2, c] = jnp.where(even, pltpu.roll(own, 23, 0), high)
    sums = [jnp.zeros((16, 128), jnp.float32) for _ in range(3)]
    for cz in range(3):
        for cy in range(3):
            for c in range(3):
                v = near[cz, c, pl.ds(2 * cy, 16), :]
                for cx, moved in enumerate((pltpu.roll(v, 1, 1), v, pltpu.roll(v, 127, 1))):
                    for r in range(3):
                        sums[r] = sums[r] + whole[r * 3 + c, cz * 9 + cy * 3 + cx] * moved
    for r in range(3):
        out(r, sums[r])


def step_kernel(first, rho_now, rho_next, last, *refs):
    whole, q, d, inverse, received = refs[:5]
    refs = refs[5:]
    if first:
        x = None
    else:
        x, refs = refs[0], refs[1:]
    if last:
        solution_out, near, turned = refs
    else:
        q_out, d_out, x_out, piece, near = refs

    def update(r, product):
        now = d[r, 2:18]
        x_now = now if x is None else x[r] + now
        q_now = q[r] - product
        d_new = rho_next * rho_now * now + 2.0 * rho_next / HALF * (inverse[r] * q_now)
        if last:
            turned[...] = x_now + d_new
            for z in range(2):
                solution_out[r, z] = turned[pl.ds(4 + z, 4, stride=2), :][:, 0:64]
        else:
            x_out[r] = x_now
            q_out[r] = q_now
            d_out[r, 0:8] = jnp.zeros((8, 128), jnp.float32)
            d_out[r, 16:24] = jnp.zeros((8, 128), jnp.float32)
            d_out[r, 2:18] = d_new

    apply_to(whole, d, received, near, update)
    if not last:
        share_planes([d_out[c] for c in range(3)], piece)


def shape(*dims):
    return jax.ShapeDtypeStruct(dims, jnp.float32)


def along(block, axis, distance):
    n = lax.axis_size(axis)
    route = [(i, i + distance) for i in range(n) if 0 <= i + distance < n]
    return lax.ppermute(block, axis, route)


def shards(blocks, classes, residual):
    nz = lax.axis_size("gz")
    w_shape, wl_shape = shape(9, ITEMS, 8, 128), shape(6, 8, 128)
    w, wl, right, left = pl.pallas_call(
        coarsen_kernel,
        grid=(9,),
        in_specs=[
            pl.BlockSpec((3, 3, 3, 1, 1, 4, 8, 128), lambda i: (0, 0, 0, i // 3, i % 3, 0, 0, 0)),
            pl.BlockSpec((4, 8, 128), lambda i: (0, 0, 0)),
            pl.BlockSpec((3, 4, 8, 128), lambda i: (0, 0, 0, 0)),
        ],
        out_specs=[VMEM] * 4,
        out_shape=[w_shape, wl_shape, shape(10, 2, 8, 128), shape(10, 2, 8, 128)],
        scratch_shapes=[pltpu.VMEM((4, 5, 8, 128), jnp.float32)],
        compiler_params=LIMIT,
    )(blocks, classes, residual)
    from_left, from_right = along(right, "gx", 1), along(left, "gx", -1)
    w, wl, message = pl.pallas_call(
        sides_kernel,
        in_specs=[VMEM] * 4,
        out_specs=[VMEM] * 3,
        out_shape=[w_shape, wl_shape, shape(10, packed_size(11), 8, 128)],
        compiler_params=LIMIT,
    )(w, wl, from_left, from_right)
    received = along(message, "gz", 1)
    w, wl, up, down = pl.pallas_call(
        planes_kernel,
        in_specs=[VMEM] * 3,
        out_specs=[VMEM] * 4,
        out_shape=[w_shape, wl_shape, shape(10, packed_size(19), 8, 128), shape(10, packed_size(14), 8, 128)],
        scratch_shapes=[pltpu.VMEM((3, 8, 128), jnp.float32)],
        compiler_params=LIMIT,
    )(w, wl, received)
    from_low, from_high = along(up, "gy", 1), along(down, "gy", -1)
    operator, whole, q, d, inverse, piece = pl.pallas_call(
        rows_kernel,
        in_specs=[VMEM] * 4,
        out_specs=[VMEM] * 6,
        out_shape=[
            shape(3, 3, 3, 3, 3, 2, 4, 64),
            shape(9, 27, 16, 128),
            shape(3, 16, 128),
            shape(3, 24, 128),
            shape(3, 16, 128),
            shape(nz, 2, 24, 128),
        ],
        scratch_shapes=[pltpu.VMEM((3, 16, 128), jnp.float32), pltpu.VMEM((8, 128), jnp.float32)],
        compiler_params=LIMIT,
    )(w, wl, from_low, from_high)
    x = []
    rho_now = 1.0 / SIGMA
    for step in range(STEPS - 1):
        rho_next = 1.0 / (2.0 * SIGMA - rho_now)
        last = step == STEPS - 2
        shared = lax.all_to_all(piece, "gz", 0, 0)
        if last:
            outs = shape(3, 2, 4, 64)
        else:
            outs = [shape(3, 16, 128), shape(3, 24, 128), shape(3, 16, 128), shape(nz, 2, 24, 128)]
        done = pl.pallas_call(
            functools.partial(step_kernel, step == 0, rho_now, rho_next, last),
            in_specs=[VMEM] * (5 + len(x)),
            out_specs=VMEM if last else [VMEM] * 4,
            out_shape=outs,
            scratch_shapes=[pltpu.VMEM((3, 3, 24, 128), jnp.float32)] + ([pltpu.VMEM((16, 128), jnp.float32)] if last else []),
            compiler_params=LIMIT,
        )(whole, q, d, inverse, shared, *x)
        if last:
            return operator, done
        q, d, x, piece = done
        x = [x]
        rho_now = rho_next


def solution(mesh):
    placed = (
        P(None, None, None, None, None, "gz", "gy", "gx"),
        P("gz", "gy", "gx"),
        P(None, "gz", "gy", "gx"),
    )
    return jax.shard_map(
        shards,
        mesh=mesh,
        in_specs=placed,
        out_specs=(P(None, None, None, None, None, "gz", "gy", "gx"), P(None, "gz", "gy", "gx")),
        check_vma=False,
    )
```

profile of v0, /device:TPU:218, one launch (start us, length us, event | category | flops | bytes accessed | tf_op | source)
XLA Modules:
  0.0 81.0 jit_solution(4312540844384970899)
XLA Ops:
  0.6 0.0 copy-start
  0.6 2.1 %copy-done = f32[3,3,3,3,3,4,8,128]{7,6,5,4,3,2,1,0:T(8,128)S(1)} copy-done((f32[3,3,3,3,3,4,8,128]{7,6,5,4,3,2,1,0:T(8,128)S(1)}, f32[3,3,3,3,3,4,8,128]{7,6,5,4,3,2,1,0:T(8,128)}, u32[]{:S(2)}) %copy-start) | copy-done | bytes 3981336
  2.8 0.8 copy-done.1
  3.6 0.7 copy-done.2
  4.3 5.2 %shard_map.50 = (f32[9,42,8,128]{3,2,1,0:T(8,128)S(1)}, f32[6,8,128]{2,1,0:T(8,128)S(1)}, f32[10,2,8,128]{3,2,1,0:T(8,128)S(1)}, f32[10,2,8,128]{3,2,1,0:T(8,128)S(1)}) custom-call(f32[3,3,3,3,3,4,8,128]{7,6,5,4,3,2,1,0:T(8,128)S(1)} %copy-done, s32[4,8,128]{2,1,0:T(8,128)S(1)} %copy-done.2, f32[3,4,8,128]{3,2,1,0:T(8,128)S(1)} %copy-done.1), custom_call_target="tpu_custom_call" | custom-call | tf_op jit(solution)/shard_map/pallas_call | solution.py:487
  9.5 5.5 %collective-permute-start = (f32[10,2,8,128]{3,2,1,0:T(8,128)S(1)}, f32[10,2,8,128]{3,2,1,0:T(8,128)S(1)}, u32[]{:S(2)}, u32[]{:S(2)}) collective-permute-start(f32[10,2,8,128]{3,2,1,0:T(8,128)S(1)} %get-tuple-element.29), channel_id=1, source_target_pairs={{0,32},{32,64},{64,96},{96,128},{128,160},{160,192},{192,224},{224... | collective-permute-start | bytes 245768 | tf_op jit(solution)/shard_map/ppermute | solution.py:481
  14.9 1.9 %collective-permute-start.1 = (f32[10,2,8,128]{3,2,1,0:T(8,128)S(1)}, f32[10,2,8,128]{3,2,1,0:T(8,128)S(1)}, u32[]{:S(2)}, u32[]{:S(2)}) collective-permute-start(f32[10,2,8,128]{3,2,1,0:T(8,128)S(1)} %get-tuple-element.30), channel_id=1, source_target_pairs={{32,0},{64,32},{96,64},{128,96},{160,128},{192,160},{224,192},{256... | collective-permute-start | bytes 245768 | tf_op jit(solution)/shard_map/ppermute | solution.py:481
  16.9 0.1 collective-permute-done.from_left
  17.0 6.4 %collective-permute-done.1.from_right = f32[10,2,8,128]{3,2,1,0:T(8,128)S(1)} collective-permute-done((f32[10,2,8,128]{3,2,1,0:T(8,128)S(1)}, f32[10,2,8,128]{3,2,1,0:T(8,128)S(1)}, u32[]{:S(2)}, u32[]{:S(2)}) %collective-permute-start.1) | collective-permute-done | bytes 81952 | tf_op jit(solution)/shard_map/ppermute | solution.py:481
  23.4 2.0 %shard_map.51 = (f32[9,42,8,128]{3,2,1,0:T(8,128)S(1)}, f32[6,8,128]{2,1,0:T(8,128)S(1)}, f32[10,7,8,128]{3,2,1,0:T(8,128)S(1)}) custom-call(f32[9,42,8,128]{3,2,1,0:T(8,128)S(1)} %get-tuple-element.27.w, f32[6,8,128]{2,1,0:T(8,128)S(1)} %get-tuple-element.28.wl, f32[10,2,8,128]{3,2,1,0:T(8,128)S(1)} %collective-permute-done.from_left, ...), custom_call_target="tpu_custom_call" | custom-call | tf_op jit(solution)/shard_map/pallas_call | solution.py:501
  25.4 1.3 %collective-permute-start.2 = (f32[10,7,8,128]{3,2,1,0:T(8,128)S(1)}, f32[10,7,8,128]{3,2,1,0:T(8,128)S(1)}, u32[]{:S(2)}, u32[]{:S(2)}) collective-permute-start(f32[10,7,8,128]{3,2,1,0:T(8,128)S(1)} %get-tuple-element.33), channel_id=1, source_target_pairs={{0,1},{1,2},{2,3},{4,5},{5,6},{6,7},{8,9},{9,10},{10,11},{12,13},{... | collective-permute-start | bytes 860168 | tf_op jit(solution)/shard_map/ppermute | solution.py:481
  26.7 1.2 %collective-permute-done.2.received = f32[10,7,8,128]{3,2,1,0:T(8,128)S(1)} collective-permute-done((f32[10,7,8,128]{3,2,1,0:T(8,128)S(1)}, f32[10,7,8,128]{3,2,1,0:T(8,128)S(1)}, u32[]{:S(2)}, u32[]{:S(2)}) %collective-permute-start.2) | collective-permute-done | bytes 286752 | tf_op jit(solution)/shard_map/ppermute | solution.py:481
  27.9 1.9 %shard_map.52 = (f32[9,42,8,128]{3,2,1,0:T(8,128)S(1)}, f32[6,8,128]{2,1,0:T(8,128)S(1)}, f32[10,11,8,128]{3,2,1,0:T(8,128)S(1)}, f32[10,8,8,128]{3,2,1,0:T(8,128)S(1)}) custom-call(f32[9,42,8,128]{3,2,1,0:T(8,128)S(1)} %get-tuple-element.31.w, f32[6,8,128]{2,1,0:T(8,128)S(1)} %get-tuple-element.32.wl, f32[10,7,8,128]{3,2,1,0:T(8,128)S(1)} %collective-permute-done.2.received), custom_call_target="tpu_custom_call" | custom-call | tf_op jit(solution)/shard_map/pallas_call | solution.py:509
  29.7 4.7 %collective-permute-start.3 = (f32[10,11,8,128]{3,2,1,0:T(8,128)S(1)}, f32[10,11,8,128]{3,2,1,0:T(8,128)S(1)}, u32[]{:S(2)}, u32[]{:S(2)}) collective-permute-start(f32[10,11,8,128]{3,2,1,0:T(8,128)S(1)} %get-tuple-element.36), channel_id=1, source_target_pairs={{0,4},{4,8},{8,12},{12,16},{16,20},{20,24},{24,28},{1,5},{5,9},{9,... | collective-permute-start | bytes 1351688 | tf_op jit(solution)/shard_map/ppermute | solution.py:481
  34.4 1.9 %collective-permute-start.4 = (f32[10,8,8,128]{3,2,1,0:T(8,128)S(1)}, f32[10,8,8,128]{3,2,1,0:T(8,128)S(1)}, u32[]{:S(2)}, u32[]{:S(2)}) collective-permute-start(f32[10,8,8,128]{3,2,1,0:T(8,128)S(1)} %get-tuple-element.37), channel_id=1, source_target_pairs={{4,0},{8,4},{12,8},{16,12},{20,16},{24,20},{28,24},{5,1},{9,5},{13... | collective-permute-start | bytes 983048 | tf_op jit(solution)/shard_map/ppermute | solution.py:481
  36.4 8.3 %collective-permute-done.4.from_high = f32[10,8,8,128]{3,2,1,0:T(8,128)S(1)} collective-permute-done((f32[10,8,8,128]{3,2,1,0:T(8,128)S(1)}, f32[10,8,8,128]{3,2,1,0:T(8,128)S(1)}, u32[]{:S(2)}, u32[]{:S(2)}) %collective-permute-start.4) | collective-permute-done | bytes 327712 | tf_op jit(solution)/shard_map/ppermute | solution.py:481
  44.6 0.0 collective-permute-done.3.from_low
  44.6 2.3 %shard_map.53 = (f32[3,3,3,3,3,2,4,64]{7,6,5,4,3,2,1,0:T(4,128)}, f32[9,27,16,128]{3,2,1,0:T(8,128)S(1)}, f32[3,16,128]{2,1,0:T(8,128)S(1)}, f32[3,24,128]{2,1,0...) custom-call(f32[9,42,8,128]{3,2,1,0:T(8,128)S(1)} %get-tuple-element.34.w, ...), custom_call_target="tpu_custom_call" | custom-call | tf_op jit(solution)/shard_map/pallas_call | solution.py:518
  46.9 16.3 %all_to_all.15.refs_4_ = f32[4,2,24,128]{3,2,1,0:T(8,128)S(1)} all-to-all(f32[4,2,24,128]{3,2,1,0:T(8,128)S(1)} %get-tuple-element.43), channel_id=1, replica_groups=mesh['gx'=16,'gy'=8,'gz'=4] {'gz'}, dimensions={0} | all-to-all | bytes 196608 | tf_op jit(solution)/shard_map/all_to_all | solution.py:538
  63.2 0.3 shard_map.54
  63.5 8.2 %all_to_all.16.refs_4_ = f32[4,2,24,128]{3,2,1,0:T(8,128)S(1)} all-to-all(f32[4,2,24,128]{3,2,1,0:T(8,128)S(1)} %get-tuple-element.46), channel_id=1, replica_groups=mesh['gx'=16,'gy'=8,'gz'=4] {'gz'}, dimensions={0} | all-to-all | bytes 196608 | tf_op jit(solution)/shard_map/all_to_all | solution.py:538
  71.6 0.3 shard_map.55
  71.9 8.2 %all_to_all.17.refs_4_ = f32[4,2,24,128]{3,2,1,0:T(8,128)S(1)} all-to-all(f32[4,2,24,128]{3,2,1,0:T(8,128)S(1)} %get-tuple-element.50), channel_id=1, replica_groups=mesh['gx'=16,'gy'=8,'gz'=4] {'gz'}, dimensions={0} | all-to-all | bytes 196608 | tf_op jit(solution)/shard_map/all_to_all | solution.py:538
  80.1 0.9 %shard_map.56 = f32[3,2,4,64]{3,2,1,0:T(4,128)} custom-call(f32[9,27,16,128]{3,2,1,0:T(8,128)S(1)} %get-tuple-element.39.refs_0_, f32[3,16,128]{2,1,0:T(8,128)S(1)} %get-tuple-element.48.refs_1_, f32[3,24,128]{2,1,0:T(8,128)S(1)} %get-tuple-element.49.refs_2_, f32[3,16,128]{2,1,0:T(8,128)S(1)} %get-tuple-element.42.refs_3_, ...), custom_call_target="tpu_custom_call" | custom-call | tf_op jit(solution)/shard_map/pallas_call | solution.py:543
  (2 shorter events, 0.0 us)
Async XLA Ops:
  0.6 2.1 %copy-start = (f32[3,3,3,3,3,4,8,128]{7,6,5,4,3,2,1,0:T(8,128)S(1)}, f32[3,3,3,3,3,4,8,128]{7,6,5,4,3,2,1,0:T(8,128)}, u32[]{:S(2)}) copy-start(f32[3,3,3,3,3,4,8,128]{7,6,5,4,3,2,1,0:T(8,128)} %blocks.1) | copy-start | bytes 11943940
  2.8 0.8 copy-start.1
  3.6 0.7 copy-start.2
  9.5 7.5 %collective-permute-start = (f32[10,2,8,128]{3,2,1,0:T(8,128)S(1)}, f32[10,2,8,128]{3,2,1,0:T(8,128)S(1)}, u32[]{:S(2)}, u32[]{:S(2)}) collective-permute-start(f32[10,2,8,128]{3,2,1,0:T(8,128)S(1)} %get-tuple-element.29), channel_id=1, source_target_pairs={{0,32},{32,64},{64,96},{96,128},{128,160},{160,192},{192,224},{224... | collective-permute-start | bytes 245768 | tf_op jit(solution)/shard_map/ppermute | solution.py:481
  14.9 8.4 %collective-permute-start.1 = (f32[10,2,8,128]{3,2,1,0:T(8,128)S(1)}, f32[10,2,8,128]{3,2,1,0:T(8,128)S(1)}, u32[]{:S(2)}, u32[]{:S(2)}) collective-permute-start(f32[10,2,8,128]{3,2,1,0:T(8,128)S(1)} %get-tuple-element.30), channel_id=1, source_target_pairs={{32,0},{64,32},{96,64},{128,96},{160,128},{192,160},{224,192},{256... | collective-permute-start | bytes 245768 | tf_op jit(solution)/shard_map/ppermute | solution.py:481
  25.4 2.5 %collective-permute-start.2 = (f32[10,7,8,128]{3,2,1,0:T(8,128)S(1)}, f32[10,7,8,128]{3,2,1,0:T(8,128)S(1)}, u32[]{:S(2)}, u32[]{:S(2)}) collective-permute-start(f32[10,7,8,128]{3,2,1,0:T(8,128)S(1)} %get-tuple-element.33), channel_id=1, source_target_pairs={{0,1},{1,2},{2,3},{4,5},{5,6},{6,7},{8,9},{9,10},{10,11},{12,13},{... | collective-permute-start | bytes 860168 | tf_op jit(solution)/shard_map/ppermute | solution.py:481
  29.7 14.9 %collective-permute-start.3 = (f32[10,11,8,128]{3,2,1,0:T(8,128)S(1)}, f32[10,11,8,128]{3,2,1,0:T(8,128)S(1)}, u32[]{:S(2)}, u32[]{:S(2)}) collective-permute-start(f32[10,11,8,128]{3,2,1,0:T(8,128)S(1)} %get-tuple-element.36), channel_id=1, source_target_pairs={{0,4},{4,8},{8,12},{12,16},{16,20},{20,24},{24,28},{1,5},{5,9},{9,... | collective-permute-start | bytes 1351688 | tf_op jit(solution)/shard_map/ppermute | solution.py:481
  34.4 10.2 %collective-permute-start.4 = (f32[10,8,8,128]{3,2,1,0:T(8,128)S(1)}, f32[10,8,8,128]{3,2,1,0:T(8,128)S(1)}, u32[]{:S(2)}, u32[]{:S(2)}) collective-permute-start(f32[10,8,8,128]{3,2,1,0:T(8,128)S(1)} %get-tuple-element.37), channel_id=1, source_target_pairs={{4,0},{8,4},{12,8},{16,12},{20,16},{24,20},{28,24},{5,1},{9,5},{13... | collective-permute-start | bytes 983048 | tf_op jit(solution)/shard_map/ppermute | solution.py:481
where the time goes:
time: 81.4 us; the launch traced here: 81 us
  blocking collectives  32.6 us (40%)
  waiting for transfers between devices  15.9 us (20%)
  starting transfers between devices  15.3 us (19%)
  Pallas kernels  12.8 us (16%)
  local copies, waits for them, and re-layouts  3.64 us (4%)
    all_to_all x3, blocking collectives, shards(): shared = lax.all_to_all(piece, 'gz', 0, 0)  32.6 us
    ppermute x5, waiting for transfers between devices, along(): return lax.ppermute(block, axis, route)  15.9 us
    ppermute x5, starting transfers between devices, along(): return lax.ppermute(block, axis, route)  15.3 us
    pallas_call x1, Pallas kernels, shards(): pl.pallas_call(coarsen_kernel, grid=(9,), in_specs=[pl.BlockSpec((3, 3, 3...  5.18 us
    unnamed x6, local copies, waits for them, and re-layouts  3.64 us
    pallas_call x1, Pallas kernels, shards(): pl.pallas_call(rows_kernel, in_specs=[VMEM] * 4, out_specs=[VMEM] * 6, ou...  2.31 us
    pallas_call x1, Pallas kernels, shards(): pl.pallas_call(sides_kernel, in_specs=[VMEM] * 4, out_specs=[VMEM] * 3, o...  2.03 us
    pallas_call x1, Pallas kernels, shards(): pl.pallas_call(planes_kernel, in_specs=[VMEM] * 3, out_specs=[VMEM] * 4,...  1.86 us
  transfers between devices with their start and end apart: 5, of which 4 were waited for; matrix products, arithmetic and copies ran while one was open for 0% of the time, Pallas kernels for 0%

commit v1 on v0

v1 whole, which is shorter than its diff:
```python
import functools
import itertools

import jax
import jax.numpy as jnp
from jax import lax
from jax.experimental import pallas as pl
from jax.experimental.pallas import tpu as pltpu
from jax.sharding import PartitionSpec as P

STEPS = 4
CHEB_LOW = 0.1
CHEB_HIGH = 1.0
CENTRE = (CHEB_HIGH + CHEB_LOW) / 2.0
HALF = (CHEB_HIGH - CHEB_LOW) / 2.0
SIGMA = CENTRE / HALF

ITEMS = 32
PLANE = 11
UPS, DOWNS = 18, 14
VMEM = pl.BlockSpec(memory_space=pltpu.VMEM)
HBM = pl.BlockSpec(memory_space=pltpu.HBM)
LIMIT = pltpu.CompilerParams(vmem_limit_bytes=40 * 1024 * 1024)


def lanes_of():
    return lax.broadcasted_iota(jnp.int32, (8, 128), 1)


def rows_of():
    return lax.broadcasted_iota(jnp.int32, (8, 128), 0)


def lroll(v, s):
    s = s % 128
    return v if s == 0 else pltpu.roll(v, s, 1)


def sroll(v, s):
    s = s % 8
    return v if s == 0 else pltpu.roll(v, s, 0)


def slot_mask(lane, j):
    right = jnp.logical_and(lane >= 3 * j, lane < 3 * j + 3)
    left = jnp.logical_and(lane >= 3 * j + 61, lane < 3 * j + 64)
    return jnp.logical_or(right, left)


def packed_size(n):
    return (n + 1) // 2 + (n + 19) // 20


def pack(vs):
    lane = lanes_of()
    out = []
    for i in range(0, len(vs), 2):
        other = lroll(vs[i + 1], 64) if i + 1 < len(vs) else jnp.zeros_like(vs[i])
        out.append(jnp.where(lane < 64, vs[i], other))
    for base in range(0, len(vs), 20):
        held = jnp.zeros((8, 128), jnp.float32)
        for j, v in enumerate(vs[base : base + 20]):
            held = jnp.where(slot_mask(lane, j), lroll(v, 3 * j - 64), held)
        out.append(held)
    return out


def unpack(load, n):
    lane = lanes_of()
    edge = jnp.logical_or(jnp.logical_and(lane >= 64, lane < 67), lane >= 125)
    mains = (n + 1) // 2
    out = []
    for i in range(n):
        main = load(i // 2)
        if i % 2:
            main = lroll(main, 64)
        held = lroll(load(mains + i // 20), 64 - 3 * (i % 20))
        out.append(jnp.where(lane < 64, main, jnp.where(edge, held, 0.0)))
    return out


def right_slot(lane, j):
    return lane // 4 == j


def left_slot(lane, j):
    at = (lane - (4 * j + 67)) % 128
    return at < 3


def pack_sides(vs):
    lane = lanes_of()
    right = jnp.zeros((8, 128), jnp.float32)
    left = jnp.zeros((8, 128), jnp.float32)
    for j, v in enumerate(vs):
        moved = lroll(v, 4 * j - 61)
        right = jnp.where(right_slot(lane, j), moved, right)
        left = jnp.where(left_slot(lane, j), moved, left)
    return right, left


def sides(from_left, from_right, j):
    lane = lanes_of()
    both = lroll(jnp.where(right_slot(lane, j), from_left, from_right), -(4 * j + 3))
    ends = jnp.logical_or(jnp.logical_or(lane >= 125, lane == 0), jnp.logical_and(lane >= 64, lane < 67))
    return jnp.where(ends, both, 0.0)


def plane_size(n):
    return n // 2 + 1


def pack_plane(vs):
    lane = lanes_of()
    out = [jnp.where(lane < 64, vs[i], lroll(vs[i + 1], 64)) for i in range(0, len(vs) - 1, 2)]
    last = jnp.where(lane < 64, vs[-1], 0.0)
    for i, v in enumerate(vs):
        last = jnp.where(lane == 64 + i, lroll(v, i), last)
    return out + [last]


def unpack_plane(load, n, from_left, from_right):
    lane = lanes_of()
    last = load(n // 2)
    out = []
    for i in range(n):
        main = load(i // 2)
        if i % 2:
            main = lroll(main, 64)
        main = jnp.where(lane < 64, main, jnp.where(lane == 64, lroll(last, -i), 0.0))
        out.append(main + sides(from_left, from_right, i))
    return out


def halves(minus, zero, plus):
    h, g = 0.5 * minus, 0.5 * plus
    quarter = 0.25 * zero
    return h, g, h + quarter, g + quarter


def coarsen_kernel(blocks_in, classes_in, residual_in, w, wl, right, left, plane, plane_right, plane_left, blocks, classes, residual, scale, sems):
    def fetch(i):
        source = blocks_in.at[:, :, :, i // 3, i % 3]
        return pltpu.make_async_copy(source, blocks.at[i], sems.at[i])

    classes_copy = pltpu.make_async_copy(classes_in, classes, sems.at[9])
    residual_copy = pltpu.make_async_copy(residual_in, residual, sems.at[10])
    classes_copy.start()
    fetch(0).start()
    residual_copy.start()
    for i in range(1, 9):
        fetch(i).start()
    gx, gy, gz = (lax.axis_index(a) for a in ("gx", "gy", "gz"))
    lane, row = lanes_of(), rows_of()
    even = row % 2 == 0
    not_last_x = (gx < lax.axis_size("gx") - 1).astype(jnp.float32)
    not_last_y = (gy < lax.axis_size("gy") - 1).astype(jnp.float32)
    not_last_z = (gz < lax.axis_size("gz") - 1).astype(jnp.float32)
    pick = jnp.where(lane < 64, 2 * lane, 127) % 128

    def squeeze(v):
        g = jnp.take_along_axis(v, pick, axis=1, mode="promise_in_bounds")
        return jnp.where(lane <= 64, g, 0.0)

    def coarsen(step):
        ydone = {}
        for ox in range(3):
            slots = {}
            for oy in range(3):
                kind = (2 if oy == 0 else 0) + (1 if ox == 0 else 0)
                s = [[None] * 4 for _ in range(3)]
                for oz in range(3):
                    for z in range(4):
                        factor = scale[kind, 4 if (z == 0 and oz == 0) else z]
                        s[oz][z] = blocks[step, oz, oy, ox, z] * factor
                _, _, a1, b1 = halves(s[0][1], s[1][1], s[2][1])
                _, _, a3, b3 = halves(s[0][3], s[1][3], s[2][3])
                h0, g0 = 0.5 * s[0][0], 0.5 * s[2][0]
                h2, g2 = 0.5 * s[0][2], 0.5 * s[2][2]
                slots[0, 0, oy] = h0
                slots[1, 0, oy] = h0 + g0 + s[1][0] + a1
                slots[2, 0, oy] = g0 + b1
                slots[0, 1, oy] = h2 + a1
                slots[1, 1, oy] = h2 + g2 + s[1][2] + b1 + a3
                slots[2, 1, oy] = (g2 + b3) * not_last_z
                slots[3, 0, oy] = a3
                slots[3, 1, oy] = b3
            beyond = [jnp.zeros((8, 128), jnp.float32) for _ in range(2)]
            for slot in range(4):
                parts = []
                for z in range(2):
                    v = [slots[slot, z, oy] for oy in range(3)]
                    h, g, a, b = halves(*v)
                    first = row == 0
                    lower = h + jnp.where(first, 0.0, sroll(a, 1))
                    middle = h + g + v[1] + jnp.where(first, 0.0, sroll(b, 1)) + sroll(a, -1)
                    upper = g + sroll(b, -1)
                    upper = jnp.where(row == 6, upper * not_last_y, upper)
                    parts.append((lower, middle, upper))
                    for cy, ghost in enumerate((a, b)):
                        at = (slot % 2) * 4 + cy * 2 + z
                        beyond[slot // 2] = jnp.where(row == at, sroll(ghost, at + 1) * not_last_y, beyond[slot // 2])
                for cy in range(3):
                    ydone[slot * 3 + cy, ox] = jnp.where(even, parts[0][cy], sroll(parts[1][cy], 1))
            ydone[12, ox], ydone[13, ox] = beyond
        kept, sent, rows = [None] * ITEMS, [None] * PLANE, {}
        for i in range(14):
            v = [ydone[i, ox] for ox in range(3)]
            h, g, a, b = halves(*v)
            first, end = lane == 0, lane == 127
            lower = h + jnp.where(first, 0.0, lroll(a, 1))
            lower = jnp.where(end, a * not_last_x, lower)
            middle = h + g + v[1] + jnp.where(first, 0.0, lroll(b, 1)) + lroll(a, -1)
            middle = jnp.where(end, b * not_last_x, middle)
            upper = g + lroll(b, -1)
            upper = jnp.where(end, 0.0, jnp.where(lane == 126, upper * not_last_x, upper))
            for cx, done in enumerate((lower, middle, upper)):
                v = squeeze(done)
                if i < 9:
                    kept[i * 3 + cx] = v
                elif i < 12:
                    sent[(i - 9) * 3 + cx] = v
                elif i == 12:
                    kept[27 + cx] = v
                else:
                    rows[cx] = v
        kept[30] = jnp.where(row < 4, rows[0], sroll(rows[1], 4))
        sent[9] = jnp.where(row < 4, sroll(rows[0], 4), rows[1])
        kept[31] = sent[10] = rows[2]
        for i, v in enumerate(kept):
            w[step, i] = v
        right[step], left[step] = pack_sides(kept)
        plane_right[step], plane_left[step] = pack_sides(sent)
        for i, v in enumerate(pack_plane(sent)):
            plane[step * plane_size(PLANE) + i] = v

    def scales():
        low_x = jnp.where(jnp.logical_and(lane == 0, gx == 0), 0.0, 1.0)
        low_y = jnp.where(jnp.logical_and(row == 0, gy == 0), 0.0, 1.0)
        low_z = (gz > 0).astype(jnp.float32)
        for z in range(4):
            k = classes[z].astype(jnp.float32)
            s = 0.05 + 0.95 * (k * k * k) / 27.0
            for cy in range(2):
                for cx in range(2):
                    v = s
                    if cy:
                        v = v * low_y
                    if cx:
                        v = v * low_x
                    scale[cy * 2 + cx, z] = v
                    if z == 0:
                        scale[cy * 2 + cx, 4] = v * low_z

    def loads():
        items = []
        for c in range(3):
            f = [residual[c, z] for z in range(4)]
            planes = [f[0] + 0.5 * f[1], 0.5 * f[1] + f[2] + 0.5 * f[3], 0.5 * f[3]]
            full, beyond = [], []
            for v in planes:
                h = 0.5 * v
                before = sroll(h, 1)
                full.append(v + sroll(h, -1) + jnp.where(row == 0, 0.0, before))
                beyond.append(h * not_last_y)
            main = jnp.where(even, full[0], sroll(full[1], 1))
            ghost = jnp.where(even, full[2], 0.0)
            for z in range(3):
                ghost = jnp.where(row == 1 + 2 * z, sroll(beyond[z], 2 + 2 * z), ghost)
            items.append((main, ghost))
        vs = []
        for v in [m for m, _ in items] + [g for _, g in items]:
            h = 0.5 * v
            v = v + lroll(h, -1) + jnp.where(lane == 0, 0.0, lroll(h, 1))
            v = jnp.where(lane == 127, h * not_last_x, v)
            vs.append(squeeze(v))
        for i, v in enumerate(vs):
            wl[i] = v

        right[9], left[9] = pack_sides(vs)
        plane_right[9], plane_left[9] = pack_sides(vs[3:])
        for i, v in enumerate(pack_plane(vs[3:])):
            plane[9 * plane_size(PLANE) + i] = v

    classes_copy.wait()
    scales()
    residual_copy.wait()
    loads()

    def body(step, carry):
        fetch(step).wait()
        coarsen(step)
        return carry

    lax.fori_loop(0, 9, body, 0)


def planes_kernel(w, wl, from_left, from_right, plane, plane_left, plane_right, w_out, wl_out, up, down, total):
    row = rows_of()
    even = row % 2 == 0
    total[...] = jnp.zeros_like(total)

    def body(rc, carry):
        got = unpack_plane(lambda i: plane[rc * plane_size(PLANE) + i], PLANE, plane_left[rc], plane_right[rc])
        from_l, from_r = from_left[rc], from_right[rc]
        f = [None] * ITEMS
        for k in range(ITEMS):
            v = w[rc, k] + sides(from_l, from_r, k)
            if k < 9:
                v = v + jnp.where(even, got[k], 0.0)
            elif k < 18:
                v = v + jnp.where(even, sroll(got[k - 9], -1), 0.0)
            elif 27 <= k < 30:
                end = (sroll(got[9], 4), got[9], got[10])[k - 27]
                v = v + jnp.where(even, jnp.where(row < 4, sroll(end, 4), sroll(end, -1)), 0.0)
            f[k] = v
            w_out[rc, k] = v
        magnitude = jnp.abs(f[0])
        for k in range(1, 27):
            magnitude = magnitude + jnp.abs(f[k])
        total[rc // 3] += magnitude
        ups, downs = [], []
        for k in range(0, 27, 2):
            two = f[k + 1] if k + 1 < 27 else None
            ups.append(jnp.where(row < 4, sroll(f[k], 4), sroll(f[31], 4) if two is None else two))
            downs.append(jnp.where(row < 4, f[k], 0.0 if two is None else sroll(two, 4)))
        ups += f[27:31]
        for ref, vs in ((up, ups), (down, downs)):
            for i, v in enumerate(pack(vs)):
                ref[rc * packed_size(len(vs)) + i] = v
        return carry

    lax.fori_loop(0, 9, body, 0)
    got = unpack_plane(lambda i: plane[9 * plane_size(PLANE) + i], 3, plane_left[9], plane_right[9])
    ups, downs = [], []
    for c in range(3):
        load = wl[c] + sides(from_left[9], from_right[9], c) + jnp.where(even, got[c], 0.0)
        ghost = wl[3 + c] + jnp.where(row == 1, sroll(got[c], -4), 0.0)
        ghost = ghost + sides(from_left[9], from_right[9], 3 + c)
        wl_out[c] = load
        wl_out[3 + c] = ghost
        d = load * (1.0 / (total[c] + 1e-06)) / CENTRE
        v = jnp.where(row < 4, sroll(load, 4), 0.0)
        v = jnp.where(row == 4, sroll(ghost, 3), v)
        v = jnp.where(row == 5, sroll(ghost, 2), v)
        ups.append(jnp.where(row >= 6, sroll(d, 4), v))
        downs.append(jnp.where(row < 4, load, jnp.where(row >= 6, sroll(d, 2), 0.0)))
    for ref, vs, size in ((up, ups, packed_size(UPS)), (down, downs, packed_size(DOWNS))):
        for i, v in enumerate(pack(vs)):
            ref[9 * size + i] = v


def piece_rows(n):
    return n + 8 * ((n + 15) // 16)


def share_planes(load, n, piece):
    gz = lax.axis_index("gz")
    even = lax.broadcasted_iota(jnp.int32, (n, 128), 0) % 2 == 0
    d = [load(c) for c in range(3)]
    for z in range(2):
        if z == 0:
            both = jnp.where(even, d[0], pltpu.roll(d[1], 1, 0))
            third = d[2]
        else:
            both = jnp.where(even, pltpu.roll(d[0], n - 1, 0), d[1])
            third = pltpu.roll(d[2], n - 1, 0)
        folds = []
        for at in range(0, n, 16):
            fold = third[at : at + 8]
            if at + 8 < n:
                fold = jnp.where(even[0:8], fold, sroll(third[at + 8 : at + 16], 1))
            folds.append(fold)
        for to in range(piece.shape[0]):
            @pl.when((to >= gz) if z else (to < gz))
            def _():
                piece[to, 0:n] = both
                for i, fold in enumerate(folds):
                    piece[to, n + 8 * i : n + 8 * i + 8] = fold


def plane_of(received, at, n, c):
    if c < 2:
        return received[at, 0:n], c
    parts = []
    for i in range(0, n, 16):
        fold = received[at, n + i // 2 : n + i // 2 + 8]
        parts.append(fold)
        if i + 8 < n:
            parts.append(sroll(fold, -1))
    return jnp.concatenate(parts, axis=0), 0


def rows_kernel(w, wl, from_low, from_high, operator, whole, q, d, inverse, piece, total, turned):
    row = rows_of()
    ghosts = jnp.logical_or(row == 4, row == 5)
    total[...] = jnp.zeros_like(total)

    def body(rc, carry):
        ups = unpack(lambda i: from_low[rc * packed_size(UPS) + i], UPS)
        downs = unpack(lambda i: from_high[rc * packed_size(DOWNS) + i], DOWNS)
        got_ends = [ups[17], sroll(ups[17], 4), sroll(ups[13], 4)]
        own_ends = [w[rc, 30], sroll(w[rc, 30], 4), w[rc, 31]]
        top_sum = jnp.zeros((8, 128), jnp.float32)
        bottom_sum = jnp.zeros((8, 128), jnp.float32)
        for cz in range(3):
            for cy in range(3):
                for cx in range(3):
                    k = cz * 9 + cy * 3 + cx
                    f = sroll(w[rc, k], 4)
                    above, below = ups[k // 2], downs[k // 2]
                    top = jnp.where(row < 4, sroll(above, 4) if k % 2 else above, f)
                    bottom = jnp.where(row < 4, f, below if k % 2 else sroll(below, 4))
                    if cy < 2:
                        at = (cz % 2) * 4 + cy * 2
                        got = ups[14 + cx] if cz < 2 else got_ends[cx]
                        own = w[rc, 27 + cx] if cz < 2 else own_ends[cx]
                        top = top + jnp.where(ghosts, sroll(got, 4 - at), 0.0)
                        bottom = bottom + jnp.where(ghosts, sroll(own, 4 - at), 0.0)
                    whole[rc, k, 0:8] = top
                    whole[rc, k, 8:16] = bottom
                    top_sum = top_sum + jnp.abs(top)
                    bottom_sum = bottom_sum + jnp.abs(bottom)
        total[rc // 3, 0:8] += top_sum
        total[rc // 3, 8:16] += bottom_sum
        for cz in range(3):
            for cy in range(3):
                for cx in range(3):
                    for z in range(2):
                        v = whole[rc, cz * 9 + cy * 3 + cx, pl.ds(4 + z, 4, stride=2), :]
                        operator[cz, cy, cx, rc // 3, rc % 3, z] = v[:, 0:64]
        return carry

    lax.fori_loop(0, 9, body, 0)
    ups = unpack(lambda i: from_low[9 * packed_size(UPS) + i], 3)
    downs = unpack(lambda i: from_high[9 * packed_size(DOWNS) + i], 3)
    for c in range(3):
        load, ghost = sroll(wl[c], 4), wl[3 + c]
        q[c, 0:8] = jnp.where(row < 4, ups[c], load + jnp.where(ghosts, ups[c], 0.0))
        below = sroll(downs[c], 4)
        below = below + jnp.where(row == 4, sroll(ghost, 3), jnp.where(row == 5, sroll(ghost, 2), 0.0))
        q[c, 8:16] = jnp.where(row < 4, load, below)
        part = 1.0 / (total[c] + 1e-06)
        inverse[c] = part
        d[c, 16:24] = jnp.zeros((8, 128), jnp.float32)
        d[c, 2:18] = part * q[c] / CENTRE
        turned[...] = ups[c]
        d[c, 0:2] = turned[6:8]
        turned[...] = downs[c]
        d[c, 18:20] = turned[6:8]
    share_planes(lambda c: d[c], 24, piece)


def apply_to(whole, d, received, n, near, out):
    gz = lax.axis_index("gz")
    even = lax.broadcasted_iota(jnp.int32, (n, 128), 0) % 2 == 0
    below = jnp.maximum(gz - 1, 0)
    above = jnp.minimum(gz + 1, received.shape[0] - 1)
    base = (24 - n) // 4
    for c in range(3):
        own = d[c]
        low, odd = plane_of(received, below, n, c)
        high, _ = plane_of(received, above, n, c)
        if odd:
            low = pltpu.roll(low, n - 1, 0)
        else:
            high = pltpu.roll(high, 1, 0)
        for cz, v in enumerate((
            jnp.where(even, low, pltpu.roll(own, 1, 0)),
            own,
            jnp.where(even, pltpu.roll(own, n - 1, 0), high),
        )):
            if base:
                near[cz, c, 0:8] = jnp.zeros((8, 128), jnp.float32)
                near[cz, c, 16:24] = jnp.zeros((8, 128), jnp.float32)
            near[cz, c, base : base + n] = v
    sums = [jnp.zeros((16, 128), jnp.float32) for _ in range(3)]
    for cz in range(3):
        for cy in range(3):
            for c in range(3):
                v = near[cz, c, pl.ds(2 * cy, 16), :]
                for cx, moved in enumerate((pltpu.roll(v, 1, 1), v, pltpu.roll(v, 127, 1))):
                    for r in range(3):
                        sums[r] = sums[r] + whole[r * 3 + c, cz * 9 + cy * 3 + cx] * moved
    for r in range(3):
        out(r, sums[r])


def step_kernel(first, rho_now, rho_next, last, *refs):
    whole, q, d, inverse, received = refs[:5]
    refs = refs[5:]
    if first:
        x = None
    else:
        x, refs = refs[0], refs[1:]
    if last:
        solution_out, near, turned = refs
    else:
        q_out, d_out, x_out, piece, near = refs

    def update(r, product):
        now = d[r, 2:18] if first else d[r]
        x_now = now if x is None else x[r] + now
        q_now = q[r] - product
        d_new = rho_next * rho_now * now + 2.0 * rho_next / HALF * (inverse[r] * q_now)
        if last:
            turned[...] = x_now + d_new
            for z in range(2):
                solution_out[r, z] = turned[pl.ds(4 + z, 4, stride=2), :][:, 0:64]
        else:
            x_out[r] = x_now
            q_out[r] = q_now
            d_out[r] = d_new

    apply_to(whole, d, received, 24 if first else 16, near, update)
    if not last:
        share_planes(lambda c: d_out[c], 16, piece)


def shape(*dims):
    return jax.ShapeDtypeStruct(dims, jnp.float32)


def along(block, axes, distances):
    sizes = [lax.axis_size(a) for a in axes]
    route = []
    for source in itertools.product(*[range(n) for n in sizes]):
        target = [i + s for i, s in zip(source, distances)]
        if all(0 <= i < n for i, n in zip(target, sizes)):
            flat = [functools.reduce(lambda t, p: t * p[1] + p[0], zip(at, sizes), 0) for at in (source, target)]
            route.append(tuple(flat))
    return lax.ppermute(block, axes, route)


def shards(blocks, classes, residual):
    nz = lax.axis_size("gz")
    w_shape, wl_shape = shape(9, ITEMS, 8, 128), shape(6, 8, 128)
    side = shape(10, 8, 128)
    w, wl, right, left, plane, plane_right, plane_left_sent = pl.pallas_call(
        coarsen_kernel,
        in_specs=[HBM] * 3,
        out_specs=[VMEM] * 7,
        out_shape=[w_shape, wl_shape, side, side, shape(9 * plane_size(PLANE) + plane_size(3), 8, 128), side, side],
        scratch_shapes=[
            pltpu.VMEM((9, 3, 3, 3, 4, 8, 128), jnp.float32),
            pltpu.VMEM((4, 8, 128), jnp.int32),
            pltpu.VMEM((3, 4, 8, 128), jnp.float32),
            pltpu.VMEM((4, 5, 8, 128), jnp.float32),
            pltpu.SemaphoreType.DMA((11,)),
        ],
        compiler_params=LIMIT,
    )(*(pltpu.with_memory_space_constraint(v, pltpu.HBM) for v in (blocks, classes, residual)))
    plane = along(plane, ("gz",), (1,))
    from_left, from_right = along(right, ("gx",), (1,)), along(left, ("gx",), (-1,))
    plane_left = along(plane_right, ("gx", "gz"), (1, 1))
    plane_right = along(plane_left_sent, ("gx", "gz"), (-1, 1))
    w, wl, up, down = pl.pallas_call(
        planes_kernel,
        in_specs=[VMEM] * 7,
        out_specs=[VMEM] * 4,
        out_shape=[w_shape, wl_shape, shape(9 * packed_size(UPS) + packed_size(3), 8, 128), shape(9 * packed_size(DOWNS) + packed_size(3), 8, 128)],
        scratch_shapes=[pltpu.VMEM((3, 8, 128), jnp.float32)],
        compiler_params=LIMIT,
    )(w, wl, from_left, from_right, plane, plane_left, plane_right)
    from_low, from_high = along(up, ("gy",), (1,)), along(down, ("gy",), (-1,))
    operator, whole, q, d, inverse, piece = pl.pallas_call(
        rows_kernel,
        in_specs=[VMEM] * 4,
        out_specs=[VMEM] * 6,
        out_shape=[
            shape(3, 3, 3, 3, 3, 2, 4, 64),
            shape(9, 27, 16, 128),
            shape(3, 16, 128),
            shape(3, 24, 128),
            shape(3, 16, 128),
            shape(nz, piece_rows(24), 128),
        ],
        scratch_shapes=[pltpu.VMEM((3, 16, 128), jnp.float32), pltpu.VMEM((8, 128), jnp.float32)],
        compiler_params=LIMIT,
    )(w, wl, from_low, from_high)
    x = []
    rho_now = 1.0 / SIGMA
    for step in range(STEPS - 1):
        rho_next = 1.0 / (2.0 * SIGMA - rho_now)
        last = step == STEPS - 2
        shared = lax.all_to_all(piece, "gz", 0, 0)
        if last:
            outs = shape(3, 2, 4, 64)
        else:
            outs = [shape(3, 16, 128), shape(3, 16, 128), shape(3, 16, 128), shape(nz, piece_rows(16), 128)]
        done = pl.pallas_call(
            functools.partial(step_kernel, step == 0, rho_now, rho_next, last),
            in_specs=[VMEM] * (5 + len(x)),
            out_specs=VMEM if last else [VMEM] * 4,
            out_shape=outs,
            scratch_shapes=[pltpu.VMEM((3, 3, 24, 128), jnp.float32)] + ([pltpu.VMEM((16, 128), jnp.float32)] if last else []),
            compiler_params=LIMIT,
        )(whole, q, d, inverse, shared, *x)
        if last:
            return operator, done
        q, d, x, piece = done
        x = [x]
        rho_now = rho_next


def solution(mesh):
    placed = (
        P(None, None, None, None, None, "gz", "gy", "gx"),
        P("gz", "gy", "gx"),
        P(None, "gz", "gy", "gx"),
    )
    return jax.shard_map(
        shards,
        mesh=mesh,
        in_specs=placed,
        out_specs=(P(None, None, None, None, None, "gz", "gy", "gx"), P(None, "gz", "gy", "gx")),
        check_vma=False,
    )
```

time: 81.4 us -> 74.4 us (0.914)
  starting transfers between devices: 15.3 us -> 25.4 us
  blocking collectives: 32.6 us -> 25.7 us
  waiting for transfers between devices: 15.9 us -> 10.8 us
  local copies, waits for them, and re-layouts: 3.64 us -> 0 us
  Pallas kernels: 12.8 us -> 11.4 us
    ppermute x5 -> x7, starting transfers between devices: 15.3 us -> 25.4 us  [along(): return lax.ppermute(block, axes, route)]
    all_to_all x3, blocking collectives: 32.6 us -> 25.7 us  [shards(): shared = lax.all_to_all(piece, 'gz', 0, 0)]
    ppermute x5 -> x7, waiting for transfers between devices: 15.9 us -> 10.8 us  [along(): return lax.ppermute(block, axes, route)]
    unnamed x6 -> x0, local copies, waits for them, and re-layouts: 3.64 us -> none
    pallas_call x3 -> x2, Pallas kernels: 9.07 us -> 7.54 us  [the longest x1 5.16 us: shards(): pl.pallas_call(coarsen_kernel, in_specs=[HBM] * 3, out_specs=[VMEM] * 7,...]
  transfers between devices with their start and end apart: 5 -> 7, of which waited for: 4 -> 3; matrix products, arithmetic and copies ran while one was open for 0% -> 0% of each run, Pallas kernels for 0% -> 0%
where the time goes in v1:
time: 74.4 us; the launch traced here: 73.9 us
  blocking collectives  25.7 us (35%)
  starting transfers between devices  25.4 us (34%)
  Pallas kernels  11.4 us (15%)
  waiting for transfers between devices  10.8 us (15%)
    all_to_all x3, blocking collectives, shards(): shared = lax.all_to_all(piece, 'gz', 0, 0)  25.7 us
    ppermute x7, starting transfers between devices, along(): return lax.ppermute(block, axes, route)  25.4 us
    ppermute x7, waiting for transfers between devices, along(): return lax.ppermute(block, axes, route)  10.8 us
    pallas_call x1, Pallas kernels, shards(): pl.pallas_call(coarsen_kernel, in_specs=[HBM] * 3, out_specs=[VMEM] * 7,...  5.16 us
    pallas_call x1, Pallas kernels, shards(): pl.pallas_call(rows_kernel, in_specs=[VMEM] * 4, out_specs=[VMEM] * 6, ou...  2.42 us
    pallas_call x1, Pallas kernels, shards(): pl.pallas_call(planes_kernel, in_specs=[VMEM] * 7, out_specs=[VMEM] * 4,...  2.38 us
  transfers between devices with their start and end apart: 7, of which 3 were waited for; matrix products, arithmetic and copies ran while one was open for 0% of the time, Pallas kernels for 0%

profile of v1, /device:TPU:218, one launch (start us, length us, event | category | flops | bytes accessed | tf_op | source)
XLA Modules:
  0.0 73.9 jit_solution(3750307813480209905)
XLA Ops:
  0.6 5.2 %shard_map.50 = (f32[9,32,8,128]{3,2,1,0:T(8,128)S(1)}, f32[6,8,128]{2,1,0:T(8,128)S(1)}, f32[10,8,128]{2,1,0:T(8,128)S(1)}, f32[10,8,128]{2,1,0:T(8,128)S(1)}, ...) custom-call(f32[3,3,3,3,3,4,8,128]{7,6,5,4,3,2,1,0:T(8,128)} %blocks_in.1, ...), custom_call_target="tpu_custom_call" | custom-call | tf_op jit(solution)/shard_map/pallas_call | solution.py:539
  5.8 1.8 %collective-permute-start.2 = (f32[56,8,128]{2,1,0:T(8,128)S(1)}, f32[56,8,128]{2,1,0:T(8,128)S(1)}, u32[]{:S(2)}, u32[]{:S(2)}) collective-permute-start(f32[56,8,128]{2,1,0:T(8,128)S(1)} %get-tuple-element.31), channel_id=1, source_target_pairs={{0,1},{1,2},{2,3},{4,5},{5,6},{6,7},{8,9},{9,10},{10,11},{12,13},{... | collective-permute-start | bytes 688136 | tf_op jit(solution)/shard_map/ppermute | solution.py:532
  7.6 5.5 %collective-permute-start = (f32[10,8,128]{2,1,0:T(8,128)S(1)}, f32[10,8,128]{2,1,0:T(8,128)S(1)}, u32[]{:S(2)}, u32[]{:S(2)}) collective-permute-start(f32[10,8,128]{2,1,0:T(8,128)S(1)} %get-tuple-element.29), channel_id=1, source_target_pairs={{0,32},{32,64},{64,96},{96,128},{128,160},{160,192},{192,224},{224... | collective-permute-start | bytes 122888 | tf_op jit(solution)/shard_map/ppermute | solution.py:532
  13.0 1.9 %collective-permute-start.1 = (f32[10,8,128]{2,1,0:T(8,128)S(1)}, f32[10,8,128]{2,1,0:T(8,128)S(1)}, u32[]{:S(2)}, u32[]{:S(2)}) collective-permute-start(f32[10,8,128]{2,1,0:T(8,128)S(1)} %get-tuple-element.30), channel_id=1, source_target_pairs={{32,0},{64,32},{96,64},{128,96},{160,128},{192,160},{224,192},{256... | collective-permute-start | bytes 122888 | tf_op jit(solution)/shard_map/ppermute | solution.py:532
  15.0 8.4 %collective-permute-start.3 = (f32[10,8,128]{2,1,0:T(8,128)S(1)}, f32[10,8,128]{2,1,0:T(8,128)S(1)}, u32[]{:S(2)}, u32[]{:S(2)}) collective-permute-start(f32[10,8,128]{2,1,0:T(8,128)S(1)} %get-tuple-element.32), channel_id=1, source_target_pairs={{0,33},{1,34},{2,35},{32,65},{33,66},{34,67},{64,97},{65,98},{66,9... | collective-permute-start | bytes 122888 | tf_op jit(solution)/shard_map/ppermute | solution.py:532
  23.3 1.3 %collective-permute-start.4 = (f32[10,8,128]{2,1,0:T(8,128)S(1)}, f32[10,8,128]{2,1,0:T(8,128)S(1)}, u32[]{:S(2)}, u32[]{:S(2)}) collective-permute-start(f32[10,8,128]{2,1,0:T(8,128)S(1)} %get-tuple-element.33), channel_id=1, source_target_pairs={{32,1},{33,2},{34,3},{64,33},{65,34},{66,35},{96,65},{97,66},{98,6... | collective-permute-start | bytes 122888 | tf_op jit(solution)/shard_map/ppermute | solution.py:532
  24.6 0.0 collective-permute-done.from_left
  24.6 0.0 collective-permute-done.1.from_right
  24.7 0.3 collective-permute-done.3.plane_left
  25.0 1.3 %collective-permute-done.4.plane_right = f32[10,8,128]{2,1,0:T(8,128)S(1)} collective-permute-done((f32[10,8,128]{2,1,0:T(8,128)S(1)}, f32[10,8,128]{2,1,0:T(8,128)S(1)}, u32[]{:S(2)}, u32[]{:S(2)}) %collective-permute-start.4) | collective-permute-done | bytes 40992 | tf_op jit(solution)/shard_map/ppermute | solution.py:532
  26.3 0.0 collective-permute-done.2.plane
  26.3 2.4 %shard_map.51 = (f32[9,32,8,128]{3,2,1,0:T(8,128)S(1)}, f32[6,8,128]{2,1,0:T(8,128)S(1)}, f32[93,8,128]{2,1,0:T(8,128)S(1)}, f32[75,8,128]{2,1,0:T(8,128)S(1)}) custom-call(f32[9,32,8,128]{3,2,1,0:T(8,128)S(1)} %get-tuple-element.27.w, f32[6,8,128]{2,1,0:T(8,128)S(1)} %get-tuple-element.28.wl, f32[10,8,128]{2,1,0:T(8,128)S(1)} %collective-permute-done.from_left, ...), custom_call_target="tpu_custom_call" | custom-call | tf_op jit(solution)/shard_map/pallas_call | solution.py:557
  28.7 4.7 %collective-permute-start.5 = (f32[93,8,128]{2,1,0:T(8,128)S(1)}, f32[93,8,128]{2,1,0:T(8,128)S(1)}, u32[]{:S(2)}, u32[]{:S(2)}) collective-permute-start(f32[93,8,128]{2,1,0:T(8,128)S(1)} %get-tuple-element.36), channel_id=1, source_target_pairs={{0,4},{4,8},{8,12},{12,16},{16,20},{20,24},{24,28},{1,5},{5,9},{9,... | collective-permute-start | bytes 1142792 | tf_op jit(solution)/shard_map/ppermute | solution.py:532
  33.4 1.9 %collective-permute-start.6 = (f32[75,8,128]{2,1,0:T(8,128)S(1)}, f32[75,8,128]{2,1,0:T(8,128)S(1)}, u32[]{:S(2)}, u32[]{:S(2)}) collective-permute-start(f32[75,8,128]{2,1,0:T(8,128)S(1)} %get-tuple-element.37), channel_id=1, source_target_pairs={{4,0},{8,4},{12,8},{16,12},{20,16},{24,20},{28,24},{5,1},{9,5},{13... | collective-permute-start | bytes 921608 | tf_op jit(solution)/shard_map/ppermute | solution.py:532
  35.3 9.1 %collective-permute-done.6.from_high = f32[75,8,128]{2,1,0:T(8,128)S(1)} collective-permute-done((f32[75,8,128]{2,1,0:T(8,128)S(1)}, f32[75,8,128]{2,1,0:T(8,128)S(1)}, u32[]{:S(2)}, u32[]{:S(2)}) %collective-permute-start.6) | collective-permute-done | bytes 307232 | tf_op jit(solution)/shard_map/ppermute | solution.py:532
  44.4 0.0 collective-permute-done.5.from_low
  44.4 2.4 %shard_map.52 = (f32[3,3,3,3,3,2,4,64]{7,6,5,4,3,2,1,0:T(4,128)}, f32[9,27,16,128]{3,2,1,0:T(8,128)S(1)}, f32[3,16,128]{2,1,0:T(8,128)S(1)}, f32[3,24,128]{2,1,0...) custom-call(f32[9,32,8,128]{3,2,1,0:T(8,128)S(1)} %get-tuple-element.34.w, ...), custom_call_target="tpu_custom_call" | custom-call | tf_op jit(solution)/shard_map/pallas_call | solution.py:566
  46.9 9.9 %all_to_all.15.refs_4_ = f32[4,40,128]{2,1,0:T(8,128)S(1)} all-to-all(f32[4,40,128]{2,1,0:T(8,128)S(1)} %get-tuple-element.43), channel_id=1, replica_groups=mesh['gx'=16,'gy'=8,'gz'=4] {'gz'}, dimensions={0} | all-to-all | bytes 163840 | tf_op jit(solution)/shard_map/all_to_all | solution.py:586
  56.7 0.3 shard_map.53
  57.0 7.9 %all_to_all.16.refs_4_ = f32[4,24,128]{2,1,0:T(8,128)S(1)} all-to-all(f32[4,24,128]{2,1,0:T(8,128)S(1)} %get-tuple-element.46), channel_id=1, replica_groups=mesh['gx'=16,'gy'=8,'gz'=4] {'gz'}, dimensions={0} | all-to-all | bytes 98304 | tf_op jit(solution)/shard_map/all_to_all | solution.py:586
  64.9 0.3 shard_map.54
  65.2 7.9 %all_to_all.17.refs_4_ = f32[4,24,128]{2,1,0:T(8,128)S(1)} all-to-all(f32[4,24,128]{2,1,0:T(8,128)S(1)} %get-tuple-element.50), channel_id=1, replica_groups=mesh['gx'=16,'gy'=8,'gz'=4] {'gz'}, dimensions={0} | all-to-all | bytes 98304 | tf_op jit(solution)/shard_map/all_to_all | solution.py:586
  73.1 0.9 %shard_map.55 = f32[3,2,4,64]{3,2,1,0:T(4,128)} custom-call(f32[9,27,16,128]{3,2,1,0:T(8,128)S(1)} %get-tuple-element.39.refs_0_, f32[3,16,128]{2,1,0:T(8,128)S(1)} %get-tuple-element.48.refs_1_, f32[3,16,128]{2,1,0:T(8,128)S(1)} %get-tuple-element.49.refs_2_, f32[3,16,128]{2,1,0:T(8,128)S(1)} %get-tuple-element.42.refs_3_, ...), custom_call_target="tpu_custom_call" | custom-call | tf_op jit(solution)/shard_map/pallas_call | solution.py:591
Async XLA Ops:
  5.8 20.5 %collective-permute-start.2 = (f32[56,8,128]{2,1,0:T(8,128)S(1)}, f32[56,8,128]{2,1,0:T(8,128)S(1)}, u32[]{:S(2)}, u32[]{:S(2)}) collective-permute-start(f32[56,8,128]{2,1,0:T(8,128)S(1)} %get-tuple-element.31), channel_id=1, source_target_pairs={{0,1},{1,2},{2,3},{4,5},{5,6},{6,7},{8,9},{9,10},{10,11},{12,13},{... | collective-permute-start | bytes 688136 | tf_op jit(solution)/shard_map/ppermute | solution.py:532
  7.6 17.1 %collective-permute-start = (f32[10,8,128]{2,1,0:T(8,128)S(1)}, f32[10,8,128]{2,1,0:T(8,128)S(1)}, u32[]{:S(2)}, u32[]{:S(2)}) collective-permute-start(f32[10,8,128]{2,1,0:T(8,128)S(1)} %get-tuple-element.29), channel_id=1, source_target_pairs={{0,32},{32,64},{64,96},{96,128},{128,160},{160,192},{192,224},{224... | collective-permute-start | bytes 122888 | tf_op jit(solution)/shard_map/ppermute | solution.py:532
  13.0 11.6 %collective-permute-start.1 = (f32[10,8,128]{2,1,0:T(8,128)S(1)}, f32[10,8,128]{2,1,0:T(8,128)S(1)}, u32[]{:S(2)}, u32[]{:S(2)}) collective-permute-start(f32[10,8,128]{2,1,0:T(8,128)S(1)} %get-tuple-element.30), channel_id=1, source_target_pairs={{32,0},{64,32},{96,64},{128,96},{160,128},{192,160},{224,192},{256... | collective-permute-start | bytes 122888 | tf_op jit(solution)/shard_map/ppermute | solution.py:532
  15.0 10.0 %collective-permute-start.3 = (f32[10,8,128]{2,1,0:T(8,128)S(1)}, f32[10,8,128]{2,1,0:T(8,128)S(1)}, u32[]{:S(2)}, u32[]{:S(2)}) collective-permute-start(f32[10,8,128]{2,1,0:T(8,128)S(1)} %get-tuple-element.32), channel_id=1, source_target_pairs={{0,33},{1,34},{2,35},{32,65},{33,66},{34,67},{64,97},{65,98},{66,9... | collective-permute-start | bytes 122888 | tf_op jit(solution)/shard_map/ppermute | solution.py:532
  23.3 3.0 %collective-permute-start.4 = (f32[10,8,128]{2,1,0:T(8,128)S(1)}, f32[10,8,128]{2,1,0:T(8,128)S(1)}, u32[]{:S(2)}, u32[]{:S(2)}) collective-permute-start(f32[10,8,128]{2,1,0:T(8,128)S(1)} %get-tuple-element.33), channel_id=1, source_target_pairs={{32,1},{33,2},{34,3},{64,33},{65,34},{66,35},{96,65},{97,66},{98,6... | collective-permute-start | bytes 122888 | tf_op jit(solution)/shard_map/ppermute | solution.py:532
  28.7 15.8 %collective-permute-start.5 = (f32[93,8,128]{2,1,0:T(8,128)S(1)}, f32[93,8,128]{2,1,0:T(8,128)S(1)}, u32[]{:S(2)}, u32[]{:S(2)}) collective-permute-start(f32[93,8,128]{2,1,0:T(8,128)S(1)} %get-tuple-element.36), channel_id=1, source_target_pairs={{0,4},{4,8},{8,12},{12,16},{16,20},{20,24},{24,28},{1,5},{5,9},{9,... | collective-permute-start | bytes 1142792 | tf_op jit(solution)/shard_map/ppermute | solution.py:532
  33.4 11.1 %collective-permute-start.6 = (f32[75,8,128]{2,1,0:T(8,128)S(1)}, f32[75,8,128]{2,1,0:T(8,128)S(1)}, u32[]{:S(2)}, u32[]{:S(2)}) collective-permute-start(f32[75,8,128]{2,1,0:T(8,128)S(1)} %get-tuple-element.37), channel_id=1, source_target_pairs={{4,0},{8,4},{12,8},{16,12},{20,16},{24,20},{28,24},{5,1},{9,5},{13... | collective-permute-start | bytes 921608 | tf_op jit(solution)/shard_map/ppermute | solution.py:532

commit v2 on v1

--- a/solution.py
+++ b/solution.py
@@ -18,6 +18,7 @@
 ITEMS = 32
 PLANE = 11
 UPS, DOWNS = 18, 14
+AHEAD = 3
 VMEM = pl.BlockSpec(memory_space=pltpu.VMEM)
 HBM = pl.BlockSpec(memory_space=pltpu.HBM)
 LIMIT = pltpu.CompilerParams(vmem_limit_bytes=40 * 1024 * 1024)
@@ -132,12 +133,6 @@
     return out
 
 
-def halves(minus, zero, plus):
-    h, g = 0.5 * minus, 0.5 * plus
-    quarter = 0.25 * zero
-    return h, g, h + quarter, g + quarter
-
-
 def coarsen_kernel(blocks_in, classes_in, residual_in, w, wl, right, left, plane, plane_right, plane_left, blocks, classes, residual, scale, sems):
     def fetch(i):
         source = blocks_in.at[:, :, :, i // 3, i % 3]
@@ -148,13 +143,19 @@
     classes_copy.start()
     fetch(0).start()
     residual_copy.start()
-    for i in range(1, 9):
+    for i in range(1, AHEAD):
         fetch(i).start()
     gx, gy, gz = (lax.axis_index(a) for a in ("gx", "gy", "gz"))
     lane, row = lanes_of(), rows_of()
     even = row % 2 == 0
     not_last_x = (gx < lax.axis_size("gx") - 1).astype(jnp.float32)
+    last_x = gx == lax.axis_size("gx") - 1
     not_last_y = (gy < lax.axis_size("gy") - 1).astype(jnp.float32)
+    keep_y = jnp.logical_or(row < 6, gy < lax.axis_size("gy") - 1)
+    inner = lane < 64
+    upper_x = jnp.logical_and(inner, jnp.logical_or(lane < 63, jnp.logical_not(last_x)))
+    after_x = jnp.logical_and(lane > 0, jnp.logical_or(inner, jnp.logical_and(lane == 64, jnp.logical_not(last_x))))
+    apart = jnp.where(inner, 2 * lane, 2 * lane - 127)
     not_last_z = (gz < lax.axis_size("gz") - 1).astype(jnp.float32)
     pick = jnp.where(lane < 64, 2 * lane, 127) % 128
 
@@ -171,51 +172,46 @@
                 s = [[None] * 4 for _ in range(3)]
                 for oz in range(3):
                     for z in range(4):
-                        factor = scale[kind, 4 if (z == 0 and oz == 0) else z]
+                        factor = scale[kind, 5 + z if oz == 1 else 4 if (z == 0 and oz == 0) else z]
                         s[oz][z] = blocks[step, oz, oy, ox, z] * factor
-                _, _, a1, b1 = halves(s[0][1], s[1][1], s[2][1])
-                _, _, a3, b3 = halves(s[0][3], s[1][3], s[2][3])
-                h0, g0 = 0.5 * s[0][0], 0.5 * s[2][0]
-                h2, g2 = 0.5 * s[0][2], 0.5 * s[2][2]
-                slots[0, 0, oy] = h0
-                slots[1, 0, oy] = h0 + g0 + s[1][0] + a1
-                slots[2, 0, oy] = g0 + b1
-                slots[0, 1, oy] = h2 + a1
-                slots[1, 1, oy] = h2 + g2 + s[1][2] + b1 + a3
-                slots[2, 1, oy] = (g2 + b3) * not_last_z
+                a1, b1 = s[0][1] + s[1][1], s[2][1] + s[1][1]
+                a3, b3 = s[0][3] + s[1][3], s[2][3] + s[1][3]
+                slots[0, 0, oy] = s[0][0]
+                slots[1, 0, oy] = s[0][0] + s[2][0] + s[1][0] + a1
+                slots[2, 0, oy] = s[2][0] + b1
+                slots[0, 1, oy] = s[0][2] + a1
+                slots[1, 1, oy] = s[0][2] + s[2][2] + s[1][2] + b1 + a3
+                slots[2, 1, oy] = (s[2][2] + b3) * not_last_z
                 slots[3, 0, oy] = a3
                 slots[3, 1, oy] = b3
-            beyond = [jnp.zeros((8, 128), jnp.float32) for _ in range(2)]
+            beyond = [None, None]
             for slot in range(4):
-                parts = []
-                for z in range(2):
-                    v = [slots[slot, z, oy] for oy in range(3)]
-                    h, g, a, b = halves(*v)
-                    first = row == 0
-                    lower = h + jnp.where(first, 0.0, sroll(a, 1))
-                    middle = h + g + v[1] + jnp.where(first, 0.0, sroll(b, 1)) + sroll(a, -1)
-                    upper = g + sroll(b, -1)
-                    upper = jnp.where(row == 6, upper * not_last_y, upper)
-                    parts.append((lower, middle, upper))
-                    for cy, ghost in enumerate((a, b)):
-                        at = (slot % 2) * 4 + cy * 2 + z
-                        beyond[slot // 2] = jnp.where(row == at, sroll(ghost, at + 1) * not_last_y, beyond[slot // 2])
-                for cy in range(3):
-                    ydone[slot * 3 + cy, ox] = jnp.where(even, parts[0][cy], sroll(parts[1][cy], 1))
+                ev, od = [], []
+                for oy in range(3):
+                    z0, z1 = slots[slot, 0, oy], slots[slot, 1, oy]
+                    ev.append(jnp.where(even, z0, sroll(z1, 1)))
+                    od.append(jnp.where(even, sroll(z0, -1), z1))
+                half = 0.5 * od[1]
+                a, b = od[0] + half, od[2] + half
+                a_before, b_before = sroll(a, 2), sroll(b, 2)
+                ydone[slot * 3, ox] = ev[0] + jnp.where(row < 2, 0.0, a_before)
+                ydone[slot * 3 + 1, ox] = ev[0] + ev[2] + (ev[1] + ev[1]) + a + jnp.where(row < 2, 0.0, b_before)
+                ydone[slot * 3 + 2, ox] = jnp.where(keep_y, ev[2] + b, 0.0)
+                if slot % 2 == 0:
+                    beyond[slot // 2] = jnp.where(row < 2, a_before, sroll(b, 4))
+                else:
+                    ends = jnp.where(row < 6, sroll(a, 6), b)
+                    beyond[slot // 2] = jnp.where(row < 4, beyond[slot // 2], ends) * not_last_y
             ydone[12, ox], ydone[13, ox] = beyond
         kept, sent, rows = [None] * ITEMS, [None] * PLANE, {}
         for i in range(14):
-            v = [ydone[i, ox] for ox in range(3)]
-            h, g, a, b = halves(*v)
-            first, end = lane == 0, lane == 127
-            lower = h + jnp.where(first, 0.0, lroll(a, 1))
-            lower = jnp.where(end, a * not_last_x, lower)
-            middle = h + g + v[1] + jnp.where(first, 0.0, lroll(b, 1)) + lroll(a, -1)
-            middle = jnp.where(end, b * not_last_x, middle)
-            upper = g + lroll(b, -1)
-            upper = jnp.where(end, 0.0, jnp.where(lane == 126, upper * not_last_x, upper))
-            for cx, done in enumerate((lower, middle, upper)):
-                v = squeeze(done)
+            v = [jnp.take_along_axis(ydone[i, ox], apart, axis=1, mode="promise_in_bounds") for ox in range(3)]
+            half = 0.5 * v[1]
+            a, b = v[0] + half, v[2] + half
+            lower = jnp.where(inner, v[0], 0.0) + jnp.where(after_x, lroll(a, 65), 0.0)
+            middle = jnp.where(inner, v[0] + v[2] + (v[1] + v[1]) + lroll(a, 64), 0.0) + jnp.where(after_x, lroll(b, 65), 0.0)
+            upper = jnp.where(upper_x, v[2] + lroll(b, 64), 0.0)
+            for cx, v in enumerate((lower, middle, upper)):
                 if i < 9:
                     kept[i * 3 + cx] = v
                 elif i < 12:
@@ -240,7 +236,7 @@
         low_z = (gz > 0).astype(jnp.float32)
         for z in range(4):
             k = classes[z].astype(jnp.float32)
-            s = 0.05 + 0.95 * (k * k * k) / 27.0
+            s = 0.125 * (0.05 + 0.95 * (k * k * k) / 27.0)
             for cy in range(2):
                 for cx in range(2):
                     v = s
@@ -249,6 +245,7 @@
                     if cx:
                         v = v * low_x
                     scale[cy * 2 + cx, z] = v
+                    scale[cy * 2 + cx, 5 + z] = (0.5 if z % 2 else 2.0) * v
                     if z == 0:
                         scale[cy * 2 + cx, 4] = v * low_z
 
@@ -289,13 +286,18 @@
 
     def body(step, carry):
         fetch(step).wait()
+
+        @pl.when(step + AHEAD < 9)
+        def _():
+            fetch(step + AHEAD).start()
+
         coarsen(step)
         return carry
 
-    lax.fori_loop(0, 9, body, 0)
-
-
-def planes_kernel(w, wl, from_left, from_right, plane, plane_left, plane_right, w_out, wl_out, up, down, total):
+    lax.fori_loop(0, 9, body, 0, unroll=9)
+
+
+def planes_kernel(plane_left, from_left, plane_right, from_right, plane, w, wl, w_out, wl_out, up, down, total):
     row = rows_of()
     even = row % 2 == 0
     total[...] = jnp.zeros_like(total)
@@ -330,7 +332,7 @@
                 ref[rc * packed_size(len(vs)) + i] = v
         return carry
 
-    lax.fori_loop(0, 9, body, 0)
+    lax.fori_loop(0, 9, body, 0, unroll=9)
     got = unpack_plane(lambda i: plane[9 * plane_size(PLANE) + i], 3, plane_left[9], plane_right[9])
     ups, downs = [], []
     for c in range(3):
@@ -354,10 +356,11 @@
     return n + 8 * ((n + 15) // 16)
 
 
-def share_planes(load, n, piece):
-    gz = lax.axis_index("gz")
+def share_planes(load, n, to_other, to_pair):
+    low_of_pair = lax.axis_index("gz") % 2 == 0
     even = lax.broadcasted_iota(jnp.int32, (n, 128), 0) % 2 == 0
     d = [load(c) for c in range(3)]
+    sent = []
     for z in range(2):
         if z == 0:
             both = jnp.where(even, d[0], pltpu.roll(d[1], 1, 0))
@@ -371,27 +374,24 @@
             if at + 8 < n:
                 fold = jnp.where(even[0:8], fold, sroll(third[at + 8 : at + 16], 1))
             folds.append(fold)
-        for to in range(piece.shape[0]):
-            @pl.when((to >= gz) if z else (to < gz))
-            def _():
-                piece[to, 0:n] = both
-                for i, fold in enumerate(folds):
-                    piece[to, n + 8 * i : n + 8 * i + 8] = fold
-
-
-def plane_of(received, at, n, c):
+        sent.append(jnp.concatenate([both] + folds, axis=0))
+    to_pair[...] = jnp.where(low_of_pair, sent[1], sent[0])
+    to_other[...] = jnp.where(low_of_pair, sent[0], sent[1])
+
+
+def plane_of(piece, n, c):
     if c < 2:
-        return received[at, 0:n], c
+        return piece[0:n], c
     parts = []
     for i in range(0, n, 16):
-        fold = received[at, n + i // 2 : n + i // 2 + 8]
+        fold = piece[n + i // 2 : n + i // 2 + 8]
         parts.append(fold)
         if i + 8 < n:
             parts.append(sroll(fold, -1))
     return jnp.concatenate(parts, axis=0), 0
 
 
-def rows_kernel(w, wl, from_low, from_high, operator, whole, q, d, inverse, piece, total, turned):
+def rows_kernel(w, wl, from_low, from_high, whole, q, d, inverse, to_other, to_pair, total, turned):
     row = rows_of()
     ghosts = jnp.logical_or(row == 4, row == 5)
     total[...] = jnp.zeros_like(total)
@@ -423,15 +423,9 @@
                     bottom_sum = bottom_sum + jnp.abs(bottom)
         total[rc // 3, 0:8] += top_sum
         total[rc // 3, 8:16] += bottom_sum
-        for cz in range(3):
-            for cy in range(3):
-                for cx in range(3):
-                    for z in range(2):
-                        v = whole[rc, cz * 9 + cy * 3 + cx, pl.ds(4 + z, 4, stride=2), :]
-                        operator[cz, cy, cx, rc // 3, rc % 3, z] = v[:, 0:64]
         return carry
 
-    lax.fori_loop(0, 9, body, 0)
+    lax.fori_loop(0, 9, body, 0, unroll=9)
     ups = unpack(lambda i: from_low[9 * packed_size(UPS) + i], 3)
     downs = unpack(lambda i: from_high[9 * packed_size(DOWNS) + i], 3)
     for c in range(3):
@@ -448,19 +442,31 @@
         d[c, 0:2] = turned[6:8]
         turned[...] = downs[c]
         d[c, 18:20] = turned[6:8]
-    share_planes(lambda c: d[c], 24, piece)
-
-
-def apply_to(whole, d, received, n, near, out):
-    gz = lax.axis_index("gz")
+    share_planes(lambda c: d[c], 24, to_other, to_pair)
+
+
+def operator_kernel(whole, operator):
+    def body(rc, carry):
+        for k in range(27):
+            for z in range(2):
+                v = whole[rc, k, pl.ds(4 + z, 4, stride=2), :]
+                operator[k // 9, k // 3 % 3, k % 3, rc // 3, rc % 3, z] = v[:, 0:64]
+        return carry
+
+    lax.fori_loop(0, 9, body, 0, unroll=3)
+
+
+def apply_to(whole, d, from_other, from_pair, n, near, out):
+    low_of_pair = lax.axis_index("gz") % 2 == 0
     even = lax.broadcasted_iota(jnp.int32, (n, 128), 0) % 2 == 0
-    below = jnp.maximum(gz - 1, 0)
-    above = jnp.minimum(gz + 1, received.shape[0] - 1)
+    other, pair = from_other[...], from_pair[...]
+    below = jnp.where(low_of_pair, other, pair)
+    above = jnp.where(low_of_pair, pair, other)
     base = (24 - n) // 4
     for c in range(3):
         own = d[c]
-        low, odd = plane_of(received, below, n, c)
-        high, _ = plane_of(received, above, n, c)
+        low, odd = plane_of(below, n, c)
+        high, _ = plane_of(above, n, c)
         if odd:
             low = pltpu.roll(low, n - 1, 0)
         else:
@@ -487,8 +493,8 @@
 
 
 def step_kernel(first, rho_now, rho_next, last, *refs):
-    whole, q, d, inverse, received = refs[:5]
-    refs = refs[5:]
+    whole, q, d, inverse, from_other, from_pair = refs[:6]
+    refs = refs[6:]
     if first:
         x = None
     else:
@@ -496,7 +502,7 @@
     if last:
         solution_out, near, turned = refs
     else:
-        q_out, d_out, x_out, piece, near = refs
+        q_out, d_out, x_out, to_other, to_pair, near = refs
 
     def update(r, product):
         now = d[r, 2:18] if first else d[r]
@@ -512,9 +518,9 @@
             q_out[r] = q_now
             d_out[r] = d_new
 
-    apply_to(whole, d, received, 24 if first else 16, near, update)
+    apply_to(whole, d, from_other, from_pair, 24 if first else 16, near, update)
     if not last:
-        share_planes(lambda c: d_out[c], 16, piece)
+        share_planes(lambda c: d_out[c], 16, to_other, to_pair)
 
 
 def shape(*dims):
@@ -532,8 +538,13 @@
     return lax.ppermute(block, axes, route)
 
 
+def exchanged(block, axis, first):
+    n = lax.axis_size(axis)
+    pairs = [(i, i + 1) for i in range(first, n - 1, 2)]
+    return lax.ppermute(block, axis, pairs + [(j, i) for i, j in pairs])
+
+
 def shards(blocks, classes, residual):
-    nz = lax.axis_size("gz")
     w_shape, wl_shape = shape(9, ITEMS, 8, 128), shape(6, 8, 128)
     side = shape(10, 8, 128)
     w, wl, right, left, plane, plane_right, plane_left_sent = pl.pallas_call(
@@ -545,15 +556,16 @@
             pltpu.VMEM((9, 3, 3, 3, 4, 8, 128), jnp.float32),
             pltpu.VMEM((4, 8, 128), jnp.int32),
             pltpu.VMEM((3, 4, 8, 128), jnp.float32),
-            pltpu.VMEM((4, 5, 8, 128), jnp.float32),
+            pltpu.VMEM((4, 9, 8, 128), jnp.float32),
             pltpu.SemaphoreType.DMA((11,)),
         ],
         compiler_params=LIMIT,
     )(*(pltpu.with_memory_space_constraint(v, pltpu.HBM) for v in (blocks, classes, residual)))
+    plane_left = along(plane_right, ("gx", "gz"), (1, 1))
+    from_left = along(right, ("gx",), (1,))
+    plane_right = along(plane_left_sent, ("gx", "gz"), (-1, 1))
+    from_right = along(left, ("gx",), (-1,))
     plane = along(plane, ("gz",), (1,))
-    from_left, from_right = along(right, ("gx",), (1,)), along(left, ("gx",), (-1,))
-    plane_left = along(plane_right, ("gx", "gz"), (1, 1))
-    plane_right = along(plane_left_sent, ("gx", "gz"), (-1, 1))
     w, wl, up, down = pl.pallas_call(
         planes_kernel,
         in_specs=[VMEM] * 7,
@@ -561,44 +573,47 @@
         out_shape=[w_shape, wl_shape, shape(9 * packed_size(UPS) + packed_size(3), 8, 128), shape(9 * packed_size(DOWNS) + packed_size(3), 8, 128)],
         scratch_shapes=[pltpu.VMEM((3, 8, 128), jnp.float32)],
         compiler_params=LIMIT,
-    )(w, wl, from_left, from_right, plane, plane_left, plane_right)
-    from_low, from_high = along(up, ("gy",), (1,)), along(down, ("gy",), (-1,))
-    operator, whole, q, d, inverse, piece = pl.pallas_call(
+    )(plane_left, from_left, plane_right, from_right, plane, w, wl)
+    from_high = along(down, ("gy",), (-1,))
+    from_low = along(up, ("gy",), (1,))
+    whole_shape, vector = shape(9, 27, 16, 128), shape(3, 16, 128)
+    whole, q, d, inverse, to_other, to_pair = pl.pallas_call(
         rows_kernel,
         in_specs=[VMEM] * 4,
         out_specs=[VMEM] * 6,
-        out_shape=[
-            shape(3, 3, 3, 3, 3, 2, 4, 64),
-            shape(9, 27, 16, 128),
-            shape(3, 16, 128),
-            shape(3, 24, 128),
-            shape(3, 16, 128),
-            shape(nz, piece_rows(24), 128),
-        ],
+        out_shape=[whole_shape, vector, shape(3, 24, 128), vector] + [shape(piece_rows(24), 128)] * 2,
         scratch_shapes=[pltpu.VMEM((3, 16, 128), jnp.float32), pltpu.VMEM((8, 128), jnp.float32)],
         compiler_params=LIMIT,
     )(w, wl, from_low, from_high)
+    operator = pl.pallas_call(
+        operator_kernel,
+        in_specs=[VMEM],
+        out_specs=VMEM,
+        out_shape=shape(3, 3, 3, 3, 3, 2, 4, 64),
+        compiler_params=LIMIT,
+        cost_estimate=pl.CostEstimate(flops=500000, bytes_accessed=3000000, transcendentals=0),
+    )(whole)
     x = []
     rho_now = 1.0 / SIGMA
     for step in range(STEPS - 1):
         rho_next = 1.0 / (2.0 * SIGMA - rho_now)
         last = step == STEPS - 2
-        shared = lax.all_to_all(piece, "gz", 0, 0)
+        from_other, from_pair = exchanged(to_other, "gz", 1), exchanged(to_pair, "gz", 0)
         if last:
             outs = shape(3, 2, 4, 64)
         else:
-            outs = [shape(3, 16, 128), shape(3, 16, 128), shape(3, 16, 128), shape(nz, piece_rows(16), 128)]
+            outs = [vector] * 3 + [shape(piece_rows(16), 128)] * 2
         done = pl.pallas_call(
             functools.partial(step_kernel, step == 0, rho_now, rho_next, last),
-            in_specs=[VMEM] * (5 + len(x)),
-            out_specs=VMEM if last else [VMEM] * 4,
+            in_specs=[VMEM] * (6 + len(x)),
+            out_specs=VMEM if last else [VMEM] * 5,
             out_shape=outs,
             scratch_shapes=[pltpu.VMEM((3, 3, 24, 128), jnp.float32)] + ([pltpu.VMEM((16, 128), jnp.float32)] if last else []),
             compiler_params=LIMIT,
-        )(whole, q, d, inverse, shared, *x)
+        )(whole, q, d, inverse, from_other, from_pair, *x)
         if last:
             return operator, done
-        q, d, x, piece = done
+        q, d, x, to_other, to_pair = done
         x = [x]
         rho_now = rho_next
 

time: 74.4 us -> 65.3 us (0.88)
  blocking collectives: 25.7 us -> 0 us
  starting transfers between devices: 25.4 us -> 38.4 us
  waiting for transfers between devices: 10.8 us -> 15.7 us
  Pallas kernels: 11.4 us -> 9.71 us
    all_to_all x3 -> x0, blocking collectives: 25.7 us -> none  [shards(): shared = lax.all_to_all(piece, 'gz', 0, 0)]
    ppermute x0 -> x6, starting transfers between devices: none -> 14.5 us  [exchanged(): return lax.ppermute(block, axis, pairs + [(j, i) for i, j in pairs])]
    ppermute x7, waiting for transfers between devices: 10.8 us -> 13.7 us  [along(): return lax.ppermute(block, axes, route)]
    ppermute x0 -> x6, waiting for transfers between devices: none -> 1.93 us  [exchanged(): return lax.ppermute(block, axis, pairs + [(j, i) for i, j in pairs])]
    pallas_call x1, Pallas kernels: 2.42 us -> 0.67 us  [shards(): pl.pallas_call(rows_kernel, in_specs=[VMEM] * 4, out_specs=[VMEM] * 6, ou...]
    ppermute x7, starting transfers between devices: 25.4 us -> 23.9 us  [along(): return lax.ppermute(block, axes, route)]
    pallas_call x0 -> x1, Pallas kernels: none -> 1.23 us  [shards(): pl.pallas_call(operator_kernel, in_specs=[VMEM], out_specs=VMEM, out_shap...]
  transfers between devices with their start and end apart: 7 -> 13, of which waited for: 3 -> 4; matrix products, arithmetic and copies ran while one was open for 0% -> 0% of each run, Pallas kernels for 0% -> 2%
where the time goes in v2:
time: 65.3 us; the launch traced here: 64.5 us
  starting transfers between devices  38.4 us (59%)
  waiting for transfers between devices  15.7 us (24%)
  Pallas kernels  9.71 us (15%)
  between operations  0.81 us (1%)
    ppermute x7, starting transfers between devices, along(): return lax.ppermute(block, axes, route)  23.9 us
    ppermute x6, starting transfers between devices, exchanged(): return lax.ppermute(block, axis, pairs + [(j, i) for i, j in pairs])  14.5 us
    ppermute x7, waiting for transfers between devices, along(): return lax.ppermute(block, axes, route)  13.7 us
    pallas_call x1, Pallas kernels, shards(): pl.pallas_call(coarsen_kernel, in_specs=[HBM] * 3, out_specs=[VMEM] * 7,...  4.79 us
    ppermute x6, waiting for transfers between devices, exchanged(): return lax.ppermute(block, axis, pairs + [(j, i) for i, j in pairs])  1.93 us
    pallas_call x1, Pallas kernels, shards(): pl.pallas_call(planes_kernel, in_specs=[VMEM] * 7, out_specs=[VMEM] * 4,...  1.64 us
    pallas_call x3, Pallas kernels, shards(): pl.pallas_call(functools.partial(step_kernel, step == 0, rho_now, rho_nex...  1.39 us
  transfers between devices with their start and end apart: 13, of which 4 were waited for; matrix products, arithmetic and copies ran while one was open for 0% of the time, Pallas kernels for 2%

profile of v2, /device:TPU:218, one launch (start us, length us, event | category | flops | bytes accessed | tf_op | source)
XLA Modules:
  0.0 64.5 jit_solution(553849535272054412)
XLA Ops:
  0.6 4.8 %shard_map.50 = (f32[9,32,8,128]{3,2,1,0:T(8,128)S(1)}, f32[6,8,128]{2,1,0:T(8,128)S(1)}, f32[10,8,128]{2,1,0:T(8,128)S(1)}, f32[10,8,128]{2,1,0:T(8,128)S(1)}, ...) custom-call(f32[3,3,3,3,3,4,8,128]{7,6,5,4,3,2,1,0:T(8,128)} %blocks_in.1, ...), custom_call_target="tpu_custom_call" | custom-call | tf_op jit(solution)/shard_map/pallas_call | solution.py:550
  5.4 1.8 %collective-permute-start.4 = (f32[56,8,128]{2,1,0:T(8,128)S(1)}, f32[56,8,128]{2,1,0:T(8,128)S(1)}, u32[]{:S(2)}, u32[]{:S(2)}) collective-permute-start(f32[56,8,128]{2,1,0:T(8,128)S(1)} %get-tuple-element.33), channel_id=1, source_target_pairs={{0,1},{1,2},{2,3},{4,5},{5,6},{6,7},{8,9},{9,10},{10,11},{12,13},{... | collective-permute-start | bytes 688136 | tf_op jit(solution)/shard_map/ppermute | solution.py:538
  7.2 8.4 %collective-permute-start = (f32[10,8,128]{2,1,0:T(8,128)S(1)}, f32[10,8,128]{2,1,0:T(8,128)S(1)}, u32[]{:S(2)}, u32[]{:S(2)}) collective-permute-start(f32[10,8,128]{2,1,0:T(8,128)S(1)} %get-tuple-element.29), channel_id=1, source_target_pairs={{0,33},{1,34},{2,35},{32,65},{33,66},{34,67},{64,97},{65,98},{66,9... | collective-permute-start | bytes 122888 | tf_op jit(solution)/shard_map/ppermute | solution.py:538
  15.6 2.5 %collective-permute-start.1 = (f32[10,8,128]{2,1,0:T(8,128)S(1)}, f32[10,8,128]{2,1,0:T(8,128)S(1)}, u32[]{:S(2)}, u32[]{:S(2)}) collective-permute-start(f32[10,8,128]{2,1,0:T(8,128)S(1)} %get-tuple-element.30), channel_id=1, source_target_pairs={{0,32},{32,64},{64,96},{96,128},{128,160},{160,192},{192,224},{224... | collective-permute-start | bytes 122888 | tf_op jit(solution)/shard_map/ppermute | solution.py:538
  18.1 1.3 %collective-permute-start.2 = (f32[10,8,128]{2,1,0:T(8,128)S(1)}, f32[10,8,128]{2,1,0:T(8,128)S(1)}, u32[]{:S(2)}, u32[]{:S(2)}) collective-permute-start(f32[10,8,128]{2,1,0:T(8,128)S(1)} %get-tuple-element.31), channel_id=1, source_target_pairs={{32,1},{33,2},{34,3},{64,33},{65,34},{66,35},{96,65},{97,66},{98,6... | collective-permute-start | bytes 122888 | tf_op jit(solution)/shard_map/ppermute | solution.py:538
  19.4 3.3 %collective-permute-start.3 = (f32[10,8,128]{2,1,0:T(8,128)S(1)}, f32[10,8,128]{2,1,0:T(8,128)S(1)}, u32[]{:S(2)}, u32[]{:S(2)}) collective-permute-start(f32[10,8,128]{2,1,0:T(8,128)S(1)} %get-tuple-element.32), channel_id=1, source_target_pairs={{32,0},{64,32},{96,64},{128,96},{160,128},{192,160},{224,192},{256... | collective-permute-start | bytes 122888 | tf_op jit(solution)/shard_map/ppermute | solution.py:538
  22.7 4.6 %collective-permute-done.3.from_right = f32[10,8,128]{2,1,0:T(8,128)S(1)} collective-permute-done((f32[10,8,128]{2,1,0:T(8,128)S(1)}, f32[10,8,128]{2,1,0:T(8,128)S(1)}, u32[]{:S(2)}, u32[]{:S(2)}) %collective-permute-start.3) | collective-permute-done | bytes 40992 | tf_op jit(solution)/shard_map/ppermute | solution.py:538
  27.4 1.6 %shard_map.51 = (f32[9,32,8,128]{3,2,1,0:T(8,128)S(1)}, f32[6,8,128]{2,1,0:T(8,128)S(1)}, f32[93,8,128]{2,1,0:T(8,128)S(1)}, f32[75,8,128]{2,1,0:T(8,128)S(1)}) custom-call(f32[10,8,128]{2,1,0:T(8,128)S(1)} %collective-permute-done.plane_left, f32[10,8,128]{2,1,0:T(8,128)S(1)} %collective-permute-done.1.from_left, ...), custom_call_target="tpu_custom_call" | custom-call | tf_op jit(solution)/shard_map/pallas_call | solution.py:569
  29.0 4.7 %collective-permute-start.5 = (f32[93,8,128]{2,1,0:T(8,128)S(1)}, f32[93,8,128]{2,1,0:T(8,128)S(1)}, u32[]{:S(2)}, u32[]{:S(2)}) collective-permute-start(f32[93,8,128]{2,1,0:T(8,128)S(1)} %get-tuple-element.38), channel_id=1, source_target_pairs={{0,4},{4,8},{8,12},{12,16},{16,20},{20,24},{24,28},{1,5},{5,9},{9,... | collective-permute-start | bytes 1142792 | tf_op jit(solution)/shard_map/ppermute | solution.py:538
  33.7 1.9 %collective-permute-start.6 = (f32[75,8,128]{2,1,0:T(8,128)S(1)}, f32[75,8,128]{2,1,0:T(8,128)S(1)}, u32[]{:S(2)}, u32[]{:S(2)}) collective-permute-start(f32[75,8,128]{2,1,0:T(8,128)S(1)} %get-tuple-element.39), channel_id=1, source_target_pairs={{4,0},{8,4},{12,8},{16,12},{20,16},{24,20},{28,24},{5,1},{9,5},{13... | collective-permute-start | bytes 921608 | tf_op jit(solution)/shard_map/ppermute | solution.py:538
  35.7 9.1 %collective-permute-done.6.from_high = f32[75,8,128]{2,1,0:T(8,128)S(1)} collective-permute-done((f32[75,8,128]{2,1,0:T(8,128)S(1)}, f32[75,8,128]{2,1,0:T(8,128)S(1)}, u32[]{:S(2)}, u32[]{:S(2)}) %collective-permute-start.6) | collective-permute-done | bytes 307232 | tf_op jit(solution)/shard_map/ppermute | solution.py:538
  44.7 0.7 %shard_map.52 = (f32[9,27,16,128]{3,2,1,0:T(8,128)S(1)}, f32[3,16,128]{2,1,0:T(8,128)S(1)}, f32[3,24,128]{2,1,0:T(8,128)S(1)}, f32[3,16,128]{2,1,0:T(8,128)S(1)}...) custom-call(f32[9,32,8,128]{3,2,1,0:T(8,128)S(1)} %get-tuple-element.36.w, f32[6,8,128]{2,1,0:T(8,128)S(1)} %get-tuple-element.37.wl, ...), custom_call_target="tpu_custom_call" | custom-call | tf_op jit(solution)/shard_map/pallas_call | solution.py:580
  45.4 0.7 %collective-permute-start.7 = (f32[40,128]{1,0:T(8,128)S(1)}, f32[40,128]{1,0:T(8,128)S(1)}, u32[]{:S(2)}, u32[]{:S(2)}) collective-permute-start(f32[40,128]{1,0:T(8,128)S(1)} %get-tuple-element.44), channel_id=1, source_target_pairs={{1,2},{2,1},{5,6},{6,5},{9,10},{10,9},{13,14},{14,13},{17,18},{18,... | collective-permute-start | bytes 61448 | tf_op jit(solution)/shard_map/ppermute | solution.py:544
  46.1 1.9 %collective-permute-start.8 = (f32[40,128]{1,0:T(8,128)S(1)}, f32[40,128]{1,0:T(8,128)S(1)}, u32[]{:S(2)}, u32[]{:S(2)}) collective-permute-start(f32[40,128]{1,0:T(8,128)S(1)} %get-tuple-element.45), channel_id=1, source_target_pairs={{0,1},{2,3},{1,0},{3,2},{4,5},{6,7},{5,4},{7,6},{8,9},{10,11},{9,8... | collective-permute-start | bytes 61448 | tf_op jit(solution)/shard_map/ppermute | solution.py:544
  48.1 1.1 %collective-permute-done.8.refs_5_ = f32[40,128]{1,0:T(8,128)S(1)} collective-permute-done((f32[40,128]{1,0:T(8,128)S(1)}, f32[40,128]{1,0:T(8,128)S(1)}, u32[]{:S(2)}, u32[]{:S(2)}) %collective-permute-start.8) | collective-permute-done | bytes 20512 | tf_op jit(solution)/shard_map/ppermute | solution.py:544
  49.2 0.2 shard_map.54
  49.4 0.7 %collective-permute-start.9 = (f32[24,128]{1,0:T(8,128)S(1)}, f32[24,128]{1,0:T(8,128)S(1)}, u32[]{:S(2)}, u32[]{:S(2)}) collective-permute-start(f32[24,128]{1,0:T(8,128)S(1)} %get-tuple-element.48), channel_id=1, source_target_pairs={{1,2},{2,1},{5,6},{6,5},{9,10},{10,9},{13,14},{14,13},{17,18},{18,... | collective-permute-start | bytes 36872 | tf_op jit(solution)/shard_map/ppermute | solution.py:544
  50.1 5.5 %collective-permute-start.10 = (f32[24,128]{1,0:T(8,128)S(1)}, f32[24,128]{1,0:T(8,128)S(1)}, u32[]{:S(2)}, u32[]{:S(2)}) collective-permute-start(f32[24,128]{1,0:T(8,128)S(1)} %get-tuple-element.49), channel_id=1, source_target_pairs={{0,1},{2,3},{1,0},{3,2},{4,5},{6,7},{5,4},{7,6},{8,9},{10,11},{9,8... | collective-permute-start | bytes 36872 | tf_op jit(solution)/shard_map/ppermute | solution.py:544
  55.6 0.8 %collective-permute-done.10.refs_5_ = f32[24,128]{1,0:T(8,128)S(1)} collective-permute-done((f32[24,128]{1,0:T(8,128)S(1)}, f32[24,128]{1,0:T(8,128)S(1)}, u32[]{:S(2)}, u32[]{:S(2)}) %collective-permute-start.10) | collective-permute-done | bytes 12320 | tf_op jit(solution)/shard_map/ppermute | solution.py:544
  56.4 0.3 shard_map.55
  56.6 0.7 %collective-permute-start.11 = (f32[24,128]{1,0:T(8,128)S(1)}, f32[24,128]{1,0:T(8,128)S(1)}, u32[]{:S(2)}, u32[]{:S(2)}) collective-permute-start(f32[24,128]{1,0:T(8,128)S(1)} %get-tuple-element.53), channel_id=1, source_target_pairs={{1,2},{2,1},{5,6},{6,5},{9,10},{10,9},{13,14},{14,13},{17,18},{18,... | collective-permute-start | bytes 36872 | tf_op jit(solution)/shard_map/ppermute | solution.py:544
  57.3 5.1 %collective-permute-start.12 = (f32[24,128]{1,0:T(8,128)S(1)}, f32[24,128]{1,0:T(8,128)S(1)}, u32[]{:S(2)}, u32[]{:S(2)}) collective-permute-start(f32[24,128]{1,0:T(8,128)S(1)} %get-tuple-element.54), channel_id=1, source_target_pairs={{0,1},{2,3},{1,0},{3,2},{4,5},{6,7},{5,4},{7,6},{8,9},{10,11},{9,8... | collective-permute-start | bytes 36872 | tf_op jit(solution)/shard_map/ppermute | solution.py:544
  62.4 1.2 %shard_map.53 = f32[3,3,3,3,3,2,4,64]{7,6,5,4,3,2,1,0:T(4,128)} custom-call(f32[9,27,16,128]{3,2,1,0:T(8,128)S(1)} %get-tuple-element.40.whole.refs_0_), custom_call_target="tpu_custom_call" | custom-call | flops 500000 | bytes 3000000 | tf_op jit(solution)/shard_map/pallas_call | solution.py:588
  63.7 0.9 %shard_map.56 = f32[3,2,4,64]{3,2,1,0:T(4,128)} custom-call(f32[9,27,16,128]{3,2,1,0:T(8,128)S(1)} %get-tuple-element.40.whole.refs_0_, f32[3,16,128]{2,1,0:T(8,128)S(1)} %get-tuple-element.51.refs_1_, f32[3,16,128]{2,1,0:T(8,128)S(1)} %get-tuple-element.52.refs_2_, f32[3,16,128]{2,1,0:T(8,128)S(1)} %get-tuple-element.43.refs_3_, ...), custom_call_target="tpu_custom_call" | custom-call | tf_op jit(solution)/shard_map/pallas_call | solution.py:606
  (9 shorter events, 0.0 us)
Async XLA Ops:
  5.4 21.9 %collective-permute-start.4 = (f32[56,8,128]{2,1,0:T(8,128)S(1)}, f32[56,8,128]{2,1,0:T(8,128)S(1)}, u32[]{:S(2)}, u32[]{:S(2)}) collective-permute-start(f32[56,8,128]{2,1,0:T(8,128)S(1)} %get-tuple-element.33), channel_id=1, source_target_pairs={{0,1},{1,2},{2,3},{4,5},{5,6},{6,7},{8,9},{9,10},{10,11},{12,13},{... | collective-permute-start | bytes 688136 | tf_op jit(solution)/shard_map/ppermute | solution.py:538
  7.2 15.5 %collective-permute-start = (f32[10,8,128]{2,1,0:T(8,128)S(1)}, f32[10,8,128]{2,1,0:T(8,128)S(1)}, u32[]{:S(2)}, u32[]{:S(2)}) collective-permute-start(f32[10,8,128]{2,1,0:T(8,128)S(1)} %get-tuple-element.29), channel_id=1, source_target_pairs={{0,33},{1,34},{2,35},{32,65},{33,66},{34,67},{64,97},{65,98},{66,9... | collective-permute-start | bytes 122888 | tf_op jit(solution)/shard_map/ppermute | solution.py:538
  15.6 7.2 %collective-permute-start.1 = (f32[10,8,128]{2,1,0:T(8,128)S(1)}, f32[10,8,128]{2,1,0:T(8,128)S(1)}, u32[]{:S(2)}, u32[]{:S(2)}) collective-permute-start(f32[10,8,128]{2,1,0:T(8,128)S(1)} %get-tuple-element.30), channel_id=1, source_target_pairs={{0,32},{32,64},{64,96},{96,128},{128,160},{160,192},{192,224},{224... | collective-permute-start | bytes 122888 | tf_op jit(solution)/shard_map/ppermute | solution.py:538
  18.1 4.7 %collective-permute-start.2 = (f32[10,8,128]{2,1,0:T(8,128)S(1)}, f32[10,8,128]{2,1,0:T(8,128)S(1)}, u32[]{:S(2)}, u32[]{:S(2)}) collective-permute-start(f32[10,8,128]{2,1,0:T(8,128)S(1)} %get-tuple-element.31), channel_id=1, source_target_pairs={{32,1},{33,2},{34,3},{64,33},{65,34},{66,35},{96,65},{97,66},{98,6... | collective-permute-start | bytes 122888 | tf_op jit(solution)/shard_map/ppermute | solution.py:538
  19.4 8.0 %collective-permute-start.3 = (f32[10,8,128]{2,1,0:T(8,128)S(1)}, f32[10,8,128]{2,1,0:T(8,128)S(1)}, u32[]{:S(2)}, u32[]{:S(2)}) collective-permute-start(f32[10,8,128]{2,1,0:T(8,128)S(1)} %get-tuple-element.32), channel_id=1, source_target_pairs={{32,0},{64,32},{96,64},{128,96},{160,128},{192,160},{224,192},{256... | collective-permute-start | bytes 122888 | tf_op jit(solution)/shard_map/ppermute | solution.py:538
  29.0 15.7 %collective-permute-start.5 = (f32[93,8,128]{2,1,0:T(8,128)S(1)}, f32[93,8,128]{2,1,0:T(8,128)S(1)}, u32[]{:S(2)}, u32[]{:S(2)}) collective-permute-start(f32[93,8,128]{2,1,0:T(8,128)S(1)} %get-tuple-element.38), channel_id=1, source_target_pairs={{0,4},{4,8},{8,12},{12,16},{16,20},{20,24},{24,28},{1,5},{5,9},{9,... | collective-permute-start | bytes 1142792 | tf_op jit(solution)/shard_map/ppermute | solution.py:538
  33.7 11.0 %collective-permute-start.6 = (f32[75,8,128]{2,1,0:T(8,128)S(1)}, f32[75,8,128]{2,1,0:T(8,128)S(1)}, u32[]{:S(2)}, u32[]{:S(2)}) collective-permute-start(f32[75,8,128]{2,1,0:T(8,128)S(1)} %get-tuple-element.39), channel_id=1, source_target_pairs={{4,0},{8,4},{12,8},{16,12},{20,16},{24,20},{28,24},{5,1},{9,5},{13... | collective-permute-start | bytes 921608 | tf_op jit(solution)/shard_map/ppermute | solution.py:538
  45.4 2.6 %collective-permute-start.7 = (f32[40,128]{1,0:T(8,128)S(1)}, f32[40,128]{1,0:T(8,128)S(1)}, u32[]{:S(2)}, u32[]{:S(2)}) collective-permute-start(f32[40,128]{1,0:T(8,128)S(1)} %get-tuple-element.44), channel_id=1, source_target_pairs={{1,2},{2,1},{5,6},{6,5},{9,10},{10,9},{13,14},{14,13},{17,18},{18,... | collective-permute-start | bytes 61448 | tf_op jit(solution)/shard_map/ppermute | solution.py:544
  46.1 3.1 %collective-permute-start.8 = (f32[40,128]{1,0:T(8,128)S(1)}, f32[40,128]{1,0:T(8,128)S(1)}, u32[]{:S(2)}, u32[]{:S(2)}) collective-permute-start(f32[40,128]{1,0:T(8,128)S(1)} %get-tuple-element.45), channel_id=1, source_target_pairs={{0,1},{2,3},{1,0},{3,2},{4,5},{6,7},{5,4},{7,6},{8,9},{10,11},{9,8... | collective-permute-start | bytes 61448 | tf_op jit(solution)/shard_map/ppermute | solution.py:544
  49.4 6.1 %collective-permute-start.9 = (f32[24,128]{1,0:T(8,128)S(1)}, f32[24,128]{1,0:T(8,128)S(1)}, u32[]{:S(2)}, u32[]{:S(2)}) collective-permute-start(f32[24,128]{1,0:T(8,128)S(1)} %get-tuple-element.48), channel_id=1, source_target_pairs={{1,2},{2,1},{5,6},{6,5},{9,10},{10,9},{13,14},{14,13},{17,18},{18,... | collective-permute-start | bytes 36872 | tf_op jit(solution)/shard_map/ppermute | solution.py:544
  50.1 6.3 %collective-permute-start.10 = (f32[24,128]{1,0:T(8,128)S(1)}, f32[24,128]{1,0:T(8,128)S(1)}, u32[]{:S(2)}, u32[]{:S(2)}) collective-permute-start(f32[24,128]{1,0:T(8,128)S(1)} %get-tuple-element.49), channel_id=1, source_target_pairs={{0,1},{2,3},{1,0},{3,2},{4,5},{6,7},{5,4},{7,6},{8,9},{10,11},{9,8... | collective-permute-start | bytes 36872 | tf_op jit(solution)/shard_map/ppermute | solution.py:544
  56.6 7.0 %collective-permute-start.11 = (f32[24,128]{1,0:T(8,128)S(1)}, f32[24,128]{1,0:T(8,128)S(1)}, u32[]{:S(2)}, u32[]{:S(2)}) collective-permute-start(f32[24,128]{1,0:T(8,128)S(1)} %get-tuple-element.53), channel_id=1, source_target_pairs={{1,2},{2,1},{5,6},{6,5},{9,10},{10,9},{13,14},{14,13},{17,18},{18,... | collective-permute-start | bytes 36872 | tf_op jit(solution)/shard_map/ppermute | solution.py:544
  57.3 6.3 %collective-permute-start.12 = (f32[24,128]{1,0:T(8,128)S(1)}, f32[24,128]{1,0:T(8,128)S(1)}, u32[]{:S(2)}, u32[]{:S(2)}) collective-permute-start(f32[24,128]{1,0:T(8,128)S(1)} %get-tuple-element.54), channel_id=1, source_target_pairs={{0,1},{2,3},{1,0},{3,2},{4,5},{6,7},{5,4},{7,6},{8,9},{10,11},{9,8... | collective-permute-start | bytes 36872 | tf_op jit(solution)/shard_map/ppermute | solution.py:544

commit v3 on v2

--- a/solution.py
+++ b/solution.py
@@ -19,6 +19,7 @@
 PLANE = 11
 UPS, DOWNS = 18, 14
 AHEAD = 3
+EDGES = 8 * 48
 VMEM = pl.BlockSpec(memory_space=pltpu.VMEM)
 HBM = pl.BlockSpec(memory_space=pltpu.HBM)
 LIMIT = pltpu.CompilerParams(vmem_limit_bytes=40 * 1024 * 1024)
@@ -356,42 +357,58 @@
     return n + 8 * ((n + 15) // 16)
 
 
-def share_planes(load, n, to_other, to_pair):
+def split_planes(one, two):
+    n = one.shape[0]
+    even = lax.broadcasted_iota(jnp.int32, one.shape, 0) % 2 == 0
+    first = jnp.where(even, one, pltpu.roll(two, 1, 0))
+    second = jnp.where(even, pltpu.roll(one, n - 1, 0), two)
+    return first, second
+
+
+def join_planes(below, above):
+    n = below.shape[0]
+    even = lax.broadcasted_iota(jnp.int32, below.shape, 0) % 2 == 0
+    one = jnp.where(even, below, pltpu.roll(above, 1, 0))
+    two = jnp.where(even, pltpu.roll(below, n - 1, 0), above)
+    return one, two
+
+
+def share(at, planes, to_other, to_pair):
     low_of_pair = lax.axis_index("gz") % 2 == 0
-    even = lax.broadcasted_iota(jnp.int32, (n, 128), 0) % 2 == 0
-    d = [load(c) for c in range(3)]
-    sent = []
-    for z in range(2):
-        if z == 0:
-            both = jnp.where(even, d[0], pltpu.roll(d[1], 1, 0))
-            third = d[2]
-        else:
-            both = jnp.where(even, pltpu.roll(d[0], n - 1, 0), d[1])
-            third = pltpu.roll(d[2], n - 1, 0)
-        folds = []
-        for at in range(0, n, 16):
-            fold = third[at : at + 8]
-            if at + 8 < n:
-                fold = jnp.where(even[0:8], fold, sroll(third[at + 8 : at + 16], 1))
-            folds.append(fold)
-        sent.append(jnp.concatenate([both] + folds, axis=0))
-    to_pair[...] = jnp.where(low_of_pair, sent[1], sent[0])
-    to_other[...] = jnp.where(low_of_pair, sent[0], sent[1])
-
-
-def plane_of(piece, n, c):
-    if c < 2:
-        return piece[0:n], c
+    first, second = planes
+    n = first.shape[0]
+    to_pair[at : at + n] = jnp.where(low_of_pair, second, first)
+    to_other[at : at + n] = jnp.where(low_of_pair, first, second)
+
+
+def shared(at, n, from_other, from_pair):
+    low_of_pair = lax.axis_index("gz") % 2 == 0
+    other, pair = from_other[at : at + n], from_pair[at : at + n]
+    return jnp.where(low_of_pair, other, pair), jnp.where(low_of_pair, pair, other)
+
+
+def share_vector(load, n, at, to_other, to_pair):
+    share(at, split_planes(load(0), load(1)), to_other, to_pair)
+    third = load(2)
+    at += n
+    for i in range(0, n, 16):
+        one = third[i : i + 8]
+        two = third[i + 8 : i + 16] if i + 8 < n else jnp.zeros_like(one)
+        share(at, split_planes(one, two), to_other, to_pair)
+        at += 8
+
+
+def shared_vector(n, at, from_other, from_pair):
+    one, two = join_planes(*shared(at, n, from_other, from_pair))
+    at += n
     parts = []
     for i in range(0, n, 16):
-        fold = piece[n + i // 2 : n + i // 2 + 8]
-        parts.append(fold)
-        if i + 8 < n:
-            parts.append(sroll(fold, -1))
-    return jnp.concatenate(parts, axis=0), 0
-
-
-def rows_kernel(w, wl, from_low, from_high, whole, q, d, inverse, to_other, to_pair, total, turned):
+        parts += join_planes(*shared(at, 8, from_other, from_pair))
+        at += 8
+    return one, two, jnp.concatenate(parts[: n // 8], axis=0)
+
+
+def rows_kernel(w, wl, from_low, from_high, whole, q, d, inverse, to_other, to_pair, total, turned, near):
     row = rows_of()
     ghosts = jnp.logical_or(row == 4, row == 5)
     total[...] = jnp.zeros_like(total)
@@ -442,7 +459,15 @@
         d[c, 0:2] = turned[6:8]
         turned[...] = downs[c]
         d[c, 18:20] = turned[6:8]
-    share_planes(lambda c: d[c], 24, to_other, to_pair)
+    for c in range(3):
+        fill_near(near, c, d[c], None)
+    for r, product in enumerate(apply_to(whole, near)):
+        q[r] = q[r] - product
+    items = [edge_of(whole, i // 9, i % 9) for i in range(81)] + [q[r] for r in range(3)] + [inverse[r] for r in range(3)]
+    packed = pack([v[h : h + 8] for v in items for h in (0, 8)])
+    for i in range(0, len(packed), 2):
+        share(4 * i, split_planes(packed[i], packed[i + 1]), to_other, to_pair)
+    share_vector(lambda c: d[c], 24, EDGES, to_other, to_pair)
 
 
 def operator_kernel(whole, operator):
@@ -456,71 +481,88 @@
     lax.fori_loop(0, 9, body, 0, unroll=3)
 
 
-def apply_to(whole, d, from_other, from_pair, n, near, out):
-    low_of_pair = lax.axis_index("gz") % 2 == 0
+def edge_of(whole, rc, at):
+    even = lax.broadcasted_iota(jnp.int32, (16, 128), 0) % 2 == 0
+    return jnp.where(even, whole[rc, at], whole[rc, 18 + at])
+
+
+def fill_near(near, c, own, beyond):
+    n = own.shape[0]
     even = lax.broadcasted_iota(jnp.int32, (n, 128), 0) % 2 == 0
-    other, pair = from_other[...], from_pair[...]
-    below = jnp.where(low_of_pair, other, pair)
-    above = jnp.where(low_of_pair, pair, other)
     base = (24 - n) // 4
-    for c in range(3):
-        own = d[c]
-        low, odd = plane_of(below, n, c)
-        high, _ = plane_of(above, n, c)
-        if odd:
-            low = pltpu.roll(low, n - 1, 0)
-        else:
-            high = pltpu.roll(high, 1, 0)
-        for cz, v in enumerate((
-            jnp.where(even, low, pltpu.roll(own, 1, 0)),
-            own,
-            jnp.where(even, pltpu.roll(own, n - 1, 0), high),
-        )):
-            if base:
-                near[cz, c, 0:8] = jnp.zeros((8, 128), jnp.float32)
-                near[cz, c, 16:24] = jnp.zeros((8, 128), jnp.float32)
-            near[cz, c, base : base + n] = v
+    if beyond is None:
+        beyond = jnp.zeros_like(own)
+    for cz, v in enumerate((
+        jnp.where(even, beyond, pltpu.roll(own, 1, 0)),
+        own,
+        jnp.where(even, pltpu.roll(own, n - 1, 0), beyond),
+    )):
+        if base:
+            near[cz, c, 0:8] = jnp.zeros((8, 128), jnp.float32)
+            near[cz, c, 16:24] = jnp.zeros((8, 128), jnp.float32)
+        near[cz, c, base : base + n] = v
+
+
+def shifted(v):
+    return pltpu.roll(v, 1, 1), v, pltpu.roll(v, 127, 1)
+
+
+def apply_to(whole, near):
     sums = [jnp.zeros((16, 128), jnp.float32) for _ in range(3)]
     for cz in range(3):
         for cy in range(3):
             for c in range(3):
-                v = near[cz, c, pl.ds(2 * cy, 16), :]
-                for cx, moved in enumerate((pltpu.roll(v, 1, 1), v, pltpu.roll(v, 127, 1))):
+                for cx, moved in enumerate(shifted(near[cz, c, pl.ds(2 * cy, 16), :])):
                     for r in range(3):
                         sums[r] = sums[r] + whole[r * 3 + c, cz * 9 + cy * 3 + cx] * moved
+    return sums
+
+
+def two_steps_kernel(rhos, whole, q, d, inverse, from_other, from_pair, q_out, d_out, x_out, to_other, to_pair, near, packed, edges):
+    even = rows_of() % 2 == 0
+    for i in range(0, packed.shape[0], 2):
+        packed[i], packed[i + 1] = join_planes(*shared(4 * i, 8, from_other, from_pair))
+    for i, v in enumerate(unpack(lambda i: packed[i], 174)):
+        edges[i // 2, 8 * (i % 2) : 8 * (i % 2) + 8] = v
+    for c, v in enumerate(shared_vector(24, EDGES, from_other, from_pair)):
+        near[0, c] = v
+        near[1, c] = d[c]
+    own = [jnp.zeros((16, 128), jnp.float32) for _ in range(3)]
+    beyond = [jnp.zeros((16, 128), jnp.float32) for _ in range(3)]
+    for cy in range(3):
+        for c in range(3):
+            outer = shifted(near[0, c, pl.ds(2 * cy, 16), :])
+            inner = shifted(near[1, c, pl.ds(2 * cy, 16), :])
+            for cx in range(3):
+                for r in range(3):
+                    rc, at = r * 3 + c, cy * 3 + cx
+                    own[r] = own[r] + edge_of(whole, rc, at) * outer[cx]
+                    beyond[r] = beyond[r] + edges[rc * 9 + at] * inner[cx]
+    (same, slope), (same_next, slope_next) = rhos
+    q_now, d_now, d_beyond = [], [], []
     for r in range(3):
-        out(r, sums[r])
-
-
-def step_kernel(first, rho_now, rho_next, last, *refs):
-    whole, q, d, inverse, from_other, from_pair = refs[:6]
-    refs = refs[6:]
-    if first:
-        x = None
-    else:
-        x, refs = refs[0], refs[1:]
-    if last:
-        solution_out, near, turned = refs
-    else:
-        q_out, d_out, x_out, to_other, to_pair, near = refs
-
-    def update(r, product):
-        now = d[r, 2:18] if first else d[r]
-        x_now = now if x is None else x[r] + now
-        q_now = q[r] - product
-        d_new = rho_next * rho_now * now + 2.0 * rho_next / HALF * (inverse[r] * q_now)
-        if last:
-            turned[...] = x_now + d_new
-            for z in range(2):
-                solution_out[r, z] = turned[pl.ds(4 + z, 4, stride=2), :][:, 0:64]
-        else:
-            x_out[r] = x_now
-            q_out[r] = q_now
-            d_out[r] = d_new
-
-    apply_to(whole, d, from_other, from_pair, 24 if first else 16, near, update)
-    if not last:
-        share_planes(lambda c: d_out[c], 16, to_other, to_pair)
+        q_now.append(q[r] - own[r])
+        d_now.append(same * d[r, 2:18] + slope * (inverse[r] * q_now[r]))
+        d_beyond.append(same * near[0, r, 2:18] + slope * (edges[84 + r] * (edges[81 + r] - beyond[r])))
+        x_out[r] = d[r, 2:18] + d_now[r]
+    for r in range(3):
+        fill_near(near, r, d_now[r], d_beyond[r])
+    for r, product in enumerate(apply_to(whole, near)):
+        q_next = q_now[r] - product
+        q_out[r] = q_next
+        d_out[r] = same_next * d_now[r] + slope_next * (inverse[r] * q_next)
+    share_vector(lambda c: d_out[c], 16, 0, to_other, to_pair)
+
+
+def last_step_kernel(rho, whole, q, d, inverse, x, from_other, from_pair, solution_out, near, turned):
+    same, slope = rho
+    for c, v in enumerate(shared_vector(16, 0, from_other, from_pair)):
+        fill_near(near, c, d[c], v)
+    for r, product in enumerate(apply_to(whole, near)):
+        d_new = same * d[r] + slope * (inverse[r] * (q[r] - product))
+        turned[...] = x[r] + d[r] + d_new
+        for z in range(2):
+            solution_out[r, z] = turned[pl.ds(4 + z, 4, stride=2), :][:, 0:64]
 
 
 def shape(*dims):
@@ -577,12 +619,13 @@
     from_high = along(down, ("gy",), (-1,))
     from_low = along(up, ("gy",), (1,))
     whole_shape, vector = shape(9, 27, 16, 128), shape(3, 16, 128)
+    near = pltpu.VMEM((3, 3, 24, 128), jnp.float32)
     whole, q, d, inverse, to_other, to_pair = pl.pallas_call(
         rows_kernel,
         in_specs=[VMEM] * 4,
         out_specs=[VMEM] * 6,
-        out_shape=[whole_shape, vector, shape(3, 24, 128), vector] + [shape(piece_rows(24), 128)] * 2,
-        scratch_shapes=[pltpu.VMEM((3, 16, 128), jnp.float32), pltpu.VMEM((8, 128), jnp.float32)],
+        out_shape=[whole_shape, vector, shape(3, 24, 128), vector] + [shape(EDGES + piece_rows(24), 128)] * 2,
+        scratch_shapes=[pltpu.VMEM((3, 16, 128), jnp.float32), pltpu.VMEM((8, 128), jnp.float32), near],
         compiler_params=LIMIT,
     )(w, wl, from_low, from_high)
     operator = pl.pallas_call(
@@ -593,29 +636,30 @@
         compiler_params=LIMIT,
         cost_estimate=pl.CostEstimate(flops=500000, bytes_accessed=3000000, transcendentals=0),
     )(whole)
-    x = []
-    rho_now = 1.0 / SIGMA
-    for step in range(STEPS - 1):
+    rhos, rho_now = [], 1.0 / SIGMA
+    for _ in range(STEPS - 1):
         rho_next = 1.0 / (2.0 * SIGMA - rho_now)
-        last = step == STEPS - 2
-        from_other, from_pair = exchanged(to_other, "gz", 1), exchanged(to_pair, "gz", 0)
-        if last:
-            outs = shape(3, 2, 4, 64)
-        else:
-            outs = [vector] * 3 + [shape(piece_rows(16), 128)] * 2
-        done = pl.pallas_call(
-            functools.partial(step_kernel, step == 0, rho_now, rho_next, last),
-            in_specs=[VMEM] * (6 + len(x)),
-            out_specs=VMEM if last else [VMEM] * 5,
-            out_shape=outs,
-            scratch_shapes=[pltpu.VMEM((3, 3, 24, 128), jnp.float32)] + ([pltpu.VMEM((16, 128), jnp.float32)] if last else []),
-            compiler_params=LIMIT,
-        )(whole, q, d, inverse, from_other, from_pair, *x)
-        if last:
-            return operator, done
-        q, d, x, to_other, to_pair = done
-        x = [x]
+        rhos.append((rho_next * rho_now, 2.0 * rho_next / HALF))
         rho_now = rho_next
+    from_other, from_pair = exchanged(to_other, "gz", 1), exchanged(to_pair, "gz", 0)
+    q, d, x, to_other, to_pair = pl.pallas_call(
+        functools.partial(two_steps_kernel, rhos[:2]),
+        in_specs=[VMEM] * 6,
+        out_specs=[VMEM] * 5,
+        out_shape=[vector] * 3 + [shape(piece_rows(16), 128)] * 2,
+        scratch_shapes=[near, pltpu.VMEM((96, 8, 128), jnp.float32), pltpu.VMEM((87, 16, 128), jnp.float32)],
+        compiler_params=LIMIT,
+    )(whole, q, d, inverse, from_other, from_pair)
+    from_other, from_pair = exchanged(to_other, "gz", 1), exchanged(to_pair, "gz", 0)
+    coarse_solution = pl.pallas_call(
+        functools.partial(last_step_kernel, rhos[2]),
+        in_specs=[VMEM] * 7,
+        out_specs=VMEM,
+        out_shape=shape(3, 2, 4, 64),
+        scratch_shapes=[near, pltpu.VMEM((16, 128), jnp.float32)],
+        compiler_params=LIMIT,
+    )(whole, q, d, inverse, x, from_other, from_pair)
+    return operator, coarse_solution
 
 
 def solution(mesh):

time: 65.3 us -> 61.4 us (0.940)
  starting transfers between devices: 38.4 us -> 33.8 us
  Pallas kernels: 9.71 us -> 10.5 us
    ppermute x6 -> x4, starting transfers between devices: 14.5 us -> 9.89 us  [exchanged(): return lax.ppermute(block, axis, pairs + [(j, i) for i, j in pairs])]
    ppermute x6 -> x4, waiting for transfers between devices: 1.93 us -> 1.42 us  [exchanged(): return lax.ppermute(block, axis, pairs + [(j, i) for i, j in pairs])]
    pallas_call x3 -> x2, Pallas kernels: 1.39 us -> 1.64 us  [the longest x1 0.87 us: shards(): pl.pallas_call(functools.partial(last_step_kernel, rhos[2]), in_specs=[VM...]
  transfers between devices with their start and end apart: 13 -> 11, of which waited for: 4 -> 3; matrix products, arithmetic and copies ran while one was open for 0% -> 0% of each run, Pallas kernels for 2% -> 2%
where the time goes in v3:
time: 61.4 us; the launch traced here: 60.2 us
  starting transfers between devices  33.8 us (55%)
  waiting for transfers between devices  15.1 us (25%)
  Pallas kernels  10.5 us (17%)
  between operations  0.78 us (1%)
    ppermute x7, starting transfers between devices, along(): return lax.ppermute(block, axes, route)  23.9 us
    ppermute x7, waiting for transfers between devices, along(): return lax.ppermute(block, axes, route)  13.7 us
    ppermute x4, starting transfers between devices, exchanged(): return lax.ppermute(block, axis, pairs + [(j, i) for i, j in pairs])  9.89 us
    pallas_call x1, Pallas kernels, shards(): pl.pallas_call(coarsen_kernel, in_specs=[HBM] * 3, out_specs=[VMEM] * 7,...  4.79 us
    pallas_call x1, Pallas kernels, shards(): pl.pallas_call(planes_kernel, in_specs=[VMEM] * 7, out_specs=[VMEM] * 4,...  1.64 us
    ppermute x4, waiting for transfers between devices, exchanged(): return lax.ppermute(block, axis, pairs + [(j, i) for i, j in pairs])  1.42 us
  transfers between devices with their start and end apart: 11, of which 3 were waited for; matrix products, arithmetic and copies ran while one was open for 0% of the time, Pallas kernels for 2%

profile of v3, /device:TPU:218, one launch (start us, length us, event | category | flops | bytes accessed | tf_op | source)
XLA Modules:
  0.0 60.2 jit_solution(9058906856509788220)
XLA Ops:
  0.6 4.8 %shard_map.50 = (f32[9,32,8,128]{3,2,1,0:T(8,128)S(1)}, f32[6,8,128]{2,1,0:T(8,128)S(1)}, f32[10,8,128]{2,1,0:T(8,128)S(1)}, f32[10,8,128]{2,1,0:T(8,128)S(1)}, ...) custom-call(f32[3,3,3,3,3,4,8,128]{7,6,5,4,3,2,1,0:T(8,128)} %blocks_in.1, ...), custom_call_target="tpu_custom_call" | custom-call | tf_op jit(solution)/shard_map/pallas_call | solution.py:592
  5.4 1.8 %collective-permute-start.4 = (f32[56,8,128]{2,1,0:T(8,128)S(1)}, f32[56,8,128]{2,1,0:T(8,128)S(1)}, u32[]{:S(2)}, u32[]{:S(2)}) collective-permute-start(f32[56,8,128]{2,1,0:T(8,128)S(1)} %get-tuple-element.28), channel_id=1, source_target_pairs={{0,1},{1,2},{2,3},{4,5},{5,6},{6,7},{8,9},{9,10},{10,11},{12,13},{... | collective-permute-start | bytes 688136 | tf_op jit(solution)/shard_map/ppermute | solution.py:580
  7.2 8.4 %collective-permute-start = (f32[10,8,128]{2,1,0:T(8,128)S(1)}, f32[10,8,128]{2,1,0:T(8,128)S(1)}, u32[]{:S(2)}, u32[]{:S(2)}) collective-permute-start(f32[10,8,128]{2,1,0:T(8,128)S(1)} %get-tuple-element.24), channel_id=1, source_target_pairs={{0,33},{1,34},{2,35},{32,65},{33,66},{34,67},{64,97},{65,98},{66,9... | collective-permute-start | bytes 122888 | tf_op jit(solution)/shard_map/ppermute | solution.py:580
  15.6 2.5 %collective-permute-start.1 = (f32[10,8,128]{2,1,0:T(8,128)S(1)}, f32[10,8,128]{2,1,0:T(8,128)S(1)}, u32[]{:S(2)}, u32[]{:S(2)}) collective-permute-start(f32[10,8,128]{2,1,0:T(8,128)S(1)} %get-tuple-element.25), channel_id=1, source_target_pairs={{0,32},{32,64},{64,96},{96,128},{128,160},{160,192},{192,224},{224... | collective-permute-start | bytes 122888 | tf_op jit(solution)/shard_map/ppermute | solution.py:580
  18.1 1.3 %collective-permute-start.2 = (f32[10,8,128]{2,1,0:T(8,128)S(1)}, f32[10,8,128]{2,1,0:T(8,128)S(1)}, u32[]{:S(2)}, u32[]{:S(2)}) collective-permute-start(f32[10,8,128]{2,1,0:T(8,128)S(1)} %get-tuple-element.26), channel_id=1, source_target_pairs={{32,1},{33,2},{34,3},{64,33},{65,34},{66,35},{96,65},{97,66},{98,6... | collective-permute-start | bytes 122888 | tf_op jit(solution)/shard_map/ppermute | solution.py:580
  19.4 3.3 %collective-permute-start.3 = (f32[10,8,128]{2,1,0:T(8,128)S(1)}, f32[10,8,128]{2,1,0:T(8,128)S(1)}, u32[]{:S(2)}, u32[]{:S(2)}) collective-permute-start(f32[10,8,128]{2,1,0:T(8,128)S(1)} %get-tuple-element.27), channel_id=1, source_target_pairs={{32,0},{64,32},{96,64},{128,96},{160,128},{192,160},{224,192},{256... | collective-permute-start | bytes 122888 | tf_op jit(solution)/shard_map/ppermute | solution.py:580
  22.7 0.0 collective-permute-done.plane_left
  22.7 0.0 collective-permute-done.1.from_left
  22.7 4.6 %collective-permute-done.3.from_right = f32[10,8,128]{2,1,0:T(8,128)S(1)} collective-permute-done((f32[10,8,128]{2,1,0:T(8,128)S(1)}, f32[10,8,128]{2,1,0:T(8,128)S(1)}, u32[]{:S(2)}, u32[]{:S(2)}) %collective-permute-start.3) | collective-permute-done | bytes 40992 | tf_op jit(solution)/shard_map/ppermute | solution.py:580
  27.4 0.0 collective-permute-done.4.plane
  27.4 1.6 %shard_map.51 = (f32[9,32,8,128]{3,2,1,0:T(8,128)S(1)}, f32[6,8,128]{2,1,0:T(8,128)S(1)}, f32[93,8,128]{2,1,0:T(8,128)S(1)}, f32[75,8,128]{2,1,0:T(8,128)S(1)}) custom-call(f32[10,8,128]{2,1,0:T(8,128)S(1)} %collective-permute-done.plane_left, f32[10,8,128]{2,1,0:T(8,128)S(1)} %collective-permute-done.1.from_left, ...), custom_call_target="tpu_custom_call" | custom-call | tf_op jit(solution)/shard_map/pallas_call | solution.py:611
  29.0 4.7 %collective-permute-start.5 = (f32[93,8,128]{2,1,0:T(8,128)S(1)}, f32[93,8,128]{2,1,0:T(8,128)S(1)}, u32[]{:S(2)}, u32[]{:S(2)}) collective-permute-start(f32[93,8,128]{2,1,0:T(8,128)S(1)} %get-tuple-element.33), channel_id=1, source_target_pairs={{0,4},{4,8},{8,12},{12,16},{16,20},{20,24},{24,28},{1,5},{5,9},{9,... | collective-permute-start | bytes 1142792 | tf_op jit(solution)/shard_map/ppermute | solution.py:580
  33.7 1.9 %collective-permute-start.6 = (f32[75,8,128]{2,1,0:T(8,128)S(1)}, f32[75,8,128]{2,1,0:T(8,128)S(1)}, u32[]{:S(2)}, u32[]{:S(2)}) collective-permute-start(f32[75,8,128]{2,1,0:T(8,128)S(1)} %get-tuple-element.34), channel_id=1, source_target_pairs={{4,0},{8,4},{12,8},{16,12},{20,16},{24,20},{28,24},{5,1},{9,5},{13... | collective-permute-start | bytes 921608 | tf_op jit(solution)/shard_map/ppermute | solution.py:580
  35.7 9.1 %collective-permute-done.6.from_high = f32[75,8,128]{2,1,0:T(8,128)S(1)} collective-permute-done((f32[75,8,128]{2,1,0:T(8,128)S(1)}, f32[75,8,128]{2,1,0:T(8,128)S(1)}, u32[]{:S(2)}, u32[]{:S(2)}) %collective-permute-start.6) | collective-permute-done | bytes 307232 | tf_op jit(solution)/shard_map/ppermute | solution.py:580
  44.7 1.2 %shard_map.52 = (f32[9,27,16,128]{3,2,1,0:T(8,128)S(1)}, f32[3,16,128]{2,1,0:T(8,128)S(1)}, f32[3,24,128]{2,1,0:T(8,128)S(1)}, f32[3,16,128]{2,1,0:T(8,128)S(1)}...) custom-call(f32[9,32,8,128]{3,2,1,0:T(8,128)S(1)} %get-tuple-element.31.w, f32[6,8,128]{2,1,0:T(8,128)S(1)} %get-tuple-element.32.wl, ...), custom_call_target="tpu_custom_call" | custom-call | tf_op jit(solution)/shard_map/pallas_call | solution.py:623
  45.9 0.7 %collective-permute-start.7 = (f32[424,128]{1,0:T(8,128)S(1)}, f32[424,128]{1,0:T(8,128)S(1)}, u32[]{:S(2)}, u32[]{:S(2)}) collective-permute-start(f32[424,128]{1,0:T(8,128)S(1)} %get-tuple-element.39), channel_id=1, source_target_pairs={{1,2},{2,1},{5,6},{6,5},{9,10},{10,9},{13,14},{14,13},{17,18},{18,... | collective-permute-start | bytes 651272 | tf_op jit(solution)/shard_map/ppermute | solution.py:586
  46.6 1.9 %collective-permute-start.8 = (f32[424,128]{1,0:T(8,128)S(1)}, f32[424,128]{1,0:T(8,128)S(1)}, u32[]{:S(2)}, u32[]{:S(2)}) collective-permute-start(f32[424,128]{1,0:T(8,128)S(1)} %get-tuple-element.40), channel_id=1, source_target_pairs={{0,1},{2,3},{1,0},{3,2},{4,5},{6,7},{5,4},{7,6},{8,9},{10,11},{9,8... | collective-permute-start | bytes 651272 | tf_op jit(solution)/shard_map/ppermute | solution.py:586
  48.6 1.4 %collective-permute-done.8.from_pair = f32[424,128]{1,0:T(8,128)S(1)} collective-permute-done((f32[424,128]{1,0:T(8,128)S(1)}, f32[424,128]{1,0:T(8,128)S(1)}, u32[]{:S(2)}, u32[]{:S(2)}) %collective-permute-start.8) | collective-permute-done | bytes 217120 | tf_op jit(solution)/shard_map/ppermute | solution.py:586
  50.0 0.8 %shard_map.54 = (f32[3,16,128]{2,1,0:T(8,128)S(1)}, f32[3,16,128]{2,1,0:T(8,128)S(1)}, f32[3,16,128]{2,1,0:T(8,128)S(1)}, f32[24,128]{1,0:T(8,128)S(1)}, f32[24,128]{1,0:T(8,128)S(1)}) custom-call(f32[9,27,16,128]{3,2,1,0:T(8,128)S(1)} %get-tuple-element.35.whole, f32[3,16,128]{2,1,0:T(8,128)S(1)} %get-tuple-element.36.q, ...), custom_call_target="tpu_custom_call" | custom-call | tf_op jit(solution)/shard_map/pallas_call | solution.py:645
  50.7 0.7 %collective-permute-start.9 = (f32[24,128]{1,0:T(8,128)S(1)}, f32[24,128]{1,0:T(8,128)S(1)}, u32[]{:S(2)}, u32[]{:S(2)}) collective-permute-start(f32[24,128]{1,0:T(8,128)S(1)} %get-tuple-element.44), channel_id=1, source_target_pairs={{1,2},{2,1},{5,6},{6,5},{9,10},{10,9},{13,14},{14,13},{17,18},{18,... | collective-permute-start | bytes 36872 | tf_op jit(solution)/shard_map/ppermute | solution.py:586
  51.4 6.6 %collective-permute-start.10 = (f32[24,128]{1,0:T(8,128)S(1)}, f32[24,128]{1,0:T(8,128)S(1)}, u32[]{:S(2)}, u32[]{:S(2)}) collective-permute-start(f32[24,128]{1,0:T(8,128)S(1)} %get-tuple-element.45), channel_id=1, source_target_pairs={{0,1},{2,3},{1,0},{3,2},{4,5},{6,7},{5,4},{7,6},{8,9},{10,11},{9,8... | collective-permute-start | bytes 36872 | tf_op jit(solution)/shard_map/ppermute | solution.py:586
  58.0 1.2 %shard_map.53 = f32[3,3,3,3,3,2,4,64]{7,6,5,4,3,2,1,0:T(4,128)} custom-call(f32[9,27,16,128]{3,2,1,0:T(8,128)S(1)} %get-tuple-element.35.whole), custom_call_target="tpu_custom_call" | custom-call | flops 500000 | bytes 3000000 | tf_op jit(solution)/shard_map/pallas_call | solution.py:631
  59.3 0.0 collective-permute-done.9.from_other
  59.3 0.9 %shard_map.55 = f32[3,2,4,64]{3,2,1,0:T(4,128)} custom-call(f32[9,27,16,128]{3,2,1,0:T(8,128)S(1)} %get-tuple-element.35.whole, f32[3,16,128]{2,1,0:T(8,128)S(1)} %get-tuple-element.41.q, f32[3,16,128]{2,1,0:T(8,128)S(1)} %get-tuple-element.42.d, f32[3,16,128]{2,1,0:T(8,128)S(1)} %get-tuple-element.38.inverse, f32[3,16,128]{2,1,0:T(8,128)S(1)} %get-tuple-element.43.x, ...), custom_call_target="tpu_custom_call" | custom-call | tf_op jit(solution)/shard_map/pallas_call | solution.py:654
  (4 shorter events, 0.0 us)
Async XLA Ops:
  5.4 21.9 %collective-permute-start.4 = (f32[56,8,128]{2,1,0:T(8,128)S(1)}, f32[56,8,128]{2,1,0:T(8,128)S(1)}, u32[]{:S(2)}, u32[]{:S(2)}) collective-permute-start(f32[56,8,128]{2,1,0:T(8,128)S(1)} %get-tuple-element.28), channel_id=1, source_target_pairs={{0,1},{1,2},{2,3},{4,5},{5,6},{6,7},{8,9},{9,10},{10,11},{12,13},{... | collective-permute-start | bytes 688136 | tf_op jit(solution)/shard_map/ppermute | solution.py:580
  7.2 15.5 %collective-permute-start = (f32[10,8,128]{2,1,0:T(8,128)S(1)}, f32[10,8,128]{2,1,0:T(8,128)S(1)}, u32[]{:S(2)}, u32[]{:S(2)}) collective-permute-start(f32[10,8,128]{2,1,0:T(8,128)S(1)} %get-tuple-element.24), channel_id=1, source_target_pairs={{0,33},{1,34},{2,35},{32,65},{33,66},{34,67},{64,97},{65,98},{66,9... | collective-permute-start | bytes 122888 | tf_op jit(solution)/shard_map/ppermute | solution.py:580
  15.6 7.2 %collective-permute-start.1 = (f32[10,8,128]{2,1,0:T(8,128)S(1)}, f32[10,8,128]{2,1,0:T(8,128)S(1)}, u32[]{:S(2)}, u32[]{:S(2)}) collective-permute-start(f32[10,8,128]{2,1,0:T(8,128)S(1)} %get-tuple-element.25), channel_id=1, source_target_pairs={{0,32},{32,64},{64,96},{96,128},{128,160},{160,192},{192,224},{224... | collective-permute-start | bytes 122888 | tf_op jit(solution)/shard_map/ppermute | solution.py:580
  18.1 4.7 %collective-permute-start.2 = (f32[10,8,128]{2,1,0:T(8,128)S(1)}, f32[10,8,128]{2,1,0:T(8,128)S(1)}, u32[]{:S(2)}, u32[]{:S(2)}) collective-permute-start(f32[10,8,128]{2,1,0:T(8,128)S(1)} %get-tuple-element.26), channel_id=1, source_target_pairs={{32,1},{33,2},{34,3},{64,33},{65,34},{66,35},{96,65},{97,66},{98,6... | collective-permute-start | bytes 122888 | tf_op jit(solution)/shard_map/ppermute | solution.py:580
  19.4 8.0 %collective-permute-start.3 = (f32[10,8,128]{2,1,0:T(8,128)S(1)}, f32[10,8,128]{2,1,0:T(8,128)S(1)}, u32[]{:S(2)}, u32[]{:S(2)}) collective-permute-start(f32[10,8,128]{2,1,0:T(8,128)S(1)} %get-tuple-element.27), channel_id=1, source_target_pairs={{32,0},{64,32},{96,64},{128,96},{160,128},{192,160},{224,192},{256... | collective-permute-start | bytes 122888 | tf_op jit(solution)/shard_map/ppermute | solution.py:580
  29.0 15.7 %collective-permute-start.5 = (f32[93,8,128]{2,1,0:T(8,128)S(1)}, f32[93,8,128]{2,1,0:T(8,128)S(1)}, u32[]{:S(2)}, u32[]{:S(2)}) collective-permute-start(f32[93,8,128]{2,1,0:T(8,128)S(1)} %get-tuple-element.33), channel_id=1, source_target_pairs={{0,4},{4,8},{8,12},{12,16},{16,20},{20,24},{24,28},{1,5},{5,9},{9,... | collective-permute-start | bytes 1142792 | tf_op jit(solution)/shard_map/ppermute | solution.py:580
  33.7 11.0 %collective-permute-start.6 = (f32[75,8,128]{2,1,0:T(8,128)S(1)}, f32[75,8,128]{2,1,0:T(8,128)S(1)}, u32[]{:S(2)}, u32[]{:S(2)}) collective-permute-start(f32[75,8,128]{2,1,0:T(8,128)S(1)} %get-tuple-element.34), channel_id=1, source_target_pairs={{4,0},{8,4},{12,8},{16,12},{20,16},{24,20},{28,24},{5,1},{9,5},{13... | collective-permute-start | bytes 921608 | tf_op jit(solution)/shard_map/ppermute | solution.py:580
  45.9 2.6 %collective-permute-start.7 = (f32[424,128]{1,0:T(8,128)S(1)}, f32[424,128]{1,0:T(8,128)S(1)}, u32[]{:S(2)}, u32[]{:S(2)}) collective-permute-start(f32[424,128]{1,0:T(8,128)S(1)} %get-tuple-element.39), channel_id=1, source_target_pairs={{1,2},{2,1},{5,6},{6,5},{9,10},{10,9},{13,14},{14,13},{17,18},{18,... | collective-permute-start | bytes 651272 | tf_op jit(solution)/shard_map/ppermute | solution.py:586
  46.6 3.4 %collective-permute-start.8 = (f32[424,128]{1,0:T(8,128)S(1)}, f32[424,128]{1,0:T(8,128)S(1)}, u32[]{:S(2)}, u32[]{:S(2)}) collective-permute-start(f32[424,128]{1,0:T(8,128)S(1)} %get-tuple-element.40), channel_id=1, source_target_pairs={{0,1},{2,3},{1,0},{3,2},{4,5},{6,7},{5,4},{7,6},{8,9},{10,11},{9,8... | collective-permute-start | bytes 651272 | tf_op jit(solution)/shard_map/ppermute | solution.py:586
  50.7 8.5 %collective-permute-start.9 = (f32[24,128]{1,0:T(8,128)S(1)}, f32[24,128]{1,0:T(8,128)S(1)}, u32[]{:S(2)}, u32[]{:S(2)}) collective-permute-start(f32[24,128]{1,0:T(8,128)S(1)} %get-tuple-element.44), channel_id=1, source_target_pairs={{1,2},{2,1},{5,6},{6,5},{9,10},{10,9},{13,14},{14,13},{17,18},{18,... | collective-permute-start | bytes 36872 | tf_op jit(solution)/shard_map/ppermute | solution.py:586
  51.4 7.9 %collective-permute-start.10 = (f32[24,128]{1,0:T(8,128)S(1)}, f32[24,128]{1,0:T(8,128)S(1)}, u32[]{:S(2)}, u32[]{:S(2)}) collective-permute-start(f32[24,128]{1,0:T(8,128)S(1)} %get-tuple-element.45), channel_id=1, source_target_pairs={{0,1},{2,3},{1,0},{3,2},{4,5},{6,7},{5,4},{7,6},{8,9},{10,11},{9,8... | collective-permute-start | bytes 36872 | tf_op jit(solution)/shard_map/ppermute | solution.py:586

commit v4 on v3

--- a/solution.py
+++ b/solution.py
@@ -43,10 +43,10 @@
     return v if s == 0 else pltpu.roll(v, s, 0)
 
 
-def slot_mask(lane, j):
-    right = jnp.logical_and(lane >= 3 * j, lane < 3 * j + 3)
-    left = jnp.logical_and(lane >= 3 * j + 61, lane < 3 * j + 64)
-    return jnp.logical_or(right, left)
+def halo_slots():
+    lane = lanes_of()
+    left = jnp.where(jnp.logical_and(lane >= 61, lane < 121), lax.div(lane - 61, 3), -1)
+    return jnp.where(lane < 60, lax.div(lane, 3), left)
 
 
 def packed_size(n):
@@ -55,6 +55,7 @@
 
 def pack(vs):
     lane = lanes_of()
+    slots = halo_slots()
     out = []
     for i in range(0, len(vs), 2):
         other = lroll(vs[i + 1], 64) if i + 1 < len(vs) else jnp.zeros_like(vs[i])
@@ -62,7 +63,7 @@
     for base in range(0, len(vs), 20):
         held = jnp.zeros((8, 128), jnp.float32)
         for j, v in enumerate(vs[base : base + 20]):
-            held = jnp.where(slot_mask(lane, j), lroll(v, 3 * j - 64), held)
+            held = jnp.where(slots == j, lroll(v, 3 * j - 64), held)
         out.append(held)
     return out
 
@@ -81,29 +82,29 @@
     return out
 
 
-def right_slot(lane, j):
-    return lane // 4 == j
-
-
-def left_slot(lane, j):
-    at = (lane - (4 * j + 67)) % 128
-    return at < 3
+def right_slots():
+    return lax.div(lanes_of(), 4)
+
+
+def left_slots():
+    lane = lanes_of()
+    return lax.div(jnp.where(lane < 67, lane + 61, lane - 67), 4)
 
 
 def pack_sides(vs):
-    lane = lanes_of()
+    rights, lefts = right_slots(), left_slots()
     right = jnp.zeros((8, 128), jnp.float32)
     left = jnp.zeros((8, 128), jnp.float32)
     for j, v in enumerate(vs):
         moved = lroll(v, 4 * j - 61)
-        right = jnp.where(right_slot(lane, j), moved, right)
-        left = jnp.where(left_slot(lane, j), moved, left)
+        right = jnp.where(rights == j, moved, right)
+        left = jnp.where(lefts == j, moved, left)
     return right, left
 
 
 def sides(from_left, from_right, j):
     lane = lanes_of()
-    both = lroll(jnp.where(right_slot(lane, j), from_left, from_right), -(4 * j + 3))
+    both = lroll(jnp.where(right_slots() == j, from_left, from_right), -(4 * j + 3))
     ends = jnp.logical_or(jnp.logical_or(lane >= 125, lane == 0), jnp.logical_and(lane >= 64, lane < 67))
     return jnp.where(ends, both, 0.0)
 
@@ -112,25 +113,22 @@
     return n // 2 + 1
 
 
-def pack_plane(vs):
+def pack_plane(vs, right):
     lane = lanes_of()
     out = [jnp.where(lane < 64, vs[i], lroll(vs[i + 1], 64)) for i in range(0, len(vs) - 1, 2)]
-    last = jnp.where(lane < 64, vs[-1], 0.0)
-    for i, v in enumerate(vs):
-        last = jnp.where(lane == 64 + i, lroll(v, i), last)
-    return out + [last]
+    return out + [jnp.where(lane < 64, vs[-1], lroll(right, 64))]
 
 
 def unpack_plane(load, n, from_left, from_right):
     lane = lanes_of()
-    last = load(n // 2)
+    beyond = jnp.logical_and(jnp.logical_and(lane >= 67, lane < 64 + 4 * n), lax.rem(lane, 4) == 3)
+    from_right = from_right + jnp.where(beyond, load(n // 2), 0.0)
     out = []
     for i in range(n):
         main = load(i // 2)
         if i % 2:
             main = lroll(main, 64)
-        main = jnp.where(lane < 64, main, jnp.where(lane == 64, lroll(last, -i), 0.0))
-        out.append(main + sides(from_left, from_right, i))
+        out.append(jnp.where(lane < 64, main, 0.0) + sides(from_left, from_right, i))
     return out
 
 
@@ -227,8 +225,9 @@
         for i, v in enumerate(kept):
             w[step, i] = v
         right[step], left[step] = pack_sides(kept)
-        plane_right[step], plane_left[step] = pack_sides(sent)
-        for i, v in enumerate(pack_plane(sent)):
+        sent_right, plane_left[step] = pack_sides(sent)
+        plane_right[step] = sent_right
+        for i, v in enumerate(pack_plane(sent, sent_right)):
             plane[step * plane_size(PLANE) + i] = v
 
     def scales():
@@ -276,8 +275,9 @@
             wl[i] = v
 
         right[9], left[9] = pack_sides(vs)
-        plane_right[9], plane_left[9] = pack_sides(vs[3:])
-        for i, v in enumerate(pack_plane(vs[3:])):
+        sent_right, plane_left[9] = pack_sides(vs[3:])
+        plane_right[9] = sent_right
+        for i, v in enumerate(pack_plane(vs[3:], sent_right)):
             plane[9 * plane_size(PLANE) + i] = v
 
     classes_copy.wait()
@@ -298,7 +298,7 @@
     lax.fori_loop(0, 9, body, 0, unroll=9)
 
 
-def planes_kernel(plane_left, from_left, plane_right, from_right, plane, w, wl, w_out, wl_out, up, down, total):
+def planes_kernel(plane_right, from_right, plane_left, from_left, plane, w, wl, w_out, wl_out, up, down, total):
     row = rows_of()
     even = row % 2 == 0
     total[...] = jnp.zeros_like(total)
@@ -615,7 +615,7 @@
         out_shape=[w_shape, wl_shape, shape(9 * packed_size(UPS) + packed_size(3), 8, 128), shape(9 * packed_size(DOWNS) + packed_size(3), 8, 128)],
         scratch_shapes=[pltpu.VMEM((3, 8, 128), jnp.float32)],
         compiler_params=LIMIT,
-    )(plane_left, from_left, plane_right, from_right, plane, w, wl)
+    )(plane_right, from_right, plane_left, from_left, plane, w, wl)
     from_high = along(down, ("gy",), (-1,))
     from_low = along(up, ("gy",), (1,))
     whole_shape, vector = shape(9, 27, 16, 128), shape(3, 16, 128)

time: 61.4 us -> 58.1 us (0.946)
  the two profiles are of different devices: /device:TPU:218 before, /device:TPU:281 now
where the time goes in v4:
time: 58.1 us; the launch traced here: 57.6 us
  starting transfers between devices  33 us (57%)
  waiting for transfers between devices  13.4 us (23%)
  Pallas kernels  10.4 us (18%)
  between operations  0.77 us (1%)
    ppermute x7, starting transfers between devices, along(): return lax.ppermute(block, axes, route)  21 us
    ppermute x4, starting transfers between devices, exchanged(): return lax.ppermute(block, axis, pairs + [(j, i) for i, j in pairs])  12 us
    ppermute x7, waiting for transfers between devices, along(): return lax.ppermute(block, axes, route)  10.9 us
    pallas_call x1, Pallas kernels, shards(): pl.pallas_call(coarsen_kernel, in_specs=[HBM] * 3, out_specs=[VMEM] * 7,...  4.81 us
    ppermute x4, waiting for transfers between devices, exchanged(): return lax.ppermute(block, axis, pairs + [(j, i) for i, j in pairs])  2.48 us
    pallas_call x1, Pallas kernels, shards(): pl.pallas_call(planes_kernel, in_specs=[VMEM] * 7, out_specs=[VMEM] * 4,...  1.54 us
    pallas_call x1, Pallas kernels, shards(): pl.pallas_call(operator_kernel, in_specs=[VMEM], out_specs=VMEM, out_shap...  1.23 us
    pallas_call x1, Pallas kernels, shards(): pl.pallas_call(rows_kernel, in_specs=[VMEM] * 4, out_specs=[VMEM] * 6, ou...  1.18 us
  transfers between devices with their start and end apart: 11, of which 4 were waited for; matrix products, arithmetic and copies ran while one was open for 0% of the time, Pallas kernels for 2%

profile of v4, /device:TPU:281, one launch (start us, length us, event | category | flops | bytes accessed | tf_op | source)
XLA Modules:
  0.0 57.6 jit_solution(4646766276933754820)
XLA Ops:
  0.6 4.8 %shard_map.50 = (f32[9,32,8,128]{3,2,1,0:T(8,128)S(1)}, f32[6,8,128]{2,1,0:T(8,128)S(1)}, f32[10,8,128]{2,1,0:T(8,128)S(1)}, f32[10,8,128]{2,1,0:T(8,128)S(1)}, ...) custom-call(f32[3,3,3,3,3,4,8,128]{7,6,5,4,3,2,1,0:T(8,128)} %blocks_in.1, ...), custom_call_target="tpu_custom_call" | custom-call | tf_op jit(solution)/shard_map/pallas_call | solution.py:592
  5.4 5.2 %collective-permute-start.4 = (f32[56,8,128]{2,1,0:T(8,128)S(1)}, f32[56,8,128]{2,1,0:T(8,128)S(1)}, u32[]{:S(2)}, u32[]{:S(2)}) collective-permute-start(f32[56,8,128]{2,1,0:T(8,128)S(1)} %get-tuple-element.28), channel_id=1, source_target_pairs={{0,1},{1,2},{2,3},{4,5},{5,6},{6,7},{8,9},{9,10},{10,11},{12,13},{... | collective-permute-start | bytes 688136 | tf_op jit(solution)/shard_map/ppermute | solution.py:580
  10.7 1.9 %collective-permute-start = (f32[10,8,128]{2,1,0:T(8,128)S(1)}, f32[10,8,128]{2,1,0:T(8,128)S(1)}, u32[]{:S(2)}, u32[]{:S(2)}) collective-permute-start(f32[10,8,128]{2,1,0:T(8,128)S(1)} %get-tuple-element.24), channel_id=1, source_target_pairs={{32,1},{33,2},{34,3},{64,33},{65,34},{66,35},{96,65},{97,66},{98,6... | collective-permute-start | bytes 122888 | tf_op jit(solution)/shard_map/ppermute | solution.py:580
  12.6 1.9 %collective-permute-start.1 = (f32[10,8,128]{2,1,0:T(8,128)S(1)}, f32[10,8,128]{2,1,0:T(8,128)S(1)}, u32[]{:S(2)}, u32[]{:S(2)}) collective-permute-start(f32[10,8,128]{2,1,0:T(8,128)S(1)} %get-tuple-element.25), channel_id=1, source_target_pairs={{32,0},{64,32},{96,64},{128,96},{160,128},{192,160},{224,192},{256... | collective-permute-start | bytes 122888 | tf_op jit(solution)/shard_map/ppermute | solution.py:580
  14.5 2.5 %collective-permute-start.2 = (f32[10,8,128]{2,1,0:T(8,128)S(1)}, f32[10,8,128]{2,1,0:T(8,128)S(1)}, u32[]{:S(2)}, u32[]{:S(2)}) collective-permute-start(f32[10,8,128]{2,1,0:T(8,128)S(1)} %get-tuple-element.26), channel_id=1, source_target_pairs={{0,33},{1,34},{2,35},{32,65},{33,66},{34,67},{64,97},{65,98},{66,9... | collective-permute-start | bytes 122888 | tf_op jit(solution)/shard_map/ppermute | solution.py:580
  17.0 3.1 %collective-permute-start.3 = (f32[10,8,128]{2,1,0:T(8,128)S(1)}, f32[10,8,128]{2,1,0:T(8,128)S(1)}, u32[]{:S(2)}, u32[]{:S(2)}) collective-permute-start(f32[10,8,128]{2,1,0:T(8,128)S(1)} %get-tuple-element.27), channel_id=1, source_target_pairs={{0,32},{32,64},{64,96},{96,128},{128,160},{160,192},{192,224},{224... | collective-permute-start | bytes 122888 | tf_op jit(solution)/shard_map/ppermute | solution.py:580
  20.1 0.0 collective-permute-done.plane_right
  20.2 1.8 %collective-permute-done.2.plane_left = f32[10,8,128]{2,1,0:T(8,128)S(1)} collective-permute-done((f32[10,8,128]{2,1,0:T(8,128)S(1)}, f32[10,8,128]{2,1,0:T(8,128)S(1)}, u32[]{:S(2)}, u32[]{:S(2)}) %collective-permute-start.2) | collective-permute-done | bytes 40992 | tf_op jit(solution)/shard_map/ppermute | solution.py:580
  22.0 1.9 %collective-permute-done.3.from_left = f32[10,8,128]{2,1,0:T(8,128)S(1)} collective-permute-done((f32[10,8,128]{2,1,0:T(8,128)S(1)}, f32[10,8,128]{2,1,0:T(8,128)S(1)}, u32[]{:S(2)}, u32[]{:S(2)}) %collective-permute-start.3) | collective-permute-done | bytes 40992 | tf_op jit(solution)/shard_map/ppermute | solution.py:580
  23.9 1.5 %shard_map.51 = (f32[9,32,8,128]{3,2,1,0:T(8,128)S(1)}, f32[6,8,128]{2,1,0:T(8,128)S(1)}, f32[93,8,128]{2,1,0:T(8,128)S(1)}, f32[75,8,128]{2,1,0:T(8,128)S(1)}) custom-call(f32[10,8,128]{2,1,0:T(8,128)S(1)} %collective-permute-done.plane_right, f32[10,8,128]{2,1,0:T(8,128)S(1)} %collective-permute-done.1.from_right, ...), custom_call_target="tpu_custom_call" | custom-call | tf_op jit(solution)/shard_map/pallas_call | solution.py:611
  25.4 4.4 %collective-permute-start.5 = (f32[93,8,128]{2,1,0:T(8,128)S(1)}, f32[93,8,128]{2,1,0:T(8,128)S(1)}, u32[]{:S(2)}, u32[]{:S(2)}) collective-permute-start(f32[93,8,128]{2,1,0:T(8,128)S(1)} %get-tuple-element.33), channel_id=1, source_target_pairs={{0,4},{4,8},{8,12},{12,16},{16,20},{20,24},{24,28},{1,5},{5,9},{9,... | collective-permute-start | bytes 1142792 | tf_op jit(solution)/shard_map/ppermute | solution.py:580
  29.8 1.9 %collective-permute-start.6 = (f32[75,8,128]{2,1,0:T(8,128)S(1)}, f32[75,8,128]{2,1,0:T(8,128)S(1)}, u32[]{:S(2)}, u32[]{:S(2)}) collective-permute-start(f32[75,8,128]{2,1,0:T(8,128)S(1)} %get-tuple-element.34), channel_id=1, source_target_pairs={{4,0},{8,4},{12,8},{16,12},{20,16},{24,20},{28,24},{5,1},{9,5},{13... | collective-permute-start | bytes 921608 | tf_op jit(solution)/shard_map/ppermute | solution.py:580
  31.8 7.2 %collective-permute-done.6.from_high = f32[75,8,128]{2,1,0:T(8,128)S(1)} collective-permute-done((f32[75,8,128]{2,1,0:T(8,128)S(1)}, f32[75,8,128]{2,1,0:T(8,128)S(1)}, u32[]{:S(2)}, u32[]{:S(2)}) %collective-permute-start.6) | collective-permute-done | bytes 307232 | tf_op jit(solution)/shard_map/ppermute | solution.py:580
  39.0 1.2 %shard_map.52 = (f32[9,27,16,128]{3,2,1,0:T(8,128)S(1)}, f32[3,16,128]{2,1,0:T(8,128)S(1)}, f32[3,24,128]{2,1,0:T(8,128)S(1)}, f32[3,16,128]{2,1,0:T(8,128)S(1)}...) custom-call(f32[9,32,8,128]{3,2,1,0:T(8,128)S(1)} %get-tuple-element.31.w, f32[6,8,128]{2,1,0:T(8,128)S(1)} %get-tuple-element.32.wl, ...), custom_call_target="tpu_custom_call" | custom-call | tf_op jit(solution)/shard_map/pallas_call | solution.py:623
  40.2 3.9 %collective-permute-start.7 = (f32[424,128]{1,0:T(8,128)S(1)}, f32[424,128]{1,0:T(8,128)S(1)}, u32[]{:S(2)}, u32[]{:S(2)}) collective-permute-start(f32[424,128]{1,0:T(8,128)S(1)} %get-tuple-element.39), channel_id=1, source_target_pairs={{1,2},{2,1},{5,6},{6,5},{9,10},{10,9},{13,14},{14,13},{17,18},{18,... | collective-permute-start | bytes 651272 | tf_op jit(solution)/shard_map/ppermute | solution.py:586
  44.1 2.3 %collective-permute-start.8 = (f32[424,128]{1,0:T(8,128)S(1)}, f32[424,128]{1,0:T(8,128)S(1)}, u32[]{:S(2)}, u32[]{:S(2)}) collective-permute-start(f32[424,128]{1,0:T(8,128)S(1)} %get-tuple-element.40), channel_id=1, source_target_pairs={{0,1},{2,3},{1,0},{3,2},{4,5},{6,7},{5,4},{7,6},{8,9},{10,11},{9,8... | collective-permute-start | bytes 651272 | tf_op jit(solution)/shard_map/ppermute | solution.py:586
  46.4 2.5 %collective-permute-done.7.from_other = f32[424,128]{1,0:T(8,128)S(1)} collective-permute-done((f32[424,128]{1,0:T(8,128)S(1)}, f32[424,128]{1,0:T(8,128)S(1)}, u32[]{:S(2)}, u32[]{:S(2)}) %collective-permute-start.7) | collective-permute-done | bytes 217120 | tf_op jit(solution)/shard_map/ppermute | solution.py:586
  48.9 0.0 collective-permute-done.8.from_pair
  48.9 0.8 %shard_map.54 = (f32[3,16,128]{2,1,0:T(8,128)S(1)}, f32[3,16,128]{2,1,0:T(8,128)S(1)}, f32[3,16,128]{2,1,0:T(8,128)S(1)}, f32[24,128]{1,0:T(8,128)S(1)}, f32[24,128]{1,0:T(8,128)S(1)}) custom-call(f32[9,27,16,128]{3,2,1,0:T(8,128)S(1)} %get-tuple-element.35.whole, f32[3,16,128]{2,1,0:T(8,128)S(1)} %get-tuple-element.36.q, ...), custom_call_target="tpu_custom_call" | custom-call | tf_op jit(solution)/shard_map/pallas_call | solution.py:645
  49.7 3.9 %collective-permute-start.9 = (f32[24,128]{1,0:T(8,128)S(1)}, f32[24,128]{1,0:T(8,128)S(1)}, u32[]{:S(2)}, u32[]{:S(2)}) collective-permute-start(f32[24,128]{1,0:T(8,128)S(1)} %get-tuple-element.44), channel_id=1, source_target_pairs={{1,2},{2,1},{5,6},{6,5},{9,10},{10,9},{13,14},{14,13},{17,18},{18,... | collective-permute-start | bytes 36872 | tf_op jit(solution)/shard_map/ppermute | solution.py:586
  53.6 1.9 %collective-permute-start.10 = (f32[24,128]{1,0:T(8,128)S(1)}, f32[24,128]{1,0:T(8,128)S(1)}, u32[]{:S(2)}, u32[]{:S(2)}) collective-permute-start(f32[24,128]{1,0:T(8,128)S(1)} %get-tuple-element.45), channel_id=1, source_target_pairs={{0,1},{2,3},{1,0},{3,2},{4,5},{6,7},{5,4},{7,6},{8,9},{10,11},{9,8... | collective-permute-start | bytes 36872 | tf_op jit(solution)/shard_map/ppermute | solution.py:586
  55.5 1.2 %shard_map.53 = f32[3,3,3,3,3,2,4,64]{7,6,5,4,3,2,1,0:T(4,128)} custom-call(f32[9,27,16,128]{3,2,1,0:T(8,128)S(1)} %get-tuple-element.35.whole), custom_call_target="tpu_custom_call" | custom-call | flops 500000 | bytes 3000000 | tf_op jit(solution)/shard_map/pallas_call | solution.py:631
  56.7 0.0 collective-permute-done.9.from_other
  56.7 0.9 %shard_map.55 = f32[3,2,4,64]{3,2,1,0:T(4,128)} custom-call(f32[9,27,16,128]{3,2,1,0:T(8,128)S(1)} %get-tuple-element.35.whole, f32[3,16,128]{2,1,0:T(8,128)S(1)} %get-tuple-element.41.q, f32[3,16,128]{2,1,0:T(8,128)S(1)} %get-tuple-element.42.d, f32[3,16,128]{2,1,0:T(8,128)S(1)} %get-tuple-element.38.inverse, f32[3,16,128]{2,1,0:T(8,128)S(1)} %get-tuple-element.43.x, ...), custom_call_target="tpu_custom_call" | custom-call | tf_op jit(solution)/shard_map/pallas_call | solution.py:654
  (4 shorter events, 0.0 us)
Async XLA Ops:
  5.4 18.4 %collective-permute-start.4 = (f32[56,8,128]{2,1,0:T(8,128)S(1)}, f32[56,8,128]{2,1,0:T(8,128)S(1)}, u32[]{:S(2)}, u32[]{:S(2)}) collective-permute-start(f32[56,8,128]{2,1,0:T(8,128)S(1)} %get-tuple-element.28), channel_id=1, source_target_pairs={{0,1},{1,2},{2,3},{4,5},{5,6},{6,7},{8,9},{9,10},{10,11},{12,13},{... | collective-permute-start | bytes 688136 | tf_op jit(solution)/shard_map/ppermute | solution.py:580
  10.7 9.5 %collective-permute-start = (f32[10,8,128]{2,1,0:T(8,128)S(1)}, f32[10,8,128]{2,1,0:T(8,128)S(1)}, u32[]{:S(2)}, u32[]{:S(2)}) collective-permute-start(f32[10,8,128]{2,1,0:T(8,128)S(1)} %get-tuple-element.24), channel_id=1, source_target_pairs={{32,1},{33,2},{34,3},{64,33},{65,34},{66,35},{96,65},{97,66},{98,6... | collective-permute-start | bytes 122888 | tf_op jit(solution)/shard_map/ppermute | solution.py:580
  12.6 7.5 %collective-permute-start.1 = (f32[10,8,128]{2,1,0:T(8,128)S(1)}, f32[10,8,128]{2,1,0:T(8,128)S(1)}, u32[]{:S(2)}, u32[]{:S(2)}) collective-permute-start(f32[10,8,128]{2,1,0:T(8,128)S(1)} %get-tuple-element.25), channel_id=1, source_target_pairs={{32,0},{64,32},{96,64},{128,96},{160,128},{192,160},{224,192},{256... | collective-permute-start | bytes 122888 | tf_op jit(solution)/shard_map/ppermute | solution.py:580
  14.5 7.4 %collective-permute-start.2 = (f32[10,8,128]{2,1,0:T(8,128)S(1)}, f32[10,8,128]{2,1,0:T(8,128)S(1)}, u32[]{:S(2)}, u32[]{:S(2)}) collective-permute-start(f32[10,8,128]{2,1,0:T(8,128)S(1)} %get-tuple-element.26), channel_id=1, source_target_pairs={{0,33},{1,34},{2,35},{32,65},{33,66},{34,67},{64,97},{65,98},{66,9... | collective-permute-start | bytes 122888 | tf_op jit(solution)/shard_map/ppermute | solution.py:580
  17.0 6.9 %collective-permute-start.3 = (f32[10,8,128]{2,1,0:T(8,128)S(1)}, f32[10,8,128]{2,1,0:T(8,128)S(1)}, u32[]{:S(2)}, u32[]{:S(2)}) collective-permute-start(f32[10,8,128]{2,1,0:T(8,128)S(1)} %get-tuple-element.27), channel_id=1, source_target_pairs={{0,32},{32,64},{64,96},{96,128},{128,160},{160,192},{192,224},{224... | collective-permute-start | bytes 122888 | tf_op jit(solution)/shard_map/ppermute | solution.py:580
  25.4 13.6 %collective-permute-start.5 = (f32[93,8,128]{2,1,0:T(8,128)S(1)}, f32[93,8,128]{2,1,0:T(8,128)S(1)}, u32[]{:S(2)}, u32[]{:S(2)}) collective-permute-start(f32[93,8,128]{2,1,0:T(8,128)S(1)} %get-tuple-element.33), channel_id=1, source_target_pairs={{0,4},{4,8},{8,12},{12,16},{16,20},{20,24},{24,28},{1,5},{5,9},{9,... | collective-permute-start | bytes 1142792 | tf_op jit(solution)/shard_map/ppermute | solution.py:580
  29.8 9.2 %collective-permute-start.6 = (f32[75,8,128]{2,1,0:T(8,128)S(1)}, f32[75,8,128]{2,1,0:T(8,128)S(1)}, u32[]{:S(2)}, u32[]{:S(2)}) collective-permute-start(f32[75,8,128]{2,1,0:T(8,128)S(1)} %get-tuple-element.34), channel_id=1, source_target_pairs={{4,0},{8,4},{12,8},{16,12},{20,16},{24,20},{28,24},{5,1},{9,5},{13... | collective-permute-start | bytes 921608 | tf_op jit(solution)/shard_map/ppermute | solution.py:580
  40.2 8.7 %collective-permute-start.7 = (f32[424,128]{1,0:T(8,128)S(1)}, f32[424,128]{1,0:T(8,128)S(1)}, u32[]{:S(2)}, u32[]{:S(2)}) collective-permute-start(f32[424,128]{1,0:T(8,128)S(1)} %get-tuple-element.39), channel_id=1, source_target_pairs={{1,2},{2,1},{5,6},{6,5},{9,10},{10,9},{13,14},{14,13},{17,18},{18,... | collective-permute-start | bytes 651272 | tf_op jit(solution)/shard_map/ppermute | solution.py:586
  44.1 4.8 %collective-permute-start.8 = (f32[424,128]{1,0:T(8,128)S(1)}, f32[424,128]{1,0:T(8,128)S(1)}, u32[]{:S(2)}, u32[]{:S(2)}) collective-permute-start(f32[424,128]{1,0:T(8,128)S(1)} %get-tuple-element.40), channel_id=1, source_target_pairs={{0,1},{2,3},{1,0},{3,2},{4,5},{6,7},{5,4},{7,6},{8,9},{10,11},{9,8... | collective-permute-start | bytes 651272 | tf_op jit(solution)/shard_map/ppermute | solution.py:586
  49.7 7.0 %collective-permute-start.9 = (f32[24,128]{1,0:T(8,128)S(1)}, f32[24,128]{1,0:T(8,128)S(1)}, u32[]{:S(2)}, u32[]{:S(2)}) collective-permute-start(f32[24,128]{1,0:T(8,128)S(1)} %get-tuple-element.44), channel_id=1, source_target_pairs={{1,2},{2,1},{5,6},{6,5},{9,10},{10,9},{13,14},{14,13},{17,18},{18,... | collective-permute-start | bytes 36872 | tf_op jit(solution)/shard_map/ppermute | solution.py:586
  53.6 3.2 %collective-permute-start.10 = (f32[24,128]{1,0:T(8,128)S(1)}, f32[24,128]{1,0:T(8,128)S(1)}, u32[]{:S(2)}, u32[]{:S(2)}) collective-permute-start(f32[24,128]{1,0:T(8,128)S(1)} %get-tuple-element.45), channel_id=1, source_target_pairs={{0,1},{2,3},{1,0},{3,2},{4,5},{6,7},{5,4},{7,6},{8,9},{10,11},{9,8... | collective-permute-start | bytes 36872 | tf_op jit(solution)/shard_map/ppermute | solution.py:586

commit v5 on v4

--- a/solution.py
+++ b/solution.py
@@ -298,7 +298,7 @@
     lax.fori_loop(0, 9, body, 0, unroll=9)
 
 
-def planes_kernel(plane_right, from_right, plane_left, from_left, plane, w, wl, w_out, wl_out, up, down, total):
+def planes_kernel(from_right, plane_right, plane_left, from_left, plane, w, wl, w_out, wl_out, up, down, total):
     row = rows_of()
     even = row % 2 == 0
     total[...] = jnp.zeros_like(total)
@@ -470,7 +470,9 @@
     share_vector(lambda c: d[c], 24, EDGES, to_other, to_pair)
 
 
-def operator_kernel(whole, operator):
+def operator_kernel(whole, operator, written):
+    written[...] = jnp.zeros_like(written)
+
     def body(rc, carry):
         for k in range(27):
             for z in range(2):
@@ -518,7 +520,7 @@
     return sums
 
 
-def two_steps_kernel(rhos, whole, q, d, inverse, from_other, from_pair, q_out, d_out, x_out, to_other, to_pair, near, packed, edges):
+def two_steps_kernel(rhos, whole, q, d, inverse, from_other, from_pair, after, q_out, d_out, x_out, to_other, to_pair, near, packed, edges):
     even = rows_of() % 2 == 0
     for i in range(0, packed.shape[0], 2):
         packed[i], packed[i + 1] = join_planes(*shared(4 * i, 8, from_other, from_pair))
@@ -615,7 +617,7 @@
         out_shape=[w_shape, wl_shape, shape(9 * packed_size(UPS) + packed_size(3), 8, 128), shape(9 * packed_size(DOWNS) + packed_size(3), 8, 128)],
         scratch_shapes=[pltpu.VMEM((3, 8, 128), jnp.float32)],
         compiler_params=LIMIT,
-    )(plane_right, from_right, plane_left, from_left, plane, w, wl)
+    )(from_right, plane_right, plane_left, from_left, plane, w, wl)
     from_high = along(down, ("gy",), (-1,))
     from_low = along(up, ("gy",), (1,))
     whole_shape, vector = shape(9, 27, 16, 128), shape(3, 16, 128)
@@ -628,11 +630,11 @@
         scratch_shapes=[pltpu.VMEM((3, 16, 128), jnp.float32), pltpu.VMEM((8, 128), jnp.float32), near],
         compiler_params=LIMIT,
     )(w, wl, from_low, from_high)
-    operator = pl.pallas_call(
+    operator, written = pl.pallas_call(
         operator_kernel,
         in_specs=[VMEM],
-        out_specs=VMEM,
-        out_shape=shape(3, 3, 3, 3, 3, 2, 4, 64),
+        out_specs=[VMEM] * 2,
+        out_shape=[shape(3, 3, 3, 3, 3, 2, 4, 64), shape(8, 128)],
         compiler_params=LIMIT,
         cost_estimate=pl.CostEstimate(flops=500000, bytes_accessed=3000000, transcendentals=0),
     )(whole)
@@ -644,12 +646,12 @@
     from_other, from_pair = exchanged(to_other, "gz", 1), exchanged(to_pair, "gz", 0)
     q, d, x, to_other, to_pair = pl.pallas_call(
         functools.partial(two_steps_kernel, rhos[:2]),
-        in_specs=[VMEM] * 6,
+        in_specs=[VMEM] * 7,
         out_specs=[VMEM] * 5,
         out_shape=[vector] * 3 + [shape(piece_rows(16), 128)] * 2,
         scratch_shapes=[near, pltpu.VMEM((96, 8, 128), jnp.float32), pltpu.VMEM((87, 16, 128), jnp.float32)],
         compiler_params=LIMIT,
-    )(whole, q, d, inverse, from_other, from_pair)
+    )(whole, q, d, inverse, from_other, from_pair, written)
     from_other, from_pair = exchanged(to_other, "gz", 1), exchanged(to_pair, "gz", 0)
     coarse_solution = pl.pallas_call(
         functools.partial(last_step_kernel, rhos[2]),

time: 58.1 us -> 58 us (level)
  transfers between devices with their start and end apart: 11 -> 11, of which waited for: 4 -> 6; matrix products, arithmetic and copies ran while one was open for 0% -> 0% of each run, Pallas kernels for 2% -> 2%
where the time goes in v5:
time: 58 us; the launch traced here: 57.5 us
  starting transfers between devices  33 us (57%)
  waiting for transfers between devices  13.3 us (23%)
  Pallas kernels  10.4 us (18%)
  between operations  0.77 us (1%)
    ppermute x7, starting transfers between devices, along(): return lax.ppermute(block, axes, route)  21 us
    ppermute x4, starting transfers between devices, exchanged(): return lax.ppermute(block, axis, pairs + [(j, i) for i, j in pairs])  12 us
    ppermute x7, waiting for transfers between devices, along(): return lax.ppermute(block, axes, route)  10.9 us
    pallas_call x1, Pallas kernels, shards(): pl.pallas_call(coarsen_kernel, in_specs=[HBM] * 3, out_specs=[VMEM] * 7,...  4.81 us
    ppermute x4, waiting for transfers between devices, exchanged(): return lax.ppermute(block, axis, pairs + [(j, i) for i, j in pairs])  2.4 us
    pallas_call x1, Pallas kernels, shards(): pl.pallas_call(planes_kernel, in_specs=[VMEM] * 7, out_specs=[VMEM] * 4,...  1.54 us
    pallas_call x1, Pallas kernels, shards(): pl.pallas_call(operator_kernel, in_specs=[VMEM], out_specs=[VMEM] * 2, ou...  1.23 us
    pallas_call x1, Pallas kernels, shards(): pl.pallas_call(rows_kernel, in_specs=[VMEM] * 4, out_specs=[VMEM] * 6, ou...  1.18 us
  transfers between devices with their start and end apart: 11, of which 6 were waited for; matrix products, arithmetic and copies ran while one was open for 0% of the time, Pallas kernels for 2%

profile of v5, /device:TPU:281, one launch (start us, length us, event | category | flops | bytes accessed | tf_op | source)
XLA Modules:
  0.0 57.5 jit_solution(4489113729832389854)
XLA Ops:
  0.6 4.8 %shard_map.50 = (f32[9,32,8,128]{3,2,1,0:T(8,128)S(1)}, f32[6,8,128]{2,1,0:T(8,128)S(1)}, f32[10,8,128]{2,1,0:T(8,128)S(1)}, f32[10,8,128]{2,1,0:T(8,128)S(1)}, ...) custom-call(f32[3,3,3,3,3,4,8,128]{7,6,5,4,3,2,1,0:T(8,128)} %blocks_in.1, ...), custom_call_target="tpu_custom_call" | custom-call | tf_op jit(solution)/shard_map/pallas_call | solution.py:594
  5.4 5.2 %collective-permute-start.4 = (f32[56,8,128]{2,1,0:T(8,128)S(1)}, f32[56,8,128]{2,1,0:T(8,128)S(1)}, u32[]{:S(2)}, u32[]{:S(2)}) collective-permute-start(f32[56,8,128]{2,1,0:T(8,128)S(1)} %get-tuple-element.30), channel_id=1, source_target_pairs={{0,1},{1,2},{2,3},{4,5},{5,6},{6,7},{8,9},{9,10},{10,11},{12,13},{... | collective-permute-start | bytes 688136 | tf_op jit(solution)/shard_map/ppermute | solution.py:582
  10.7 1.9 %collective-permute-start = (f32[10,8,128]{2,1,0:T(8,128)S(1)}, f32[10,8,128]{2,1,0:T(8,128)S(1)}, u32[]{:S(2)}, u32[]{:S(2)}) collective-permute-start(f32[10,8,128]{2,1,0:T(8,128)S(1)} %get-tuple-element.26), channel_id=1, source_target_pairs={{32,0},{64,32},{96,64},{128,96},{160,128},{192,160},{224,192},{256... | collective-permute-start | bytes 122888 | tf_op jit(solution)/shard_map/ppermute | solution.py:582
  12.6 1.9 %collective-permute-start.1 = (f32[10,8,128]{2,1,0:T(8,128)S(1)}, f32[10,8,128]{2,1,0:T(8,128)S(1)}, u32[]{:S(2)}, u32[]{:S(2)}) collective-permute-start(f32[10,8,128]{2,1,0:T(8,128)S(1)} %get-tuple-element.27), channel_id=1, source_target_pairs={{32,1},{33,2},{34,3},{64,33},{65,34},{66,35},{96,65},{97,66},{98,6... | collective-permute-start | bytes 122888 | tf_op jit(solution)/shard_map/ppermute | solution.py:582
  14.5 2.5 %collective-permute-start.2 = (f32[10,8,128]{2,1,0:T(8,128)S(1)}, f32[10,8,128]{2,1,0:T(8,128)S(1)}, u32[]{:S(2)}, u32[]{:S(2)}) collective-permute-start(f32[10,8,128]{2,1,0:T(8,128)S(1)} %get-tuple-element.28), channel_id=1, source_target_pairs={{0,33},{1,34},{2,35},{32,65},{33,66},{34,67},{64,97},{65,98},{66,9... | collective-permute-start | bytes 122888 | tf_op jit(solution)/shard_map/ppermute | solution.py:582
  17.0 3.1 %collective-permute-start.3 = (f32[10,8,128]{2,1,0:T(8,128)S(1)}, f32[10,8,128]{2,1,0:T(8,128)S(1)}, u32[]{:S(2)}, u32[]{:S(2)}) collective-permute-start(f32[10,8,128]{2,1,0:T(8,128)S(1)} %get-tuple-element.29), channel_id=1, source_target_pairs={{0,32},{32,64},{64,96},{96,128},{128,160},{160,192},{192,224},{224... | collective-permute-start | bytes 122888 | tf_op jit(solution)/shard_map/ppermute | solution.py:582
  20.1 0.0 collective-permute-done.from_right
  20.2 1.8 %collective-permute-done.2.plane_left = f32[10,8,128]{2,1,0:T(8,128)S(1)} collective-permute-done((f32[10,8,128]{2,1,0:T(8,128)S(1)}, f32[10,8,128]{2,1,0:T(8,128)S(1)}, u32[]{:S(2)}, u32[]{:S(2)}) %collective-permute-start.2) | collective-permute-done | bytes 40992 | tf_op jit(solution)/shard_map/ppermute | solution.py:582
  22.0 1.9 %collective-permute-done.3.from_left = f32[10,8,128]{2,1,0:T(8,128)S(1)} collective-permute-done((f32[10,8,128]{2,1,0:T(8,128)S(1)}, f32[10,8,128]{2,1,0:T(8,128)S(1)}, u32[]{:S(2)}, u32[]{:S(2)}) %collective-permute-start.3) | collective-permute-done | bytes 40992 | tf_op jit(solution)/shard_map/ppermute | solution.py:582
  23.9 1.5 %shard_map.51 = (f32[9,32,8,128]{3,2,1,0:T(8,128)S(1)}, f32[6,8,128]{2,1,0:T(8,128)S(1)}, f32[93,8,128]{2,1,0:T(8,128)S(1)}, f32[75,8,128]{2,1,0:T(8,128)S(1)}) custom-call(f32[10,8,128]{2,1,0:T(8,128)S(1)} %collective-permute-done.from_right, f32[10,8,128]{2,1,0:T(8,128)S(1)} %collective-permute-done.1.plane_right, ...), custom_call_target="tpu_custom_call" | custom-call | tf_op jit(solution)/shard_map/pallas_call | solution.py:613
  25.4 4.4 %collective-permute-start.5 = (f32[93,8,128]{2,1,0:T(8,128)S(1)}, f32[93,8,128]{2,1,0:T(8,128)S(1)}, u32[]{:S(2)}, u32[]{:S(2)}) collective-permute-start(f32[93,8,128]{2,1,0:T(8,128)S(1)} %get-tuple-element.35), channel_id=1, source_target_pairs={{0,4},{4,8},{8,12},{12,16},{16,20},{20,24},{24,28},{1,5},{5,9},{9,... | collective-permute-start | bytes 1142792 | tf_op jit(solution)/shard_map/ppermute | solution.py:582
  29.8 1.9 %collective-permute-start.6 = (f32[75,8,128]{2,1,0:T(8,128)S(1)}, f32[75,8,128]{2,1,0:T(8,128)S(1)}, u32[]{:S(2)}, u32[]{:S(2)}) collective-permute-start(f32[75,8,128]{2,1,0:T(8,128)S(1)} %get-tuple-element.36), channel_id=1, source_target_pairs={{4,0},{8,4},{12,8},{16,12},{20,16},{24,20},{28,24},{5,1},{9,5},{13... | collective-permute-start | bytes 921608 | tf_op jit(solution)/shard_map/ppermute | solution.py:582
  31.8 7.2 %collective-permute-done.6.from_high = f32[75,8,128]{2,1,0:T(8,128)S(1)} collective-permute-done((f32[75,8,128]{2,1,0:T(8,128)S(1)}, f32[75,8,128]{2,1,0:T(8,128)S(1)}, u32[]{:S(2)}, u32[]{:S(2)}) %collective-permute-start.6) | collective-permute-done | bytes 307232 | tf_op jit(solution)/shard_map/ppermute | solution.py:582
  39.0 1.2 %shard_map.52 = (f32[9,27,16,128]{3,2,1,0:T(8,128)S(1)}, f32[3,16,128]{2,1,0:T(8,128)S(1)}, f32[3,24,128]{2,1,0:T(8,128)S(1)}, f32[3,16,128]{2,1,0:T(8,128)S(1)}...) custom-call(f32[9,32,8,128]{3,2,1,0:T(8,128)S(1)} %get-tuple-element.33.w, f32[6,8,128]{2,1,0:T(8,128)S(1)} %get-tuple-element.34.wl, ...), custom_call_target="tpu_custom_call" | custom-call | tf_op jit(solution)/shard_map/pallas_call | solution.py:625
  40.2 3.9 %collective-permute-start.7 = (f32[424,128]{1,0:T(8,128)S(1)}, f32[424,128]{1,0:T(8,128)S(1)}, u32[]{:S(2)}, u32[]{:S(2)}) collective-permute-start(f32[424,128]{1,0:T(8,128)S(1)} %get-tuple-element.42), channel_id=1, source_target_pairs={{1,2},{2,1},{5,6},{6,5},{9,10},{10,9},{13,14},{14,13},{17,18},{18,... | collective-permute-start | bytes 651272 | tf_op jit(solution)/shard_map/ppermute | solution.py:588
  44.1 2.3 %collective-permute-start.8 = (f32[424,128]{1,0:T(8,128)S(1)}, f32[424,128]{1,0:T(8,128)S(1)}, u32[]{:S(2)}, u32[]{:S(2)}) collective-permute-start(f32[424,128]{1,0:T(8,128)S(1)} %get-tuple-element.43), channel_id=1, source_target_pairs={{0,1},{2,3},{1,0},{3,2},{4,5},{6,7},{5,4},{7,6},{8,9},{10,11},{9,8... | collective-permute-start | bytes 651272 | tf_op jit(solution)/shard_map/ppermute | solution.py:588
  46.4 1.2 %shard_map.53 = (f32[3,3,3,3,3,2,4,64]{7,6,5,4,3,2,1,0:T(4,128)}, f32[8,128]{1,0:T(8,128)S(1)}) custom-call(f32[9,27,16,128]{3,2,1,0:T(8,128)S(1)} %get-tuple-element.37.whole), custom_call_target="tpu_custom_call" | custom-call | flops 500000 | bytes 3000000 | tf_op jit(solution)/shard_map/pallas_call | solution.py:633
  47.6 1.2 %collective-permute-done.7.from_other = f32[424,128]{1,0:T(8,128)S(1)} collective-permute-done((f32[424,128]{1,0:T(8,128)S(1)}, f32[424,128]{1,0:T(8,128)S(1)}, u32[]{:S(2)}, u32[]{:S(2)}) %collective-permute-start.7) | collective-permute-done | bytes 217120 | tf_op jit(solution)/shard_map/ppermute | solution.py:588
  48.9 0.8 %shard_map.54 = (f32[3,16,128]{2,1,0:T(8,128)S(1)}, f32[3,16,128]{2,1,0:T(8,128)S(1)}, f32[3,16,128]{2,1,0:T(8,128)S(1)}, f32[24,128]{1,0:T(8,128)S(1)}, f32[24,128]{1,0:T(8,128)S(1)}) custom-call(f32[9,27,16,128]{3,2,1,0:T(8,128)S(1)} %get-tuple-element.37.whole, f32[3,16,128]{2,1,0:T(8,128)S(1)} %get-tuple-element.39.q, ...), custom_call_target="tpu_custom_call" | custom-call | tf_op jit(solution)/shard_map/pallas_call | solution.py:647
  49.7 3.9 %collective-permute-start.9 = (f32[24,128]{1,0:T(8,128)S(1)}, f32[24,128]{1,0:T(8,128)S(1)}, u32[]{:S(2)}, u32[]{:S(2)}) collective-permute-start(f32[24,128]{1,0:T(8,128)S(1)} %get-tuple-element.48), channel_id=1, source_target_pairs={{1,2},{2,1},{5,6},{6,5},{9,10},{10,9},{13,14},{14,13},{17,18},{18,... | collective-permute-start | bytes 36872 | tf_op jit(solution)/shard_map/ppermute | solution.py:588
  53.6 1.9 %collective-permute-start.10 = (f32[24,128]{1,0:T(8,128)S(1)}, f32[24,128]{1,0:T(8,128)S(1)}, u32[]{:S(2)}, u32[]{:S(2)}) collective-permute-start(f32[24,128]{1,0:T(8,128)S(1)} %get-tuple-element.49), channel_id=1, source_target_pairs={{0,1},{2,3},{1,0},{3,2},{4,5},{6,7},{5,4},{7,6},{8,9},{10,11},{9,8... | collective-permute-start | bytes 36872 | tf_op jit(solution)/shard_map/ppermute | solution.py:588
  55.5 0.7 %collective-permute-done.9.from_other = f32[24,128]{1,0:T(8,128)S(1)} collective-permute-done((f32[24,128]{1,0:T(8,128)S(1)}, f32[24,128]{1,0:T(8,128)S(1)}, u32[]{:S(2)}, u32[]{:S(2)}) %collective-permute-start.9) | collective-permute-done | bytes 12320 | tf_op jit(solution)/shard_map/ppermute | solution.py:588
  56.2 0.4 collective-permute-done.10.from_pair
  56.6 0.9 %shard_map.55 = f32[3,2,4,64]{3,2,1,0:T(4,128)} custom-call(f32[9,27,16,128]{3,2,1,0:T(8,128)S(1)} %get-tuple-element.37.whole, f32[3,16,128]{2,1,0:T(8,128)S(1)} %get-tuple-element.45.q, f32[3,16,128]{2,1,0:T(8,128)S(1)} %get-tuple-element.46.d, f32[3,16,128]{2,1,0:T(8,128)S(1)} %get-tuple-element.41.inverse, f32[3,16,128]{2,1,0:T(8,128)S(1)} %get-tuple-element.47.x, ...), custom_call_target="tpu_custom_call" | custom-call | tf_op jit(solution)/shard_map/pallas_call | solution.py:656
  (4 shorter events, 0.0 us)
Async XLA Ops:
  5.4 18.4 %collective-permute-start.4 = (f32[56,8,128]{2,1,0:T(8,128)S(1)}, f32[56,8,128]{2,1,0:T(8,128)S(1)}, u32[]{:S(2)}, u32[]{:S(2)}) collective-permute-start(f32[56,8,128]{2,1,0:T(8,128)S(1)} %get-tuple-element.30), channel_id=1, source_target_pairs={{0,1},{1,2},{2,3},{4,5},{5,6},{6,7},{8,9},{9,10},{10,11},{12,13},{... | collective-permute-start | bytes 688136 | tf_op jit(solution)/shard_map/ppermute | solution.py:582
  10.7 9.5 %collective-permute-start = (f32[10,8,128]{2,1,0:T(8,128)S(1)}, f32[10,8,128]{2,1,0:T(8,128)S(1)}, u32[]{:S(2)}, u32[]{:S(2)}) collective-permute-start(f32[10,8,128]{2,1,0:T(8,128)S(1)} %get-tuple-element.26), channel_id=1, source_target_pairs={{32,0},{64,32},{96,64},{128,96},{160,128},{192,160},{224,192},{256... | collective-permute-start | bytes 122888 | tf_op jit(solution)/shard_map/ppermute | solution.py:582
  12.6 7.5 %collective-permute-start.1 = (f32[10,8,128]{2,1,0:T(8,128)S(1)}, f32[10,8,128]{2,1,0:T(8,128)S(1)}, u32[]{:S(2)}, u32[]{:S(2)}) collective-permute-start(f32[10,8,128]{2,1,0:T(8,128)S(1)} %get-tuple-element.27), channel_id=1, source_target_pairs={{32,1},{33,2},{34,3},{64,33},{65,34},{66,35},{96,65},{97,66},{98,6... | collective-permute-start | bytes 122888 | tf_op jit(solution)/shard_map/ppermute | solution.py:582
  14.5 7.4 %collective-permute-start.2 = (f32[10,8,128]{2,1,0:T(8,128)S(1)}, f32[10,8,128]{2,1,0:T(8,128)S(1)}, u32[]{:S(2)}, u32[]{:S(2)}) collective-permute-start(f32[10,8,128]{2,1,0:T(8,128)S(1)} %get-tuple-element.28), channel_id=1, source_target_pairs={{0,33},{1,34},{2,35},{32,65},{33,66},{34,67},{64,97},{65,98},{66,9... | collective-permute-start | bytes 122888 | tf_op jit(solution)/shard_map/ppermute | solution.py:582
  17.0 6.9 %collective-permute-start.3 = (f32[10,8,128]{2,1,0:T(8,128)S(1)}, f32[10,8,128]{2,1,0:T(8,128)S(1)}, u32[]{:S(2)}, u32[]{:S(2)}) collective-permute-start(f32[10,8,128]{2,1,0:T(8,128)S(1)} %get-tuple-element.29), channel_id=1, source_target_pairs={{0,32},{32,64},{64,96},{96,128},{128,160},{160,192},{192,224},{224... | collective-permute-start | bytes 122888 | tf_op jit(solution)/shard_map/ppermute | solution.py:582
  25.4 13.6 %collective-permute-start.5 = (f32[93,8,128]{2,1,0:T(8,128)S(1)}, f32[93,8,128]{2,1,0:T(8,128)S(1)}, u32[]{:S(2)}, u32[]{:S(2)}) collective-permute-start(f32[93,8,128]{2,1,0:T(8,128)S(1)} %get-tuple-element.35), channel_id=1, source_target_pairs={{0,4},{4,8},{8,12},{12,16},{16,20},{20,24},{24,28},{1,5},{5,9},{9,... | collective-permute-start | bytes 1142792 | tf_op jit(solution)/shard_map/ppermute | solution.py:582
  29.8 9.2 %collective-permute-start.6 = (f32[75,8,128]{2,1,0:T(8,128)S(1)}, f32[75,8,128]{2,1,0:T(8,128)S(1)}, u32[]{:S(2)}, u32[]{:S(2)}) collective-permute-start(f32[75,8,128]{2,1,0:T(8,128)S(1)} %get-tuple-element.36), channel_id=1, source_target_pairs={{4,0},{8,4},{12,8},{16,12},{20,16},{24,20},{28,24},{5,1},{9,5},{13... | collective-permute-start | bytes 921608 | tf_op jit(solution)/shard_map/ppermute | solution.py:582
  40.2 8.7 %collective-permute-start.7 = (f32[424,128]{1,0:T(8,128)S(1)}, f32[424,128]{1,0:T(8,128)S(1)}, u32[]{:S(2)}, u32[]{:S(2)}) collective-permute-start(f32[424,128]{1,0:T(8,128)S(1)} %get-tuple-element.42), channel_id=1, source_target_pairs={{1,2},{2,1},{5,6},{6,5},{9,10},{10,9},{13,14},{14,13},{17,18},{18,... | collective-permute-start | bytes 651272 | tf_op jit(solution)/shard_map/ppermute | solution.py:588
  44.1 4.8 %collective-permute-start.8 = (f32[424,128]{1,0:T(8,128)S(1)}, f32[424,128]{1,0:T(8,128)S(1)}, u32[]{:S(2)}, u32[]{:S(2)}) collective-permute-start(f32[424,128]{1,0:T(8,128)S(1)} %get-tuple-element.43), channel_id=1, source_target_pairs={{0,1},{2,3},{1,0},{3,2},{4,5},{6,7},{5,4},{7,6},{8,9},{10,11},{9,8... | collective-permute-start | bytes 651272 | tf_op jit(solution)/shard_map/ppermute | solution.py:588
  49.7 6.5 %collective-permute-start.9 = (f32[24,128]{1,0:T(8,128)S(1)}, f32[24,128]{1,0:T(8,128)S(1)}, u32[]{:S(2)}, u32[]{:S(2)}) collective-permute-start(f32[24,128]{1,0:T(8,128)S(1)} %get-tuple-element.48), channel_id=1, source_target_pairs={{1,2},{2,1},{5,6},{6,5},{9,10},{10,9},{13,14},{14,13},{17,18},{18,... | collective-permute-start | bytes 36872 | tf_op jit(solution)/shard_map/ppermute | solution.py:588
  53.6 3.1 %collective-permute-start.10 = (f32[24,128]{1,0:T(8,128)S(1)}, f32[24,128]{1,0:T(8,128)S(1)}, u32[]{:S(2)}, u32[]{:S(2)}) collective-permute-start(f32[24,128]{1,0:T(8,128)S(1)} %get-tuple-element.49), channel_id=1, source_target_pairs={{0,1},{2,3},{1,0},{3,2},{4,5},{6,7},{5,4},{7,6},{8,9},{10,11},{9,8... | collective-permute-start | bytes 36872 | tf_op jit(solution)/shard_map/ppermute | solution.py:588

commit v6 on v5

--- a/solution.py
+++ b/solution.py
@@ -408,7 +408,7 @@
     return one, two, jnp.concatenate(parts[: n // 8], axis=0)
 
 
-def rows_kernel(w, wl, from_low, from_high, whole, q, d, inverse, to_other, to_pair, total, turned, near):
+def rows_kernel(from_high, from_low, w, wl, whole, q, d, inverse, to_other, to_pair, total, turned, near):
     row = rows_of()
     ghosts = jnp.logical_or(row == 4, row == 5)
     total[...] = jnp.zeros_like(total)
@@ -614,7 +614,7 @@
         planes_kernel,
         in_specs=[VMEM] * 7,
         out_specs=[VMEM] * 4,
-        out_shape=[w_shape, wl_shape, shape(9 * packed_size(UPS) + packed_size(3), 8, 128), shape(9 * packed_size(DOWNS) + packed_size(3), 8, 128)],
+        out_shape=[w_shape, wl_shape, shape(9 * packed_size(UPS) + packed_size(3), 8, 128), shape(9 * packed_size(UPS) + packed_size(3), 8, 128)],
         scratch_shapes=[pltpu.VMEM((3, 8, 128), jnp.float32)],
         compiler_params=LIMIT,
     )(from_right, plane_right, plane_left, from_left, plane, w, wl)
@@ -629,7 +629,7 @@
         out_shape=[whole_shape, vector, shape(3, 24, 128), vector] + [shape(EDGES + piece_rows(24), 128)] * 2,
         scratch_shapes=[pltpu.VMEM((3, 16, 128), jnp.float32), pltpu.VMEM((8, 128), jnp.float32), near],
         compiler_params=LIMIT,
-    )(w, wl, from_low, from_high)
+    )(from_high, from_low, w, wl)
     operator, written = pl.pallas_call(
         operator_kernel,
         in_specs=[VMEM],

time: 58 us -> 56.8 us (0.979)
  the two profiles are of different devices: /device:TPU:281 before, /device:TPU:289 now
where the time goes in v6:
time: 56.8 us; the launch traced here: 56.3 us
  starting transfers between devices  31.2 us (55%)
  waiting for transfers between devices  14 us (25%)
  Pallas kernels  10.4 us (18%)
  between operations  0.77 us (1%)
    ppermute x7, starting transfers between devices, along(): return lax.ppermute(block, axes, route)  19.9 us
    ppermute x7, waiting for transfers between devices, along(): return lax.ppermute(block, axes, route)  11.2 us
    ppermute x4, starting transfers between devices, exchanged(): return lax.ppermute(block, axis, pairs + [(j, i) for i, j in pairs])  11.2 us
    pallas_call x1, Pallas kernels, shards(): pl.pallas_call(coarsen_kernel, in_specs=[HBM] * 3, out_specs=[VMEM] * 7,...  4.81 us
    ppermute x4, waiting for transfers between devices, exchanged(): return lax.ppermute(block, axis, pairs + [(j, i) for i, j in pairs])  2.75 us
    pallas_call x1, Pallas kernels, shards(): pl.pallas_call(planes_kernel, in_specs=[VMEM] * 7, out_specs=[VMEM] * 4,...  1.54 us
    pallas_call x1, Pallas kernels, shards(): pl.pallas_call(operator_kernel, in_specs=[VMEM], out_specs=[VMEM] * 2, ou...  1.23 us
    pallas_call x1, Pallas kernels, shards(): pl.pallas_call(rows_kernel, in_specs=[VMEM] * 4, out_specs=[VMEM] * 6, ou...  1.18 us
  transfers between devices with their start and end apart: 11, of which 6 were waited for; matrix products, arithmetic and copies ran while one was open for 0% of the time, Pallas kernels for 2%

profile of v6, /device:TPU:289, one launch (start us, length us, event | category | flops | bytes accessed | tf_op | source)
XLA Modules:
  0.0 56.3 jit_solution(2195382785700169867)
XLA Ops:
  0.6 4.8 %shard_map.50 = (f32[9,32,8,128]{3,2,1,0:T(8,128)S(1)}, f32[6,8,128]{2,1,0:T(8,128)S(1)}, f32[10,8,128]{2,1,0:T(8,128)S(1)}, f32[10,8,128]{2,1,0:T(8,128)S(1)}, ...) custom-call(f32[3,3,3,3,3,4,8,128]{7,6,5,4,3,2,1,0:T(8,128)} %blocks_in.1, ...), custom_call_target="tpu_custom_call" | custom-call | tf_op jit(solution)/shard_map/pallas_call | solution.py:594
  5.4 5.2 %collective-permute-start.4 = (f32[56,8,128]{2,1,0:T(8,128)S(1)}, f32[56,8,128]{2,1,0:T(8,128)S(1)}, u32[]{:S(2)}, u32[]{:S(2)}) collective-permute-start(f32[56,8,128]{2,1,0:T(8,128)S(1)} %get-tuple-element.30), channel_id=1, source_target_pairs={{0,1},{1,2},{2,3},{4,5},{5,6},{6,7},{8,9},{9,10},{10,11},{12,13},{... | collective-permute-start | bytes 688136 | tf_op jit(solution)/shard_map/ppermute | solution.py:582
  10.7 1.9 %collective-permute-start = (f32[10,8,128]{2,1,0:T(8,128)S(1)}, f32[10,8,128]{2,1,0:T(8,128)S(1)}, u32[]{:S(2)}, u32[]{:S(2)}) collective-permute-start(f32[10,8,128]{2,1,0:T(8,128)S(1)} %get-tuple-element.26), channel_id=1, source_target_pairs={{32,0},{64,32},{96,64},{128,96},{160,128},{192,160},{224,192},{256... | collective-permute-start | bytes 122888 | tf_op jit(solution)/shard_map/ppermute | solution.py:582
  12.6 1.9 %collective-permute-start.1 = (f32[10,8,128]{2,1,0:T(8,128)S(1)}, f32[10,8,128]{2,1,0:T(8,128)S(1)}, u32[]{:S(2)}, u32[]{:S(2)}) collective-permute-start(f32[10,8,128]{2,1,0:T(8,128)S(1)} %get-tuple-element.27), channel_id=1, source_target_pairs={{32,1},{33,2},{34,3},{64,33},{65,34},{66,35},{96,65},{97,66},{98,6... | collective-permute-start | bytes 122888 | tf_op jit(solution)/shard_map/ppermute | solution.py:582
  14.5 2.5 %collective-permute-start.2 = (f32[10,8,128]{2,1,0:T(8,128)S(1)}, f32[10,8,128]{2,1,0:T(8,128)S(1)}, u32[]{:S(2)}, u32[]{:S(2)}) collective-permute-start(f32[10,8,128]{2,1,0:T(8,128)S(1)} %get-tuple-element.28), channel_id=1, source_target_pairs={{0,33},{1,34},{2,35},{32,65},{33,66},{34,67},{64,97},{65,98},{66,9... | collective-permute-start | bytes 122888 | tf_op jit(solution)/shard_map/ppermute | solution.py:582
  17.0 3.1 %collective-permute-start.3 = (f32[10,8,128]{2,1,0:T(8,128)S(1)}, f32[10,8,128]{2,1,0:T(8,128)S(1)}, u32[]{:S(2)}, u32[]{:S(2)}) collective-permute-start(f32[10,8,128]{2,1,0:T(8,128)S(1)} %get-tuple-element.29), channel_id=1, source_target_pairs={{0,32},{32,64},{64,96},{96,128},{128,160},{160,192},{192,224},{224... | collective-permute-start | bytes 122888 | tf_op jit(solution)/shard_map/ppermute | solution.py:582
  20.1 0.0 collective-permute-done.from_right
  20.2 1.8 %collective-permute-done.2.plane_left = f32[10,8,128]{2,1,0:T(8,128)S(1)} collective-permute-done((f32[10,8,128]{2,1,0:T(8,128)S(1)}, f32[10,8,128]{2,1,0:T(8,128)S(1)}, u32[]{:S(2)}, u32[]{:S(2)}) %collective-permute-start.2) | collective-permute-done | bytes 40992 | tf_op jit(solution)/shard_map/ppermute | solution.py:582
  22.0 1.9 %collective-permute-done.3.from_left = f32[10,8,128]{2,1,0:T(8,128)S(1)} collective-permute-done((f32[10,8,128]{2,1,0:T(8,128)S(1)}, f32[10,8,128]{2,1,0:T(8,128)S(1)}, u32[]{:S(2)}, u32[]{:S(2)}) %collective-permute-start.3) | collective-permute-done | bytes 40992 | tf_op jit(solution)/shard_map/ppermute | solution.py:582
  23.9 1.5 %shard_map.51 = (f32[9,32,8,128]{3,2,1,0:T(8,128)S(1)}, f32[6,8,128]{2,1,0:T(8,128)S(1)}, f32[93,8,128]{2,1,0:T(8,128)S(1)}, f32[93,8,128]{2,1,0:T(8,128)S(1)}) custom-call(f32[10,8,128]{2,1,0:T(8,128)S(1)} %collective-permute-done.from_right, f32[10,8,128]{2,1,0:T(8,128)S(1)} %collective-permute-done.1.plane_right, ...), custom_call_target="tpu_custom_call" | custom-call | tf_op jit(solution)/shard_map/pallas_call | solution.py:613
  25.4 2.1 %collective-permute-start.5 = (f32[93,8,128]{2,1,0:T(8,128)S(1)}, f32[93,8,128]{2,1,0:T(8,128)S(1)}, u32[]{:S(2)}, u32[]{:S(2)}) collective-permute-start(f32[93,8,128]{2,1,0:T(8,128)S(1)} %get-tuple-element.33), channel_id=1, source_target_pairs={{4,0},{8,4},{12,8},{16,12},{20,16},{24,20},{28,24},{5,1},{9,5},{13... | collective-permute-start | bytes 1142792 | tf_op jit(solution)/shard_map/ppermute | solution.py:582
  27.5 3.2 %collective-permute-start.6 = (f32[93,8,128]{2,1,0:T(8,128)S(1)}, f32[93,8,128]{2,1,0:T(8,128)S(1)}, u32[]{:S(2)}, u32[]{:S(2)}) collective-permute-start(f32[93,8,128]{2,1,0:T(8,128)S(1)} %get-tuple-element.34), channel_id=1, source_target_pairs={{0,4},{4,8},{8,12},{12,16},{16,20},{20,24},{24,28},{1,5},{5,9},{9,... | collective-permute-start | bytes 1142792 | tf_op jit(solution)/shard_map/ppermute | solution.py:582
  30.7 4.5 %collective-permute-done.5.from_high = f32[93,8,128]{2,1,0:T(8,128)S(1)} collective-permute-done((f32[93,8,128]{2,1,0:T(8,128)S(1)}, f32[93,8,128]{2,1,0:T(8,128)S(1)}, u32[]{:S(2)}, u32[]{:S(2)}) %collective-permute-start.5) | collective-permute-done | bytes 380960 | tf_op jit(solution)/shard_map/ppermute | solution.py:582
  35.2 3.0 %collective-permute-done.6.from_low = f32[93,8,128]{2,1,0:T(8,128)S(1)} collective-permute-done((f32[93,8,128]{2,1,0:T(8,128)S(1)}, f32[93,8,128]{2,1,0:T(8,128)S(1)}, u32[]{:S(2)}, u32[]{:S(2)}) %collective-permute-start.6) | collective-permute-done | bytes 380960 | tf_op jit(solution)/shard_map/ppermute | solution.py:582
  38.2 1.2 %shard_map.52 = (f32[9,27,16,128]{3,2,1,0:T(8,128)S(1)}, f32[3,16,128]{2,1,0:T(8,128)S(1)}, f32[3,24,128]{2,1,0:T(8,128)S(1)}, f32[3,16,128]{2,1,0:T(8,128)S(1)}...) custom-call(f32[93,8,128]{2,1,0:T(8,128)S(1)} %collective-permute-done.5.from_high, ...), custom_call_target="tpu_custom_call" | custom-call | tf_op jit(solution)/shard_map/pallas_call | solution.py:625
  39.4 3.1 %collective-permute-start.7 = (f32[424,128]{1,0:T(8,128)S(1)}, f32[424,128]{1,0:T(8,128)S(1)}, u32[]{:S(2)}, u32[]{:S(2)}) collective-permute-start(f32[424,128]{1,0:T(8,128)S(1)} %get-tuple-element.42), channel_id=1, source_target_pairs={{1,2},{2,1},{5,6},{6,5},{9,10},{10,9},{13,14},{14,13},{17,18},{18,... | collective-permute-start | bytes 651272 | tf_op jit(solution)/shard_map/ppermute | solution.py:588
  42.5 3.1 %collective-permute-start.8 = (f32[424,128]{1,0:T(8,128)S(1)}, f32[424,128]{1,0:T(8,128)S(1)}, u32[]{:S(2)}, u32[]{:S(2)}) collective-permute-start(f32[424,128]{1,0:T(8,128)S(1)} %get-tuple-element.43), channel_id=1, source_target_pairs={{0,1},{2,3},{1,0},{3,2},{4,5},{6,7},{5,4},{7,6},{8,9},{10,11},{9,8... | collective-permute-start | bytes 651272 | tf_op jit(solution)/shard_map/ppermute | solution.py:588
  45.7 1.2 %shard_map.53 = (f32[3,3,3,3,3,2,4,64]{7,6,5,4,3,2,1,0:T(4,128)}, f32[8,128]{1,0:T(8,128)S(1)}) custom-call(f32[9,27,16,128]{3,2,1,0:T(8,128)S(1)} %get-tuple-element.37.whole), custom_call_target="tpu_custom_call" | custom-call | flops 500000 | bytes 3000000 | tf_op jit(solution)/shard_map/pallas_call | solution.py:633
  46.9 1.2 %collective-permute-done.7.from_other = f32[424,128]{1,0:T(8,128)S(1)} collective-permute-done((f32[424,128]{1,0:T(8,128)S(1)}, f32[424,128]{1,0:T(8,128)S(1)}, u32[]{:S(2)}, u32[]{:S(2)}) %collective-permute-start.7) | collective-permute-done | bytes 217120 | tf_op jit(solution)/shard_map/ppermute | solution.py:588
  48.1 0.8 %shard_map.54 = (f32[3,16,128]{2,1,0:T(8,128)S(1)}, f32[3,16,128]{2,1,0:T(8,128)S(1)}, f32[3,16,128]{2,1,0:T(8,128)S(1)}, f32[24,128]{1,0:T(8,128)S(1)}, f32[24,128]{1,0:T(8,128)S(1)}) custom-call(f32[9,27,16,128]{3,2,1,0:T(8,128)S(1)} %get-tuple-element.37.whole, f32[3,16,128]{2,1,0:T(8,128)S(1)} %get-tuple-element.39.q, ...), custom_call_target="tpu_custom_call" | custom-call | tf_op jit(solution)/shard_map/pallas_call | solution.py:647
  48.9 3.1 %collective-permute-start.9 = (f32[24,128]{1,0:T(8,128)S(1)}, f32[24,128]{1,0:T(8,128)S(1)}, u32[]{:S(2)}, u32[]{:S(2)}) collective-permute-start(f32[24,128]{1,0:T(8,128)S(1)} %get-tuple-element.48), channel_id=1, source_target_pairs={{1,2},{2,1},{5,6},{6,5},{9,10},{10,9},{13,14},{14,13},{17,18},{18,... | collective-permute-start | bytes 36872 | tf_op jit(solution)/shard_map/ppermute | solution.py:588
  52.0 1.9 %collective-permute-start.10 = (f32[24,128]{1,0:T(8,128)S(1)}, f32[24,128]{1,0:T(8,128)S(1)}, u32[]{:S(2)}, u32[]{:S(2)}) collective-permute-start(f32[24,128]{1,0:T(8,128)S(1)} %get-tuple-element.49), channel_id=1, source_target_pairs={{0,1},{2,3},{1,0},{3,2},{4,5},{6,7},{5,4},{7,6},{8,9},{10,11},{9,8... | collective-permute-start | bytes 36872 | tf_op jit(solution)/shard_map/ppermute | solution.py:588
  53.9 1.5 %collective-permute-done.9.from_other = f32[24,128]{1,0:T(8,128)S(1)} collective-permute-done((f32[24,128]{1,0:T(8,128)S(1)}, f32[24,128]{1,0:T(8,128)S(1)}, u32[]{:S(2)}, u32[]{:S(2)}) %collective-permute-start.9) | collective-permute-done | bytes 12320 | tf_op jit(solution)/shard_map/ppermute | solution.py:588
  55.4 0.9 %shard_map.55 = f32[3,2,4,64]{3,2,1,0:T(4,128)} custom-call(f32[9,27,16,128]{3,2,1,0:T(8,128)S(1)} %get-tuple-element.37.whole, f32[3,16,128]{2,1,0:T(8,128)S(1)} %get-tuple-element.45.q, f32[3,16,128]{2,1,0:T(8,128)S(1)} %get-tuple-element.46.d, f32[3,16,128]{2,1,0:T(8,128)S(1)} %get-tuple-element.41.inverse, f32[3,16,128]{2,1,0:T(8,128)S(1)} %get-tuple-element.47.x, ...), custom_call_target="tpu_custom_call" | custom-call | tf_op jit(solution)/shard_map/pallas_call | solution.py:656
  (4 shorter events, 0.0 us)
Async XLA Ops:
  5.4 18.4 %collective-permute-start.4 = (f32[56,8,128]{2,1,0:T(8,128)S(1)}, f32[56,8,128]{2,1,0:T(8,128)S(1)}, u32[]{:S(2)}, u32[]{:S(2)}) collective-permute-start(f32[56,8,128]{2,1,0:T(8,128)S(1)} %get-tuple-element.30), channel_id=1, source_target_pairs={{0,1},{1,2},{2,3},{4,5},{5,6},{6,7},{8,9},{9,10},{10,11},{12,13},{... | collective-permute-start | bytes 688136 | tf_op jit(solution)/shard_map/ppermute | solution.py:582
  10.7 9.5 %collective-permute-start = (f32[10,8,128]{2,1,0:T(8,128)S(1)}, f32[10,8,128]{2,1,0:T(8,128)S(1)}, u32[]{:S(2)}, u32[]{:S(2)}) collective-permute-start(f32[10,8,128]{2,1,0:T(8,128)S(1)} %get-tuple-element.26), channel_id=1, source_target_pairs={{32,0},{64,32},{96,64},{128,96},{160,128},{192,160},{224,192},{256... | collective-permute-start | bytes 122888 | tf_op jit(solution)/shard_map/ppermute | solution.py:582
  12.6 7.5 %collective-permute-start.1 = (f32[10,8,128]{2,1,0:T(8,128)S(1)}, f32[10,8,128]{2,1,0:T(8,128)S(1)}, u32[]{:S(2)}, u32[]{:S(2)}) collective-permute-start(f32[10,8,128]{2,1,0:T(8,128)S(1)} %get-tuple-element.27), channel_id=1, source_target_pairs={{32,1},{33,2},{34,3},{64,33},{65,34},{66,35},{96,65},{97,66},{98,6... | collective-permute-start | bytes 122888 | tf_op jit(solution)/shard_map/ppermute | solution.py:582
  14.5 7.4 %collective-permute-start.2 = (f32[10,8,128]{2,1,0:T(8,128)S(1)}, f32[10,8,128]{2,1,0:T(8,128)S(1)}, u32[]{:S(2)}, u32[]{:S(2)}) collective-permute-start(f32[10,8,128]{2,1,0:T(8,128)S(1)} %get-tuple-element.28), channel_id=1, source_target_pairs={{0,33},{1,34},{2,35},{32,65},{33,66},{34,67},{64,97},{65,98},{66,9... | collective-permute-start | bytes 122888 | tf_op jit(solution)/shard_map/ppermute | solution.py:582
  17.0 6.9 %collective-permute-start.3 = (f32[10,8,128]{2,1,0:T(8,128)S(1)}, f32[10,8,128]{2,1,0:T(8,128)S(1)}, u32[]{:S(2)}, u32[]{:S(2)}) collective-permute-start(f32[10,8,128]{2,1,0:T(8,128)S(1)} %get-tuple-element.29), channel_id=1, source_target_pairs={{0,32},{32,64},{64,96},{96,128},{128,160},{160,192},{192,224},{224... | collective-permute-start | bytes 122888 | tf_op jit(solution)/shard_map/ppermute | solution.py:582
  25.4 9.8 %collective-permute-start.5 = (f32[93,8,128]{2,1,0:T(8,128)S(1)}, f32[93,8,128]{2,1,0:T(8,128)S(1)}, u32[]{:S(2)}, u32[]{:S(2)}) collective-permute-start(f32[93,8,128]{2,1,0:T(8,128)S(1)} %get-tuple-element.33), channel_id=1, source_target_pairs={{4,0},{8,4},{12,8},{16,12},{20,16},{24,20},{28,24},{5,1},{9,5},{13... | collective-permute-start | bytes 1142792 | tf_op jit(solution)/shard_map/ppermute | solution.py:582
  27.5 10.7 %collective-permute-start.6 = (f32[93,8,128]{2,1,0:T(8,128)S(1)}, f32[93,8,128]{2,1,0:T(8,128)S(1)}, u32[]{:S(2)}, u32[]{:S(2)}) collective-permute-start(f32[93,8,128]{2,1,0:T(8,128)S(1)} %get-tuple-element.34), channel_id=1, source_target_pairs={{0,4},{4,8},{8,12},{12,16},{16,20},{20,24},{24,28},{1,5},{5,9},{9,... | collective-permute-start | bytes 1142792 | tf_op jit(solution)/shard_map/ppermute | solution.py:582
  39.4 8.7 %collective-permute-start.7 = (f32[424,128]{1,0:T(8,128)S(1)}, f32[424,128]{1,0:T(8,128)S(1)}, u32[]{:S(2)}, u32[]{:S(2)}) collective-permute-start(f32[424,128]{1,0:T(8,128)S(1)} %get-tuple-element.42), channel_id=1, source_target_pairs={{1,2},{2,1},{5,6},{6,5},{9,10},{10,9},{13,14},{14,13},{17,18},{18,... | collective-permute-start | bytes 651272 | tf_op jit(solution)/shard_map/ppermute | solution.py:588
  42.5 5.6 %collective-permute-start.8 = (f32[424,128]{1,0:T(8,128)S(1)}, f32[424,128]{1,0:T(8,128)S(1)}, u32[]{:S(2)}, u32[]{:S(2)}) collective-permute-start(f32[424,128]{1,0:T(8,128)S(1)} %get-tuple-element.43), channel_id=1, source_target_pairs={{0,1},{2,3},{1,0},{3,2},{4,5},{6,7},{5,4},{7,6},{8,9},{10,11},{9,8... | collective-permute-start | bytes 651272 | tf_op jit(solution)/shard_map/ppermute | solution.py:588
  48.9 6.5 %collective-permute-start.9 = (f32[24,128]{1,0:T(8,128)S(1)}, f32[24,128]{1,0:T(8,128)S(1)}, u32[]{:S(2)}, u32[]{:S(2)}) collective-permute-start(f32[24,128]{1,0:T(8,128)S(1)} %get-tuple-element.48), channel_id=1, source_target_pairs={{1,2},{2,1},{5,6},{6,5},{9,10},{10,9},{13,14},{14,13},{17,18},{18,... | collective-permute-start | bytes 36872 | tf_op jit(solution)/shard_map/ppermute | solution.py:588
  52.0 3.4 %collective-permute-start.10 = (f32[24,128]{1,0:T(8,128)S(1)}, f32[24,128]{1,0:T(8,128)S(1)}, u32[]{:S(2)}, u32[]{:S(2)}) collective-permute-start(f32[24,128]{1,0:T(8,128)S(1)} %get-tuple-element.49), channel_id=1, source_target_pairs={{0,1},{2,3},{1,0},{3,2},{4,5},{6,7},{5,4},{7,6},{8,9},{10,11},{9,8... | collective-permute-start | bytes 36872 | tf_op jit(solution)/shard_map/ppermute | solution.py:588

commit v7 on v6

--- a/solution.py
+++ b/solution.py
@@ -298,7 +298,7 @@
     lax.fori_loop(0, 9, body, 0, unroll=9)
 
 
-def planes_kernel(from_right, plane_right, plane_left, from_left, plane, w, wl, w_out, wl_out, up, down, total):
+def planes_kernel(plane_right, from_right, plane_left, from_left, plane, w, wl, w_out, wl_out, up, down, total):
     row = rows_of()
     even = row % 2 == 0
     total[...] = jnp.zeros_like(total)
@@ -617,7 +617,7 @@
         out_shape=[w_shape, wl_shape, shape(9 * packed_size(UPS) + packed_size(3), 8, 128), shape(9 * packed_size(UPS) + packed_size(3), 8, 128)],
         scratch_shapes=[pltpu.VMEM((3, 8, 128), jnp.float32)],
         compiler_params=LIMIT,
-    )(from_right, plane_right, plane_left, from_left, plane, w, wl)
+    )(plane_right, from_right, plane_left, from_left, plane, w, wl)
     from_high = along(down, ("gy",), (-1,))
     from_low = along(up, ("gy",), (1,))
     whole_shape, vector = shape(9, 27, 16, 128), shape(3, 16, 128)

time: 56.8 us -> 56.9 us (level)
  no operation moved by 1% of the time
where the time goes in v7:
time: 56.9 us; the launch traced here: 56.3 us
  starting transfers between devices  31.2 us (55%)
  waiting for transfers between devices  14 us (25%)
  Pallas kernels  10.4 us (18%)
  between operations  0.77 us (1%)
    ppermute x7, starting transfers between devices, along(): return lax.ppermute(block, axes, route)  19.9 us
    ppermute x7, waiting for transfers between devices, along(): return lax.ppermute(block, axes, route)  11.2 us
    ppermute x4, starting transfers between devices, exchanged(): return lax.ppermute(block, axis, pairs + [(j, i) for i, j in pairs])  11.2 us
    pallas_call x1, Pallas kernels, shards(): pl.pallas_call(coarsen_kernel, in_specs=[HBM] * 3, out_specs=[VMEM] * 7,...  4.81 us
    ppermute x4, waiting for transfers between devices, exchanged(): return lax.ppermute(block, axis, pairs + [(j, i) for i, j in pairs])  2.75 us
    pallas_call x1, Pallas kernels, shards(): pl.pallas_call(planes_kernel, in_specs=[VMEM] * 7, out_specs=[VMEM] * 4,...  1.54 us
    pallas_call x1, Pallas kernels, shards(): pl.pallas_call(operator_kernel, in_specs=[VMEM], out_specs=[VMEM] * 2, ou...  1.23 us
    pallas_call x1, Pallas kernels, shards(): pl.pallas_call(rows_kernel, in_specs=[VMEM] * 4, out_specs=[VMEM] * 6, ou...  1.18 us
  transfers between devices with their start and end apart: 11, of which 6 were waited for; matrix products, arithmetic and copies ran while one was open for 0% of the time, Pallas kernels for 2%

profile of v7, /device:TPU:289, one launch (start us, length us, event | category | flops | bytes accessed | tf_op | source)
XLA Modules:
  0.0 56.3 jit_solution(12838075874045034406)
XLA Ops:
  0.6 4.8 %shard_map.50 = (f32[9,32,8,128]{3,2,1,0:T(8,128)S(1)}, f32[6,8,128]{2,1,0:T(8,128)S(1)}, f32[10,8,128]{2,1,0:T(8,128)S(1)}, f32[10,8,128]{2,1,0:T(8,128)S(1)}, ...) custom-call(f32[3,3,3,3,3,4,8,128]{7,6,5,4,3,2,1,0:T(8,128)} %blocks_in.1, ...), custom_call_target="tpu_custom_call" | custom-call | tf_op jit(solution)/shard_map/pallas_call | solution.py:594
  5.4 5.2 %collective-permute-start.4 = (f32[56,8,128]{2,1,0:T(8,128)S(1)}, f32[56,8,128]{2,1,0:T(8,128)S(1)}, u32[]{:S(2)}, u32[]{:S(2)}) collective-permute-start(f32[56,8,128]{2,1,0:T(8,128)S(1)} %get-tuple-element.30), channel_id=1, source_target_pairs={{0,1},{1,2},{2,3},{4,5},{5,6},{6,7},{8,9},{9,10},{10,11},{12,13},{... | collective-permute-start | bytes 688136 | tf_op jit(solution)/shard_map/ppermute | solution.py:582
  10.7 1.9 %collective-permute-start = (f32[10,8,128]{2,1,0:T(8,128)S(1)}, f32[10,8,128]{2,1,0:T(8,128)S(1)}, u32[]{:S(2)}, u32[]{:S(2)}) collective-permute-start(f32[10,8,128]{2,1,0:T(8,128)S(1)} %get-tuple-element.26), channel_id=1, source_target_pairs={{32,1},{33,2},{34,3},{64,33},{65,34},{66,35},{96,65},{97,66},{98,6... | collective-permute-start | bytes 122888 | tf_op jit(solution)/shard_map/ppermute | solution.py:582
  12.6 1.9 %collective-permute-start.1 = (f32[10,8,128]{2,1,0:T(8,128)S(1)}, f32[10,8,128]{2,1,0:T(8,128)S(1)}, u32[]{:S(2)}, u32[]{:S(2)}) collective-permute-start(f32[10,8,128]{2,1,0:T(8,128)S(1)} %get-tuple-element.27), channel_id=1, source_target_pairs={{32,0},{64,32},{96,64},{128,96},{160,128},{192,160},{224,192},{256... | collective-permute-start | bytes 122888 | tf_op jit(solution)/shard_map/ppermute | solution.py:582
  14.5 2.5 %collective-permute-start.2 = (f32[10,8,128]{2,1,0:T(8,128)S(1)}, f32[10,8,128]{2,1,0:T(8,128)S(1)}, u32[]{:S(2)}, u32[]{:S(2)}) collective-permute-start(f32[10,8,128]{2,1,0:T(8,128)S(1)} %get-tuple-element.28), channel_id=1, source_target_pairs={{0,33},{1,34},{2,35},{32,65},{33,66},{34,67},{64,97},{65,98},{66,9... | collective-permute-start | bytes 122888 | tf_op jit(solution)/shard_map/ppermute | solution.py:582
  17.0 3.1 %collective-permute-start.3 = (f32[10,8,128]{2,1,0:T(8,128)S(1)}, f32[10,8,128]{2,1,0:T(8,128)S(1)}, u32[]{:S(2)}, u32[]{:S(2)}) collective-permute-start(f32[10,8,128]{2,1,0:T(8,128)S(1)} %get-tuple-element.29), channel_id=1, source_target_pairs={{0,32},{32,64},{64,96},{96,128},{128,160},{160,192},{192,224},{224... | collective-permute-start | bytes 122888 | tf_op jit(solution)/shard_map/ppermute | solution.py:582
  20.1 0.0 collective-permute-done.plane_right
  20.2 1.8 %collective-permute-done.2.plane_left = f32[10,8,128]{2,1,0:T(8,128)S(1)} collective-permute-done((f32[10,8,128]{2,1,0:T(8,128)S(1)}, f32[10,8,128]{2,1,0:T(8,128)S(1)}, u32[]{:S(2)}, u32[]{:S(2)}) %collective-permute-start.2) | collective-permute-done | bytes 40992 | tf_op jit(solution)/shard_map/ppermute | solution.py:582
  22.0 1.9 %collective-permute-done.3.from_left = f32[10,8,128]{2,1,0:T(8,128)S(1)} collective-permute-done((f32[10,8,128]{2,1,0:T(8,128)S(1)}, f32[10,8,128]{2,1,0:T(8,128)S(1)}, u32[]{:S(2)}, u32[]{:S(2)}) %collective-permute-start.3) | collective-permute-done | bytes 40992 | tf_op jit(solution)/shard_map/ppermute | solution.py:582
  23.9 1.5 %shard_map.51 = (f32[9,32,8,128]{3,2,1,0:T(8,128)S(1)}, f32[6,8,128]{2,1,0:T(8,128)S(1)}, f32[93,8,128]{2,1,0:T(8,128)S(1)}, f32[93,8,128]{2,1,0:T(8,128)S(1)}) custom-call(f32[10,8,128]{2,1,0:T(8,128)S(1)} %collective-permute-done.plane_right, f32[10,8,128]{2,1,0:T(8,128)S(1)} %collective-permute-done.1.from_right, ...), custom_call_target="tpu_custom_call" | custom-call | tf_op jit(solution)/shard_map/pallas_call | solution.py:613
  25.4 2.1 %collective-permute-start.5 = (f32[93,8,128]{2,1,0:T(8,128)S(1)}, f32[93,8,128]{2,1,0:T(8,128)S(1)}, u32[]{:S(2)}, u32[]{:S(2)}) collective-permute-start(f32[93,8,128]{2,1,0:T(8,128)S(1)} %get-tuple-element.33), channel_id=1, source_target_pairs={{4,0},{8,4},{12,8},{16,12},{20,16},{24,20},{28,24},{5,1},{9,5},{13... | collective-permute-start | bytes 1142792 | tf_op jit(solution)/shard_map/ppermute | solution.py:582
  27.5 3.2 %collective-permute-start.6 = (f32[93,8,128]{2,1,0:T(8,128)S(1)}, f32[93,8,128]{2,1,0:T(8,128)S(1)}, u32[]{:S(2)}, u32[]{:S(2)}) collective-permute-start(f32[93,8,128]{2,1,0:T(8,128)S(1)} %get-tuple-element.34), channel_id=1, source_target_pairs={{0,4},{4,8},{8,12},{12,16},{16,20},{20,24},{24,28},{1,5},{5,9},{9,... | collective-permute-start | bytes 1142792 | tf_op jit(solution)/shard_map/ppermute | solution.py:582
  30.7 4.5 %collective-permute-done.5.from_high = f32[93,8,128]{2,1,0:T(8,128)S(1)} collective-permute-done((f32[93,8,128]{2,1,0:T(8,128)S(1)}, f32[93,8,128]{2,1,0:T(8,128)S(1)}, u32[]{:S(2)}, u32[]{:S(2)}) %collective-permute-start.5) | collective-permute-done | bytes 380960 | tf_op jit(solution)/shard_map/ppermute | solution.py:582
  35.2 3.0 %collective-permute-done.6.from_low = f32[93,8,128]{2,1,0:T(8,128)S(1)} collective-permute-done((f32[93,8,128]{2,1,0:T(8,128)S(1)}, f32[93,8,128]{2,1,0:T(8,128)S(1)}, u32[]{:S(2)}, u32[]{:S(2)}) %collective-permute-start.6) | collective-permute-done | bytes 380960 | tf_op jit(solution)/shard_map/ppermute | solution.py:582
  38.2 1.2 %shard_map.52 = (f32[9,27,16,128]{3,2,1,0:T(8,128)S(1)}, f32[3,16,128]{2,1,0:T(8,128)S(1)}, f32[3,24,128]{2,1,0:T(8,128)S(1)}, f32[3,16,128]{2,1,0:T(8,128)S(1)}...) custom-call(f32[93,8,128]{2,1,0:T(8,128)S(1)} %collective-permute-done.5.from_high, ...), custom_call_target="tpu_custom_call" | custom-call | tf_op jit(solution)/shard_map/pallas_call | solution.py:625
  39.4 3.1 %collective-permute-start.7 = (f32[424,128]{1,0:T(8,128)S(1)}, f32[424,128]{1,0:T(8,128)S(1)}, u32[]{:S(2)}, u32[]{:S(2)}) collective-permute-start(f32[424,128]{1,0:T(8,128)S(1)} %get-tuple-element.42), channel_id=1, source_target_pairs={{1,2},{2,1},{5,6},{6,5},{9,10},{10,9},{13,14},{14,13},{17,18},{18,... | collective-permute-start | bytes 651272 | tf_op jit(solution)/shard_map/ppermute | solution.py:588
  42.5 3.1 %collective-permute-start.8 = (f32[424,128]{1,0:T(8,128)S(1)}, f32[424,128]{1,0:T(8,128)S(1)}, u32[]{:S(2)}, u32[]{:S(2)}) collective-permute-start(f32[424,128]{1,0:T(8,128)S(1)} %get-tuple-element.43), channel_id=1, source_target_pairs={{0,1},{2,3},{1,0},{3,2},{4,5},{6,7},{5,4},{7,6},{8,9},{10,11},{9,8... | collective-permute-start | bytes 651272 | tf_op jit(solution)/shard_map/ppermute | solution.py:588
  45.7 1.2 %shard_map.53 = (f32[3,3,3,3,3,2,4,64]{7,6,5,4,3,2,1,0:T(4,128)}, f32[8,128]{1,0:T(8,128)S(1)}) custom-call(f32[9,27,16,128]{3,2,1,0:T(8,128)S(1)} %get-tuple-element.37.whole), custom_call_target="tpu_custom_call" | custom-call | flops 500000 | bytes 3000000 | tf_op jit(solution)/shard_map/pallas_call | solution.py:633
  46.9 1.2 %collective-permute-done.7.from_other = f32[424,128]{1,0:T(8,128)S(1)} collective-permute-done((f32[424,128]{1,0:T(8,128)S(1)}, f32[424,128]{1,0:T(8,128)S(1)}, u32[]{:S(2)}, u32[]{:S(2)}) %collective-permute-start.7) | collective-permute-done | bytes 217120 | tf_op jit(solution)/shard_map/ppermute | solution.py:588
  48.1 0.8 %shard_map.54 = (f32[3,16,128]{2,1,0:T(8,128)S(1)}, f32[3,16,128]{2,1,0:T(8,128)S(1)}, f32[3,16,128]{2,1,0:T(8,128)S(1)}, f32[24,128]{1,0:T(8,128)S(1)}, f32[24,128]{1,0:T(8,128)S(1)}) custom-call(f32[9,27,16,128]{3,2,1,0:T(8,128)S(1)} %get-tuple-element.37.whole, f32[3,16,128]{2,1,0:T(8,128)S(1)} %get-tuple-element.39.q, ...), custom_call_target="tpu_custom_call" | custom-call | tf_op jit(solution)/shard_map/pallas_call | solution.py:647
  48.9 3.1 %collective-permute-start.9 = (f32[24,128]{1,0:T(8,128)S(1)}, f32[24,128]{1,0:T(8,128)S(1)}, u32[]{:S(2)}, u32[]{:S(2)}) collective-permute-start(f32[24,128]{1,0:T(8,128)S(1)} %get-tuple-element.48), channel_id=1, source_target_pairs={{1,2},{2,1},{5,6},{6,5},{9,10},{10,9},{13,14},{14,13},{17,18},{18,... | collective-permute-start | bytes 36872 | tf_op jit(solution)/shard_map/ppermute | solution.py:588
  52.0 1.9 %collective-permute-start.10 = (f32[24,128]{1,0:T(8,128)S(1)}, f32[24,128]{1,0:T(8,128)S(1)}, u32[]{:S(2)}, u32[]{:S(2)}) collective-permute-start(f32[24,128]{1,0:T(8,128)S(1)} %get-tuple-element.49), channel_id=1, source_target_pairs={{0,1},{2,3},{1,0},{3,2},{4,5},{6,7},{5,4},{7,6},{8,9},{10,11},{9,8... | collective-permute-start | bytes 36872 | tf_op jit(solution)/shard_map/ppermute | solution.py:588
  53.9 1.5 %collective-permute-done.9.from_other = f32[24,128]{1,0:T(8,128)S(1)} collective-permute-done((f32[24,128]{1,0:T(8,128)S(1)}, f32[24,128]{1,0:T(8,128)S(1)}, u32[]{:S(2)}, u32[]{:S(2)}) %collective-permute-start.9) | collective-permute-done | bytes 12320 | tf_op jit(solution)/shard_map/ppermute | solution.py:588
  55.4 0.9 %shard_map.55 = f32[3,2,4,64]{3,2,1,0:T(4,128)} custom-call(f32[9,27,16,128]{3,2,1,0:T(8,128)S(1)} %get-tuple-element.37.whole, f32[3,16,128]{2,1,0:T(8,128)S(1)} %get-tuple-element.45.q, f32[3,16,128]{2,1,0:T(8,128)S(1)} %get-tuple-element.46.d, f32[3,16,128]{2,1,0:T(8,128)S(1)} %get-tuple-element.41.inverse, f32[3,16,128]{2,1,0:T(8,128)S(1)} %get-tuple-element.47.x, ...), custom_call_target="tpu_custom_call" | custom-call | tf_op jit(solution)/shard_map/pallas_call | solution.py:656
  (4 shorter events, 0.0 us)
Async XLA Ops:
  5.4 18.4 %collective-permute-start.4 = (f32[56,8,128]{2,1,0:T(8,128)S(1)}, f32[56,8,128]{2,1,0:T(8,128)S(1)}, u32[]{:S(2)}, u32[]{:S(2)}) collective-permute-start(f32[56,8,128]{2,1,0:T(8,128)S(1)} %get-tuple-element.30), channel_id=1, source_target_pairs={{0,1},{1,2},{2,3},{4,5},{5,6},{6,7},{8,9},{9,10},{10,11},{12,13},{... | collective-permute-start | bytes 688136 | tf_op jit(solution)/shard_map/ppermute | solution.py:582
  10.7 9.5 %collective-permute-start = (f32[10,8,128]{2,1,0:T(8,128)S(1)}, f32[10,8,128]{2,1,0:T(8,128)S(1)}, u32[]{:S(2)}, u32[]{:S(2)}) collective-permute-start(f32[10,8,128]{2,1,0:T(8,128)S(1)} %get-tuple-element.26), channel_id=1, source_target_pairs={{32,1},{33,2},{34,3},{64,33},{65,34},{66,35},{96,65},{97,66},{98,6... | collective-permute-start | bytes 122888 | tf_op jit(solution)/shard_map/ppermute | solution.py:582
  12.6 7.5 %collective-permute-start.1 = (f32[10,8,128]{2,1,0:T(8,128)S(1)}, f32[10,8,128]{2,1,0:T(8,128)S(1)}, u32[]{:S(2)}, u32[]{:S(2)}) collective-permute-start(f32[10,8,128]{2,1,0:T(8,128)S(1)} %get-tuple-element.27), channel_id=1, source_target_pairs={{32,0},{64,32},{96,64},{128,96},{160,128},{192,160},{224,192},{256... | collective-permute-start | bytes 122888 | tf_op jit(solution)/shard_map/ppermute | solution.py:582
  14.5 7.4 %collective-permute-start.2 = (f32[10,8,128]{2,1,0:T(8,128)S(1)}, f32[10,8,128]{2,1,0:T(8,128)S(1)}, u32[]{:S(2)}, u32[]{:S(2)}) collective-permute-start(f32[10,8,128]{2,1,0:T(8,128)S(1)} %get-tuple-element.28), channel_id=1, source_target_pairs={{0,33},{1,34},{2,35},{32,65},{33,66},{34,67},{64,97},{65,98},{66,9... | collective-permute-start | bytes 122888 | tf_op jit(solution)/shard_map/ppermute | solution.py:582
  17.0 6.9 %collective-permute-start.3 = (f32[10,8,128]{2,1,0:T(8,128)S(1)}, f32[10,8,128]{2,1,0:T(8,128)S(1)}, u32[]{:S(2)}, u32[]{:S(2)}) collective-permute-start(f32[10,8,128]{2,1,0:T(8,128)S(1)} %get-tuple-element.29), channel_id=1, source_target_pairs={{0,32},{32,64},{64,96},{96,128},{128,160},{160,192},{192,224},{224... | collective-permute-start | bytes 122888 | tf_op jit(solution)/shard_map/ppermute | solution.py:582
  25.4 9.8 %collective-permute-start.5 = (f32[93,8,128]{2,1,0:T(8,128)S(1)}, f32[93,8,128]{2,1,0:T(8,128)S(1)}, u32[]{:S(2)}, u32[]{:S(2)}) collective-permute-start(f32[93,8,128]{2,1,0:T(8,128)S(1)} %get-tuple-element.33), channel_id=1, source_target_pairs={{4,0},{8,4},{12,8},{16,12},{20,16},{24,20},{28,24},{5,1},{9,5},{13... | collective-permute-start | bytes 1142792 | tf_op jit(solution)/shard_map/ppermute | solution.py:582
  27.5 10.7 %collective-permute-start.6 = (f32[93,8,128]{2,1,0:T(8,128)S(1)}, f32[93,8,128]{2,1,0:T(8,128)S(1)}, u32[]{:S(2)}, u32[]{:S(2)}) collective-permute-start(f32[93,8,128]{2,1,0:T(8,128)S(1)} %get-tuple-element.34), channel_id=1, source_target_pairs={{0,4},{4,8},{8,12},{12,16},{16,20},{20,24},{24,28},{1,5},{5,9},{9,... | collective-permute-start | bytes 1142792 | tf_op jit(solution)/shard_map/ppermute | solution.py:582
  39.4 8.7 %collective-permute-start.7 = (f32[424,128]{1,0:T(8,128)S(1)}, f32[424,128]{1,0:T(8,128)S(1)}, u32[]{:S(2)}, u32[]{:S(2)}) collective-permute-start(f32[424,128]{1,0:T(8,128)S(1)} %get-tuple-element.42), channel_id=1, source_target_pairs={{1,2},{2,1},{5,6},{6,5},{9,10},{10,9},{13,14},{14,13},{17,18},{18,... | collective-permute-start | bytes 651272 | tf_op jit(solution)/shard_map/ppermute | solution.py:588
  42.5 5.6 %collective-permute-start.8 = (f32[424,128]{1,0:T(8,128)S(1)}, f32[424,128]{1,0:T(8,128)S(1)}, u32[]{:S(2)}, u32[]{:S(2)}) collective-permute-start(f32[424,128]{1,0:T(8,128)S(1)} %get-tuple-element.43), channel_id=1, source_target_pairs={{0,1},{2,3},{1,0},{3,2},{4,5},{6,7},{5,4},{7,6},{8,9},{10,11},{9,8... | collective-permute-start | bytes 651272 | tf_op jit(solution)/shard_map/ppermute | solution.py:588
  48.9 6.5 %collective-permute-start.9 = (f32[24,128]{1,0:T(8,128)S(1)}, f32[24,128]{1,0:T(8,128)S(1)}, u32[]{:S(2)}, u32[]{:S(2)}) collective-permute-start(f32[24,128]{1,0:T(8,128)S(1)} %get-tuple-element.48), channel_id=1, source_target_pairs={{1,2},{2,1},{5,6},{6,5},{9,10},{10,9},{13,14},{14,13},{17,18},{18,... | collective-permute-start | bytes 36872 | tf_op jit(solution)/shard_map/ppermute | solution.py:588
  52.0 3.4 %collective-permute-start.10 = (f32[24,128]{1,0:T(8,128)S(1)}, f32[24,128]{1,0:T(8,128)S(1)}, u32[]{:S(2)}, u32[]{:S(2)}) collective-permute-start(f32[24,128]{1,0:T(8,128)S(1)} %get-tuple-element.49), channel_id=1, source_target_pairs={{0,1},{2,3},{1,0},{3,2},{4,5},{6,7},{5,4},{7,6},{8,9},{10,11},{9,8... | collective-permute-start | bytes 36872 | tf_op jit(solution)/shard_map/ppermute | solution.py:588
